TPU v7x, 256 devices: a whole 4x4x8 slice. The times are simulated.
256 devices in a mesh: fsdp: 64 (over z, x_lo, y), tp: 4 (over x_hi, core).
Axes of the slice: x: 4 (x_hi: 2, x_lo: 2; x = x_hi * 2 + x_lo), y: 4, z: 8, core: 2. Of those that a mesh axis runs over, the one named last changes fastest.
Arguments:
- tokens: bfloat16 [65536, 5120], P('fsdp', 'tp'), may hold values from -16 to 16
- grad_out: bfloat16 [65536, 2, 1024], P('fsdp', None, 'tp'), may hold values from -700 to 700, as said below
- weight: float32 [5120, 2, 1024], P('fsdp', None, 'tp'), may hold values from -0.009765625 to 0.009765625
- moment_one: float32 [5120, 2, 1024], P('fsdp', None, 'tp'), may hold values from -0.00061035156 to 0.00061035156
- moment_two: float32 [5120, 2, 1024], P('fsdp', None, 'tp'), may hold values from 1e-09 to 1e-07
- rollout_hidden: bfloat16 [256, 4, 5120], P('fsdp'), may hold values from -6 to 6
- queries: bfloat16 [256, 4, 8192], P('fsdp', None, 'tp'), may hold values from -160 to 160
- cache_keys: bfloat16 [256, 2048, 1024], P('fsdp', None, 'tp'), may hold values from -5 to 5
- cache_values: bfloat16 [256, 2048, 1024], P('fsdp', None, 'tp'), may hold values from -6 to 6
- cache_lengths: int32 [256], P('fsdp'), may hold values from 256 to 2048, as said below
- key_gain: float32 [128], replicated, may hold values from 0.1 to 1.9
Outputs:
- new_weight: float32 [5120, 2, 1024], P('fsdp', None, 'tp')
- adam_step: float32 [5120, 2, 1024], P('fsdp', None, 'tp')
- new_keys: bfloat16 [256, 4, 1024], P('fsdp', None, 'tp')
- new_values: bfloat16 [256, 4, 1024], P('fsdp', None, 'tp')
- attended: bfloat16 [256, 4, 8192], P('fsdp', None, 'tp')
Inputs may be any that keep to these rules, and one draw needn't show every extreme that they name: `grad_out`: real values; the first row's ramp across the tokens and the spread across columns make every scale of order one to ten. `cache_lengths`: at least one row has exactly 2048 filled slots; every row has at least 256.
All inputs are finite; a program needn't handle non-finite values.
Results may differ from a plain program's by a relative error of at most 0.0049.
Values may be sent and summed in bfloat16 or wider, within the bound.
No kernel may reach another device: no remote copies, remote signals or barrier semaphores. Data moves between devices by JAX's collectives and lax.ppermute only.
A program may use at most 128 MiB of HBM per device.

v0:
```python
import math

import jax
import jax.numpy as jnp
from jax import lax
from jax.sharding import PartitionSpec as P

QH = 64
KVH = 8
HD = 128


beta_one = 0.9
beta_two = 0.999
learn_rate = 0.001
decay_rate = 0.1
adam_eps = 1e-08
step_number = 10.0
clip_rms = 0.001
norm_eps = 1e-06
rope_base = 1000000.0


def adamw_update(weight, gradient, moment_one, moment_two, factor):
    clipped = gradient * factor
    first_moment = beta_one * moment_one + (1.0 - beta_one) * clipped
    second_moment = beta_two * moment_two + (1.0 - beta_two) * clipped * clipped
    first_hat = first_moment / (1.0 - beta_one**step_number)
    second_hat = second_moment / (1.0 - beta_two**step_number)
    direction = first_hat / (jnp.sqrt(second_hat) + adam_eps) + decay_rate * weight
    return (weight - learn_rate * direction, direction)


def rotate_keys(values, positions):
    half_width = values.shape[-1] // 2
    frequency = rope_base ** (-2.0 * jnp.arange(half_width, dtype=jnp.float32) / values.shape[-1])
    angles = positions.astype(jnp.float32)[..., None] * frequency
    cosine = jnp.cos(angles)
    sine_part = jnp.sin(angles)
    first_half = values[..., :half_width]
    second_half = values[..., half_width:]
    return jnp.concatenate(
        [
            first_half * cosine - second_half * sine_part,
            second_half * cosine + first_half * sine_part,
        ],
        axis=-1,
    )


def norm_keys(raw_keys, key_gain):
    return (
        raw_keys
        * lax.rsqrt(jnp.mean(raw_keys * raw_keys, axis=-1, keepdims=True) + norm_eps)
        * key_gain
    )


def local(
    tokens,
    grad_out,
    weight,
    moment_one,
    moment_two,
    rollout_hidden,
    queries,
    cache_keys,
    cache_values,
    cache_lengths,
    key_gain,
):
    token_count = tokens.shape[0]
    total_tokens = token_count * lax.axis_size("fsdp")
    own_rows = weight.shape[0]
    columns = weight.shape[1] * weight.shape[2]
    entry_count = own_rows * lax.axis_size("fsdp") * columns * lax.axis_size("tp")
    features = lax.all_gather(tokens, "tp", axis=1, tiled=True)
    upstream = grad_out.reshape(token_count, columns)
    gradient = (
        lax.psum_scatter(
            lax.dot_general(
                features, upstream, (((0,), (0,)), ((), ())), preferred_element_type=jnp.float32
            ),
            "fsdp",
            scatter_dimension=0,
            tiled=True,
        )
        / total_tokens
    )
    squares = lax.psum(jnp.sum(gradient * gradient), ("fsdp", "tp"))
    factor = jnp.minimum(1.0, clip_rms / jnp.sqrt(squares / float(entry_count) + norm_eps))
    new_weight, adam_step = adamw_update(
        weight.reshape(own_rows, columns),
        gradient,
        moment_one.reshape(own_rows, columns),
        moment_two.reshape(own_rows, columns),
        factor,
    )
    rollout_weight = new_weight.astype(jnp.bfloat16)
    row_count, step_count, model_width = rollout_hidden.shape
    flat_hidden = rollout_hidden.reshape(row_count * step_count, model_width)
    projected = jnp.dot(
        flat_hidden,
        lax.all_gather(rollout_weight, "fsdp", axis=0, tiled=True),
        preferred_element_type=jnp.float32,
    )
    head_count = weight.shape[2] // HD
    projected = projected.reshape(row_count, step_count, 2, head_count, HD)
    positions = cache_lengths[:, None] + jnp.arange(step_count, dtype=jnp.int32)[None, :]
    fresh_keys = rotate_keys(norm_keys(projected[:, :, 0], key_gain), positions[:, :, None]).astype(
        jnp.bfloat16
    )
    fresh_values = projected[:, :, 1].astype(jnp.bfloat16)
    groups = QH // KVH
    query_heads = queries.reshape(row_count, step_count, head_count, groups, HD)
    old_keys = cache_keys.reshape(row_count, cache_keys.shape[1], head_count, HD)
    old_values = cache_values.reshape(row_count, cache_values.shape[1], head_count, HD)
    scale_factor = 1.0 / math.sqrt(HD)
    old_scores = (
        jnp.einsum("rsgqd,rcgd->rgqsc", query_heads, old_keys, preferred_element_type=jnp.float32)
        * scale_factor
    )
    fresh_scores = (
        jnp.einsum("rsgqd,rtgd->rgqst", query_heads, fresh_keys, preferred_element_type=jnp.float32)
        * scale_factor
    )
    old_valid = jnp.arange(old_keys.shape[1], dtype=jnp.int32)[None, :] < cache_lengths[:, None]
    fresh_valid = jnp.arange(step_count)[:, None] >= jnp.arange(step_count)[None, :]
    old_scores = jnp.where(old_valid[:, None, None, None, :], old_scores, -jnp.inf)
    fresh_scores = jnp.where(fresh_valid, fresh_scores, -jnp.inf)
    top_score = jnp.maximum(
        jnp.max(old_scores, axis=-1, keepdims=True), jnp.max(fresh_scores, axis=-1, keepdims=True)
    )
    old_exp = jnp.exp(old_scores - top_score)
    fresh_exp = jnp.exp(fresh_scores - top_score)
    denominator = jnp.sum(old_exp, axis=-1, keepdims=True) + jnp.sum(
        fresh_exp, axis=-1, keepdims=True
    )
    old_weights = (old_exp / denominator).astype(jnp.bfloat16)
    fresh_weights = (fresh_exp / denominator).astype(jnp.bfloat16)
    mixed = jnp.einsum(
        "rgqsc,rcgd->rsgqd", old_weights, old_values, preferred_element_type=jnp.float32
    )
    mixed = mixed + jnp.einsum(
        "rgqst,rtgd->rsgqd", fresh_weights, fresh_values, preferred_element_type=jnp.float32
    )
    attended = mixed.astype(jnp.bfloat16).reshape(row_count, step_count, head_count * groups * HD)
    new_keys = fresh_keys.reshape(row_count, step_count, head_count * HD)
    new_values = fresh_values.reshape(row_count, step_count, head_count * HD)
    return (
        new_weight.reshape(weight.shape),
        adam_step.reshape(weight.shape),
        new_keys,
        new_values,
        attended,
    )


def solution(mesh):
    in_specs = (
        P("fsdp", "tp"),
        P("fsdp", None, "tp"),
        P("fsdp", None, "tp"),
        P("fsdp", None, "tp"),
        P("fsdp", None, "tp"),
        P("fsdp", None, None),
        P("fsdp", None, "tp"),
        P("fsdp", None, "tp"),
        P("fsdp", None, "tp"),
        P("fsdp"),
        P(),
    )
    out_specs = (
        P("fsdp", None, "tp"),
        P("fsdp", None, "tp"),
        P("fsdp", None, "tp"),
        P("fsdp", None, "tp"),
        P("fsdp", None, "tp"),
    )
    return jax.shard_map(local, mesh=mesh, in_specs=in_specs, out_specs=out_specs, check_vma=False)
```

profile of v0, /device:TPU:24, one launch (start us, length us, event | category | flops | bytes accessed | tf_op | source)
XLA Modules:
  0.0 829.4 jit_solution(3741176501406381461)
XLA Ops:
  7.2 0.7 all-gather.3.cloned.1.call-update
  7.9 1.4 copy.41
  9.4 79.9 %all-gather.3.cloned.1.call-done = bf16[1024,5120]{1,0:T(8,128)(2,1)} async-done(((bf16[1024,1280]{1,0:T(8,128)(2,1)}), bf16[1024,5120]{1,0:T(8,128)(2,1)}) %all-gather.3.cloned.1.call-update) | async-done | bytes 10485776 | tf_op jit(solution)/shard_map/all_gather | solution.py:77
  89.3 12.5 %fusion.42 = f32[5120,512]{1,0:T(8,128)} fusion(bf16[1024,5120]{1,0:T(8,128)(2,1)} %all-gather.3.cloned.1.call-done, bf16[1024,512]{1,0:T(8,128)(2,1)S(1)} %bitcast.59), kind=kOutput, calls=%fused_computation.59 | convolution fusion | flops 5368709120 | bytes 22020096 | tf_op jit(solution)/shard_map/dot_general | solution.py:81
  102.0 0.8 copy-done
  102.8 0.1 broadcast_multiply_fusion.1
  102.9 0.1 broadcast_multiply_fusion
  103.0 326.0 %reduce-scatter.2.cloned.1.call-done = f32[80,512]{1,0:T(8,128)} async-done(((f32[5120,512]{1,0:T(8,128)}), f32[80,512]{1,0:T(8,128)}) %reduce-scatter.2.cloned.1.call-update) | async-done | bytes 163856 | tf_op jit(solution)/shard_map/reduce_scatter | solution.py:80
  429.0 1.6 multiply_reduce_fusion
  430.6 81.6 %psum.7 = f32[]{:T(128)} all-reduce(f32[]{:T(128)} %multiply_reduce_fusion), channel_id=1, replica_groups=mesh['fsdp'=64,'tp'=4] {'fsdp','tp'}, use_global_device_ids=true, to_apply=%region_2.0 | all-reduce | flops 1 | bytes 8 | tf_op jit(solution)/shard_map/psum | solution.py:90
  512.9 1.7 fusion.37
  514.8 7.0 reshape.138
  521.7 7.0 reshape.140
  528.8 0.1 add_convert_fusion
  528.9 0.1 multiply_cosine_fusion
  529.0 0.1 iota_compare_fusion
  529.1 3.8 fusion.39
  532.9 0.8 reshape.134
  533.7 0.8 reshape.135
  534.4 278.6 %all-gather.5.cloned.1.call-done = bf16[5120,512]{1,0:T(8,128)(2,1)} async-done(((bf16[80,512]{1,0:T(8,128)(2,1)}), bf16[5120,512]{1,0:T(8,128)(2,1)}) %all-gather.5.cloned.1.call-update) | async-done | bytes 5242896 | tf_op jit(solution)/shard_map/all_gather | solution.py:104
  813.0 3.3 convolution_bitcast_fusion.1
  816.4 0.1 multiply_reduce_fusion.1
  816.5 0.1 multiply_multiply_fusion.1
  816.6 0.1 multiply_subtract_fusion.1
  816.6 0.7 fusion.41
  817.3 0.4 fusion.40
  817.8 0.1 fusion.31
  817.9 0.4 fusion.13
  818.3 0.6 copy.76
  818.9 3.1 fusion.14
  822.0 0.2 fusion.18
  822.3 0.6 reshape.141
  (32 shorter events, 0.4 us)
Async XLA Ops:
  7.2 82.2 %all-gather.3.cloned.1.call-start = ((), (), s32[]{:S(2)}) async-start(), calls=%async_computation.1 | async-start | bytes 13107200 | tf_op jit(solution)/shard_map/all_gather | solution.py:77
  7.9 421.1 %reduce-scatter.2.cloned.1.call-start = ((), (), s32[]{:S(2)}) async-start(), calls=%async_computation.2 | async-start | bytes 10649600 | tf_op jit(solution)/shard_map/reduce_scatter | solution.py:80
  101.9 0.9 copy-start
  101.9 1.0 copy-start.1
  101.9 328.7 %copy-start.2 = (f32[80,2,256]{2,1,0:T(2,128)S(1)}, f32[80,2,256]{2,1,0:T(2,128)}, u32[]{:S(2)}) copy-start(f32[80,2,256]{2,1,0:T(2,128)} %param.13) | copy-start | bytes 491524
  101.9 412.8 %copy-start.3 = (bf16[4,4,5120]{2,1,0:T(4,128)(2,1)S(1)}, bf16[4,4,5120]{2,1,0:T(4,128)(2,1)}, u32[]{:S(2)}) copy-start(bf16[4,4,5120]{2,1,0:T(4,128)(2,1)} %param.16) | copy-start | bytes 491524
  101.9 412.8 %copy-start.4 = (bf16[4,4,2048]{2,1,0:T(4,128)(2,1)S(1)}, bf16[4,4,2048]{2,1,0:T(4,128)(2,1)}, u32[]{:S(2)}) copy-start(bf16[4,4,2048]{2,1,0:T(4,128)(2,1)} %param.17) | copy-start | bytes 196612
  101.9 711.1 %all-gather.5.cloned.1.call-start = ((), (), s32[]{:S(2)}) async-start(), calls=%async_computation.3 | async-start | bytes 5324800 | tf_op jit(solution)/shard_map/all_gather | solution.py:104
  521.7 7.1 copy-start.5
  532.9 283.6 %copy-start.6 = (f32[128]{0:T(128)S(1)}, f32[128]{0:T(128)}, u32[]{:S(2)}) copy-start(f32[128]{0:T(128)} %param.21) | copy-start | bytes 1540
Sparse Core Ops, SparseCore 0:
  9.8 79.4 all-gather.2
  102.0 326.9 reduce-scatter.1
  514.8 298.2 all-gather.4
where the time goes:
time: 835 us; the launch traced here: 829 us
  waiting for transfers between devices  685 us (82%)
  blocking collectives  81.6 us (10%)
  matrix products  23.3 us (3%)
  local copies, waits for them, and re-layouts  19.3 us (2%)
  between operations  14.6 us (2%)
    reduce_scatter x1, waiting for transfers between devices, local(): lax.psum_scatter(lax.dot_general(features, upstream, (((0,), (0,)), ((),...  326 us
    all_gather x1, waiting for transfers between devices, local(): lax.all_gather(rollout_weight, 'fsdp', axis=0, tiled=True)  279 us
    psum x1, blocking collectives, local(): squares = lax.psum(jnp.sum(gradient * gradient), ('fsdp', 'tp'))  81.6 us
    all_gather x1, waiting for transfers between devices, local(): features = lax.all_gather(tokens, 'tp', axis=1, tiled=True)  79.9 us
  transfers between devices with their start and end apart: 3, of which 3 were waited for; matrix products, arithmetic and copies ran while one was open for 3% of the time, Pallas kernels for 0%

commit v1 on v0

v1 whole, which is shorter than its diff:
```python
import functools
import math

import jax
import jax.numpy as jnp
from jax import lax
from jax.experimental import pallas as pl
from jax.experimental.pallas import tpu as pltpu
from jax.sharding import Mesh
from jax.sharding import PartitionSpec as P

QH = 64
KVH = 8
HD = 128

beta_one = 0.9
beta_two = 0.999
learn_rate = 0.001
decay_rate = 0.1
adam_eps = 1e-08
step_number = 10.0
clip_rms = 0.001
norm_eps = 1e-06
rope_base = 1000000.0

SIZES = {"z": 8, "xl": 2, "y": 4, "xh": 2, "core": 2}
FSDP = ("z", "xl", "y")
TP = ("xh", "core")
EVERY = FSDP + TP

BF16 = jnp.bfloat16
F32 = jnp.float32


def adamw_update(weight, gradient, moment_one, moment_two, factor):
    clipped = gradient * factor
    first_moment = beta_one * moment_one + (1.0 - beta_one) * clipped
    second_moment = beta_two * moment_two + (1.0 - beta_two) * clipped * clipped
    first_hat = first_moment / (1.0 - beta_one**step_number)
    second_hat = second_moment / (1.0 - beta_two**step_number)
    direction = first_hat / (jnp.sqrt(second_hat) + adam_eps) + decay_rate * weight
    return (weight - learn_rate * direction, direction)


def rotate_keys(values, positions):
    half_width = values.shape[-1] // 2
    frequency = rope_base ** (-2.0 * jnp.arange(half_width, dtype=F32) / values.shape[-1])
    angles = positions.astype(F32)[..., None] * frequency
    cosine = jnp.cos(angles)
    sine_part = jnp.sin(angles)
    first_half = values[..., :half_width]
    second_half = values[..., half_width:]
    return jnp.concatenate(
        [
            first_half * cosine - second_half * sine_part,
            second_half * cosine + first_half * sine_part,
        ],
        axis=-1,
    )


def norm_keys(raw_keys, key_gain):
    return (
        raw_keys
        * lax.rsqrt(jnp.mean(raw_keys * raw_keys, axis=-1, keepdims=True) + norm_eps)
        * key_gain
    )


def swap(values, axis):
    return lax.ppermute(values, axis, [(0, 1), (1, 0)])


PAIRING = ([(0, 1), (1, 0), (2, 3), (3, 2)], [(0, 3), (3, 0), (1, 2), (2, 1)])


def partner(position, pairing):
    return position ^ 1 if pairing == 0 else 3 - position


def at_y(block, position):
    return lax.dynamic_index_in_dim(block, position, axis=2, keepdims=False)


def reduce_y(block, first):
    second = 1 - first
    me = lax.axis_index("y")
    far = partner(me, first)
    away = jnp.stack([at_y(block, partner(far, second)), at_y(block, far)])
    got = lax.ppermute(away, "y", PAIRING[first])
    near = partner(me, second)
    passed = (at_y(block, near).astype(F32) + got[0].astype(F32)).astype(BF16)
    last = lax.ppermute(passed, "y", PAIRING[second])
    return at_y(block, me).astype(F32) + got[1].astype(F32) + last.astype(F32)


def old_attention_kernel(length_ref, query_ref, key_ref, value_ref, out_ref, top_ref, total_ref):
    length = length_ref[pl.program_id(0)]
    scores = lax.dot_general(
        query_ref[0, 0], key_ref[0], (((1,), (1,)), ((), ())), preferred_element_type=F32
    ) * (1.0 / math.sqrt(HD))
    slot = lax.broadcasted_iota(jnp.int32, scores.shape, 1)
    scores = jnp.where(slot < length, scores, -jnp.inf)
    top = jnp.max(scores, axis=-1, keepdims=True)
    weights = jnp.exp(scores - top)
    total = jnp.sum(weights, axis=-1, keepdims=True)
    out_ref[0, 0] = jnp.dot(weights.astype(BF16), value_ref[0], preferred_element_type=F32)
    top_ref[0, 0] = jnp.broadcast_to(top, top_ref.shape[2:])
    total_ref[0, 0] = jnp.broadcast_to(total, total_ref.shape[2:])


def old_attention(query_heads, cache_keys, cache_values, cache_lengths):
    rows, heads, queries, _ = query_heads.shape
    cache = cache_keys.shape[1]
    small = pl.BlockSpec((1, 1, queries, HD), lambda r, h, lengths: (r, h, 0, 0))
    large = pl.BlockSpec((1, cache, HD), lambda r, h, lengths: (r, 0, h))
    shape = jax.ShapeDtypeStruct((rows, heads, queries, HD), F32)
    return pl.pallas_call(
        old_attention_kernel,
        out_shape=(shape, shape, shape),
        grid_spec=pltpu.PrefetchScalarGridSpec(
            num_scalar_prefetch=1,
            grid=(rows, heads),
            in_specs=[small, large, large],
            out_specs=[small, small, small],
        ),
        compiler_params=pltpu.CompilerParams(vmem_limit_bytes=24 * 1024 * 1024),
        name="old_attention",
    )(cache_lengths, query_heads, cache_keys, cache_values)


def local(
    tokens,
    grad_out,
    weight,
    moment_one,
    moment_two,
    rollout_hidden,
    queries,
    cache_keys,
    cache_values,
    cache_lengths,
    key_gain,
):
    token_count = tokens.shape[0]
    total_tokens = token_count * 64
    own_rows = weight.shape[0]
    columns = weight.shape[1] * weight.shape[2]
    entry_count = own_rows * 64 * columns * 4
    z = lax.axis_index("z")
    xl = lax.axis_index("xl")
    xh = lax.axis_index("xh")
    core = lax.axis_index("core")

    upstream = grad_out.reshape(token_count, columns)
    with jax.named_scope("exchange"):
        tokens_other = swap(tokens, "core")
        upstream_other = swap(upstream, "xh")

    with jax.named_scope("hidden"):
        row_count, step_count, model_width = rollout_hidden.shape
        states = row_count * step_count
        hidden = rollout_hidden.reshape(states, 64, own_rows).transpose(1, 0, 2)
        hidden = lax.all_to_all(hidden, FSDP, 0, 0).reshape(64 * states, own_rows)

    def product(left, right):
        out = lax.dot_general(left, right, (((0,), (0,)), ((), ())), preferred_element_type=F32)
        return out.astype(BF16).reshape(2, 2, 4, own_rows, columns)

    def reduce_xl(block):
        block = block.astype(BF16)
        kept = lax.dynamic_index_in_dim(block, xl, axis=1, keepdims=False)
        sent = lax.dynamic_index_in_dim(block, 1 - xl, axis=1, keepdims=False)
        return (kept.astype(F32) + swap(sent, "xl").astype(F32)).astype(BF16)

    halves = []
    for name, right in (("own", upstream), ("other", upstream_other)):
        with jax.named_scope("gradient_" + name):
            first = reduce_xl(reduce_y(product(tokens, right), 0))
            second = reduce_xl(reduce_y(product(tokens_other, right), 1))
            halves.append(
                jnp.where(
                    core == 0,
                    jnp.concatenate([first, second]),
                    jnp.concatenate([second, first]),
                )
            )
    with jax.named_scope("reduce_z"):
        own, other = halves
        parts = jnp.where(
            xh == 0, jnp.concatenate([own, other]), jnp.concatenate([other, own])
        )
        parts = lax.all_to_all(parts, "z", 0, 0)
        gradient = jnp.sum(parts.astype(F32), axis=0) / total_tokens
    with jax.named_scope("place"):
        pairs = []
        for a in range(8):
            for b in range(2):
                pairs.append((a * 2 + b, a * 2 + b if a // 4 == b else (a + 4) % 8 * 2 + 1 - b))
        placed = lax.ppermute(gradient, ("z", "xh"), pairs)
    with jax.named_scope("squares"):
        squares = jnp.sum(gradient * gradient)
        squares = lax.all_to_all(jnp.broadcast_to(squares, (256, 1, 128)), EVERY, 0, 0)
        squares = jnp.sum(squares[:, 0, 0])
        factor = jnp.minimum(1.0, clip_rms / jnp.sqrt(squares / float(entry_count) + norm_eps))
    with jax.named_scope("adam"):
        new_weight, adam_step = adamw_update(
            weight.reshape(own_rows, columns),
            placed,
            moment_one.reshape(own_rows, columns),
            moment_two.reshape(own_rows, columns),
            factor,
        )
        rollout_weight = new_weight.astype(BF16)
    with jax.named_scope("project"):
        partial = jnp.dot(hidden, rollout_weight, preferred_element_type=F32).astype(BF16)
        partial = lax.all_to_all(partial.reshape(64, states, columns), FSDP, 0, 0)
        projected = jnp.sum(partial.astype(F32), axis=0)

    with jax.named_scope("old"):
        head_count = weight.shape[2] // HD
        groups = QH // KVH
        scale_factor = 1.0 / math.sqrt(HD)
        query_heads = queries.reshape(row_count, step_count, head_count, groups, HD)
        query_heads = query_heads.transpose(0, 2, 1, 3, 4)
        query_heads = query_heads.reshape(row_count, head_count, step_count * groups, HD)
        old_sum, old_top, old_total = old_attention(
            query_heads, cache_keys, cache_values, cache_lengths
        )
    with jax.named_scope("fresh"):
        projected = projected.reshape(row_count, step_count, 2, head_count, HD)
        positions = cache_lengths[:, None] + jnp.arange(step_count, dtype=jnp.int32)[None, :]
        fresh_keys = rotate_keys(
            norm_keys(projected[:, :, 0], key_gain), positions[:, :, None]
        ).astype(BF16)
        fresh_values = projected[:, :, 1].astype(BF16)
        fresh_scores = (
            jnp.einsum("rgqd,rtgd->rgqt", query_heads, fresh_keys, preferred_element_type=F32)
            * scale_factor
        )
        step_of = jnp.arange(step_count * groups) // groups
        fresh_valid = step_of[:, None] >= jnp.arange(step_count)[None, :]
        fresh_scores = jnp.where(fresh_valid, fresh_scores, -jnp.inf)
        old_top = old_top[..., :1]
        old_total = old_total[..., :1]
        top = jnp.maximum(old_top, jnp.max(fresh_scores, axis=-1, keepdims=True))
        fresh_exp = jnp.exp(fresh_scores - top)
        old_scale = jnp.exp(old_top - top)
        denominator = old_total * old_scale + jnp.sum(fresh_exp, axis=-1, keepdims=True)
        mixed = old_sum * (old_scale / denominator)
        mixed = mixed + jnp.einsum(
            "rgqt,rtgd->rgqd",
            (fresh_exp / denominator).astype(BF16),
            fresh_values,
            preferred_element_type=F32,
        )
        attended = mixed.astype(BF16).reshape(row_count, head_count, step_count, groups, HD)
        attended = attended.transpose(0, 2, 1, 3, 4)
        attended = attended.reshape(row_count, step_count, head_count * groups * HD)
        new_keys = fresh_keys.reshape(row_count, step_count, head_count * HD)
        new_values = fresh_values.reshape(row_count, step_count, head_count * HD)
    return (
        new_weight.reshape(weight.shape),
        adam_step.reshape(weight.shape),
        new_keys,
        new_values,
        attended,
    )


def solution(mesh):
    fine = Mesh(mesh.devices.reshape(tuple(SIZES.values())), tuple(SIZES))
    in_specs = (
        P(FSDP, TP),
        P(FSDP, None, TP),
        P(FSDP, None, TP),
        P(FSDP, None, TP),
        P(FSDP, None, TP),
        P(FSDP, None, None),
        P(FSDP, None, TP),
        P(FSDP, None, TP),
        P(FSDP, None, TP),
        P(FSDP),
        P(),
    )
    out_specs = (P(FSDP, None, TP),) * 5
    return jax.shard_map(local, mesh=fine, in_specs=in_specs, out_specs=out_specs, check_vma=False)
```

time: 835 us -> 197 us (0.24)
  waiting for transfers between devices: 685 us -> 83.5 us
  blocking collectives: 81.6 us -> 26.1 us
  starting transfers between devices: 0.12 us -> 37.1 us
  between operations: 14.6 us -> 1.93 us
  matrix products: 23.3 us -> 14.6 us
    all_gather x2 -> x0, waiting for transfers between devices: 359 us -> none  [the longest x1 279 us: local(): lax.all_gather(rollout_weight, 'fsdp', axis=0, tiled=True)]
    reduce_scatter x1 -> x0, waiting for transfers between devices: 326 us -> none  [local(): lax.psum_scatter(lax.dot_general(features, upstream, (((0,), (0,)), ((),...]
    psum x1 -> x0, blocking collectives: 81.6 us -> none  [local(): squares = lax.psum(jnp.sum(gradient * gradient), ('fsdp', 'tp'))]
    ppermute x0 -> x15, waiting for transfers between devices: none -> 48.5 us  [the longest x4 30.9 us: reduce_y(): got = lax.ppermute(away, 'y', PAIRING[first])]
    all_to_all x0 -> x3, waiting for transfers between devices: none -> 35.1 us  [the longest x1 14.7 us: local(): partial = lax.all_to_all(partial.reshape(64, states, columns), FSDP, 0, 0)]
    all_to_all x0 -> x1, blocking collectives: none -> 26.1 us  [local(): parts = lax.all_to_all(parts, 'z', 0, 0)]
    all_to_all x0 -> x3, starting transfers between devices: none -> 19.4 us  [the longest x1 7.63 us: local(): lax.all_to_all(jnp.broadcast_to(squares, (256, 1, 128)), EVERY, 0, 0)]
    ppermute x0 -> x15, starting transfers between devices: none -> 17.7 us  [the longest x6 7.75 us: swap(): return lax.ppermute(values, axis, [(0, 1), (1, 0)])]
  transfers between devices with their start and end apart: 3 -> 18, of which waited for: 3 -> 12; matrix products, arithmetic and copies ran while one was open for 3% -> 12% of each run, Pallas kernels for 0% -> 3%
where the time goes in v1:
time: 197 us; the launch traced here: 196 us
  waiting for transfers between devices  83.5 us (42%)
  starting transfers between devices  37.1 us (19%)
  blocking collectives  26.1 us (13%)
  matrix products  14.6 us (7%)
  local copies, waits for them, and re-layouts  13.6 us (7%)
  other arithmetic  12.5 us (6%)
  Pallas kernels  6.55 us (3%)
    ppermute x4, waiting for transfers between devices, reduce_y(): got = lax.ppermute(away, 'y', PAIRING[first])  30.9 us
    all_to_all x1, blocking collectives, local(): parts = lax.all_to_all(parts, 'z', 0, 0)  26.1 us
    all_to_all x1, waiting for transfers between devices, local(): partial = lax.all_to_all(partial.reshape(64, states, columns), FSDP, 0, 0)  14.7 us
    dot_general x4, matrix products, product(): lax.dot_general(left, right, (((0,), (0,)), ((), ())), preferred_element_...  13.7 us
    all_to_all x1, waiting for transfers between devices, local(): hidden = lax.all_to_all(hidden, FSDP, 0, 0).reshape(64 * states, own_rows)  11.1 us
    ppermute x4, waiting for transfers between devices, reduce_y(): last = lax.ppermute(passed, 'y', PAIRING[second])  10.6 us
    all_to_all x1, waiting for transfers between devices, local(): lax.all_to_all(jnp.broadcast_to(squares, (256, 1, 128)), EVERY, 0, 0)  9.3 us
    ppermute x6, starting transfers between devices, swap(): return lax.ppermute(values, axis, [(0, 1), (1, 0)])  7.75 us
  transfers between devices with their start and end apart: 18, of which 12 were waited for; matrix products, arithmetic and copies ran while one was open for 12% of the time, Pallas kernels for 3%

profile of v1, /device:TPU:24, one launch (start us, length us, event | category | flops | bytes accessed | tf_op | source)
XLA Modules:
  0.0 196.0 jit_solution(649827416198808932)
XLA Ops:
  0.7 1.4 copy.107
  2.2 3.3 %convolution_convert_fusion.3 = bf16[1280,512]{1,0:T(8,128)(2,1)S(1)} fusion(bf16[1024,1280]{1,0:T(8,128)(2,1)} %param.11, bf16[1024,512]{1,0:T(8,128)(2,1)S(1)} %bitcast.192), kind=kOutput, calls=%fused_computation.3 | convolution fusion | flops 1342832640 | bytes 4980736 | tf_op jit(solution)/shard_map/gradient_own/dot_general | solution.py:167
  7.2 3.0 %collective-permute-start.7 = (bf16[1024,512]{1,0:T(8,128)(2,1)S(1)}, bf16[1024,512]{1,0:T(8,128)(2,1)}, u32[]{:S(2)}, u32[]{:S(2)}) collective-permute-start(bf16[1024,512]{1,0:T(8,128)(2,1)S(1)} %bitcast.193), channel_id=1, source_target_pairs={{0,2},{2,0},{1,3},{3,1},{4,6},{6,4},{5,7},{7,5},{8,10},{10,8},{9,1... | collective-permute-start | bytes 3145736 | tf_op jit(solution)/shard_map/exchange/ppermute | solution.py:71
  10.2 13.6 %collective-permute-done = bf16[2,2,2,80,512]{4,3,2,1,0:T(8,128)(2,1)S(1)} collective-permute-done((bf16[2,2,2,80,512]{4,3,2,1,0:T(8,128)(2,1)}, bf16[2,2,2,80,512]{4,3,2,1,0:T(8,128)(2,1)S(1)}, u32[]{:S(2)}, u32[]{:S(2)}) %collective-permute-start) | collective-permute-done | bytes 655392 | tf_op jit(solution)/shard_map/gradient_own/ppermute | solution.py:90
  23.9 2.1 %collective-permute-start.1 = (bf16[2,2,80,512]{3,2,1,0:T(8,128)(2,1)S(1)}, bf16[2,2,80,512]{3,2,1,0:T(8,128)(2,1)}, u32[]{:S(2)}, u32[]{:S(2)}) collective-permute-start(bf16[2,2,80,512]{3,2,1,0:T(8,128)(2,1)S(1)} %fusion.14), channel_id=1, source_target_pairs={{0,12},{12,0},{4,8},{8,4},{1,13},{13,1},{5,9},{9,5},{2,14},{14,2},... | collective-permute-start | bytes 983048 | tf_op jit(solution)/shard_map/gradient_own/ppermute | solution.py:93
  26.0 8.8 %collective-permute-done.1 = bf16[2,2,80,512]{3,2,1,0:T(8,128)(2,1)} collective-permute-done((bf16[2,2,80,512]{3,2,1,0:T(8,128)(2,1)S(1)}, bf16[2,2,80,512]{3,2,1,0:T(8,128)(2,1)}, u32[]{:S(2)}, u32[]{:S(2)}) %collective-permute-start.1) | collective-permute-done | bytes 327712 | tf_op jit(solution)/shard_map/gradient_own/ppermute | solution.py:93
  35.9 3.6 %convolution_convert_fusion.1 = bf16[1280,512]{1,0:T(8,128)(2,1)S(1)} fusion(bf16[1024,1280]{1,0:T(8,128)(2,1)} %param.11, bf16[1024,512]{1,0:T(8,128)(2,1)} %collective-permute-done.7), kind=kOutput, calls=%fused_computation.1 | convolution fusion | flops 1342832640 | bytes 4980736 | tf_op jit(solution)/shard_map/gradient_other/dot_general | solution.py:167
  39.5 3.3 %convolution_convert_fusion.2 = bf16[1280,512]{1,0:T(8,128)(2,1)S(1)} fusion(bf16[1024,1280]{1,0:T(8,128)(2,1)} %collective-permute-done.3, bf16[1024,512]{1,0:T(8,128)(2,1)S(1)} %bitcast.194), kind=kOutput, calls=%fused_computation.2 | convolution fusion | flops 1342832640 | bytes 4980736 | tf_op jit(solution)/shard_map/gradient_own/dot_general | solution.py:167
  43.9 2.0 %collective-permute-start.4 = (bf16[2,2,2,80,512]{4,3,1,2,0:T(8,128)(2,1)}, bf16[2,2,2,80,512]{4,3,1,2,0:T(8,128)(2,1)}, u32[]{:S(2)}, u32[]{:S(2)}) collective-permute-start(bf16[2,2,2,80,512]{4,3,1,2,0:T(8,128)(2,1)} %pad_maximum_fusion.1), channel_id=1, source_target_pairs={{0,12},{12,0},{4,8},{8,4},{1,13},{13,1},{5,9},{9,5},{2,14},{14,2},... | collective-permute-start | bytes 1966088 | tf_op jit(solution)/shard_map/gradient_own/ppermute | solution.py:90
  45.9 3.6 %convolution_convert_fusion = bf16[1280,512]{1,0:T(8,128)(2,1)S(1)} fusion(bf16[1024,1280]{1,0:T(8,128)(2,1)} %collective-permute-done.3, bf16[1024,512]{1,0:T(8,128)(2,1)} %collective-permute-done.7), kind=kOutput, calls=%fused_computation | convolution fusion | flops 1342832640 | bytes 4980736 | tf_op jit(solution)/shard_map/gradient_other/dot_general | solution.py:167
  50.9 2.8 %collective-permute-start.11 = (bf16[2,2,2,80,512]{4,3,1,2,0:T(8,128)(2,1)S(1)}, bf16[2,2,2,80,512]{4,3,1,2,0:T(8,128)(2,1)S(1)}, u32[]{:S(2)}, u32[]{:S(2)}) collective-permute-start(bf16[2,2,2,80,512]{4,3,1,2,0:T(8,128)(2,1)S(1)} %pad_maximum_fusion.3), channel_id=1, source_target_pairs={{0,12},{12,0},{4,8},{8,4},{1,13},{13,1},{5,9},{9,5},{2,14},{14,2},... | collective-permute-start | bytes 1966088 | tf_op jit(solution)/shard_map/gradient_other/ppermute | solution.py:90
  53.7 2.4 %collective-permute-done.2 = bf16[2,80,512]{2,1,0:T(8,128)(2,1)S(1)} collective-permute-done((bf16[2,80,512]{2,1,0:T(8,128)(2,1)S(1)}, bf16[2,80,512]{2,1,0:T(8,128)(2,1)S(1)}, u32[]{:S(2)}, u32[]{:S(2)}) %collective-permute-start.2) | collective-permute-done | bytes 163872 | tf_op jit(solution)/shard_map/gradient_own/ppermute | solution.py:71
  56.1 6.9 %collective-permute-done.4 = bf16[2,2,2,80,512]{4,3,1,2,0:T(8,128)(2,1)} collective-permute-done((bf16[2,2,2,80,512]{4,3,1,2,0:T(8,128)(2,1)}, bf16[2,2,2,80,512]{4,3,1,2,0:T(8,128)(2,1)}, u32[]{:S(2)}, u32[]{:S(2)}) %collective-permute-start.4) | collective-permute-done | bytes 655392 | tf_op jit(solution)/shard_map/gradient_own/ppermute | solution.py:90
  64.2 4.4 %collective-permute-done.8 = bf16[2,2,2,80,512]{4,3,1,2,0:T(8,128)(2,1)} collective-permute-done((bf16[2,2,2,80,512]{4,3,1,2,0:T(8,128)(2,1)}, bf16[2,2,2,80,512]{4,3,1,2,0:T(8,128)(2,1)}, u32[]{:S(2)}, u32[]{:S(2)}) %collective-permute-start.8) | collective-permute-done | bytes 655392 | tf_op jit(solution)/shard_map/gradient_other/ppermute | solution.py:90
  71.1 6.0 %collective-permute-done.11 = bf16[2,2,2,80,512]{4,3,1,2,0:T(8,128)(2,1)S(1)} collective-permute-done((bf16[2,2,2,80,512]{4,3,1,2,0:T(8,128)(2,1)S(1)}, bf16[2,2,2,80,512]{4,3,1,2,0:T(8,128)(2,1)S(1)}, u32[]{:S(2)}, u32[]{:S(2)}) %collective-permute-start.11) | collective-permute-done | bytes 655392 | tf_op jit(solution)/shard_map/gradient_other/ppermute | solution.py:90
  78.5 1.6 collective-permute-start.6
  80.1 1.8 collective-permute-done.9
  83.0 1.6 collective-permute-start.10
  84.8 1.4 collective-permute-start.13
  86.2 3.0 %collective-permute-done.10 = bf16[2,80,512]{2,1,0:T(8,128)(2,1)S(1)} collective-permute-done((bf16[2,80,512]{2,1,0:T(8,128)(2,1)S(1)}, bf16[2,80,512]{2,1,0:T(8,128)(2,1)S(1)}, u32[]{:S(2)}, u32[]{:S(2)}) %collective-permute-start.10) | collective-permute-done | bytes 163872 | tf_op jit(solution)/shard_map/gradient_other/ppermute | solution.py:71
  89.3 1.7 collective-permute-done.13
  91.2 26.1 %all_to_all.20 = bf16[8,80,512]{2,1,0:T(8,128)(2,1)S(1)} all-to-all(bf16[8,80,512]{2,1,0:T(8,128)(2,1)S(1)} %maximum_select_fusion), channel_id=1, replica_groups=mesh['z'=8,'xl'=2,'y'=4,'xh'=2,'core'=2] {'z'}, dimensions={0} | all-to-all | bytes 1310720 | tf_op jit(solution)/shard_map/reduce_z/all_to_all | solution.py:193
  118.1 1.4 broadcast_in_dim.14
  119.4 7.6 %all-to-all-start.1 = ((f32[256,1,128]{2,1,0:T(1,128)}), f32[256,1,128]{2,1,0:T(1,128)S(1)}, u32[]{:S(2)}, u32[]{:S(2)}) async-start(f32[256,1,128]{2,1,0:T(1,128)} %broadcast_in_dim.14), calls=%async_computation.1 | async-start | bytes 262144 | tf_op jit(solution)/shard_map/squares/all_to_all | solution.py:203
  129.2 9.3 %all-to-all-done.1 = f32[256,1,128]{2,1,0:T(1,128)S(1)} async-done(((f32[256,1,128]{2,1,0:T(1,128)}), f32[256,1,128]{2,1,0:T(1,128)S(1)}, u32[]{:S(2)}, u32[]{:S(2)}) %all-to-all-start.1) | async-done | bytes 131104 | tf_op jit(solution)/shard_map/squares/all_to_all | solution.py:203
  138.5 6.0 %all-to-all-start.2 = ((bf16[64,16,80]{2,1,0:T(8,128)(2,1)}), bf16[64,16,80]{2,1,0:T(8,128)(2,1)S(1)}, u32[]{:S(2)}, u32[]{:S(2)}) async-start(bf16[64,16,80]{2,1,0:T(8,128)(2,1)} %bitcast.177), calls=%async_computation.2 | async-start | bytes 524288 | tf_op jit(solution)/shard_map/hidden/all_to_all | solution.py:164
  146.3 11.1 %all-to-all-done.2 = bf16[64,16,80]{2,1,0:T(8,128)(2,1)S(1)} async-done(((bf16[64,16,80]{2,1,0:T(8,128)(2,1)}), bf16[64,16,80]{2,1,0:T(8,128)(2,1)S(1)}, u32[]{:S(2)}, u32[]{:S(2)}) %all-to-all-start.2) | async-done | bytes 163872 | tf_op jit(solution)/shard_map/hidden/all_to_all | solution.py:164
  159.2 5.8 %all-to-all-start.3 = ((bf16[64,16,512]{2,1,0:T(8,128)(2,1)}), bf16[64,16,512]{2,1,0:T(8,128)(2,1)S(1)}, u32[]{:S(2)}, u32[]{:S(2)}) async-start(bf16[64,16,512]{2,1,0:T(8,128)(2,1)} %bitcast.39), calls=%async_computation.3 | async-start | bytes 2097152 | tf_op jit(solution)/shard_map/project/all_to_all | solution.py:217
  165.1 2.2 %copy-done = bf16[4,2048,256]{2,1,0:T(8,128)(2,1)S(1)} copy-done((bf16[4,2048,256]{2,1,0:T(8,128)(2,1)S(1)}, bf16[4,2048,256]{2,1,0:T(8,128)(2,1)}, u32[]{:S(2)}) %copy-start) | copy-done | bytes 4194328
  167.2 2.2 %copy-done.1 = bf16[4,2048,256]{2,1,0:T(8,128)(2,1)S(1)} copy-done((bf16[4,2048,256]{2,1,0:T(8,128)(2,1)S(1)}, bf16[4,2048,256]{2,1,0:T(8,128)(2,1)}, u32[]{:S(2)}) %copy-start.1) | copy-done | bytes 4194328
  169.4 6.6 %old_attention.1 = (f32[4,2,32,128]{3,2,1,0:T(8,128)S(1)}, f32[4,2,32,128]{3,2,1,0:T(8,128)S(1)}, f32[4,2,32,128]{3,2,1,0:T(8,128)S(1)}) custom-call(s32[4]{0:T(128)S(1)} %copy-done.2, bf16[4,2,32,128]{3,2,1,0:T(8,128)(2,1)S(1)} %bitcast.180, bf16[4,2048,256]{2,1,0:T(8,128)(2,1)S(1)} %copy-done, bf16[4,2048,256]{2,1,0:T(8,128)(2,1)S(1)} %copy-done.1), custom_call_target="tpu_custom_call" | custom-call | tf_op jit(solution)/shard_map/old/old_attention/pallas_call | solution.py:118
  177.8 14.7 %all-to-all-done.3 = bf16[64,16,512]{2,1,0:T(8,128)(2,1)S(1)} async-done(((bf16[64,16,512]{2,1,0:T(8,128)(2,1)}), bf16[64,16,512]{2,1,0:T(8,128)(2,1)S(1)}, u32[]{:S(2)}, u32[]{:S(2)}) %all-to-all-start.3) | async-done | bytes 1048608 | tf_op jit(solution)/shard_map/project/all_to_all | solution.py:217
  (104 shorter events, 23.2 us)
Async XLA Ops:
  0.6 38.9 %collective-permute-start.3 = (bf16[1024,1280]{1,0:T(8,128)(2,1)}, bf16[1024,1280]{1,0:T(8,128)(2,1)}, u32[]{:S(2)}, u32[]{:S(2)}) collective-permute-start(bf16[1024,1280]{1,0:T(8,128)(2,1)} %param.11), channel_id=1, source_target_pairs={{0,1},{1,0},{2,3},{3,2},{4,5},{5,4},{6,7},{7,6},{8,9},{9,8},{10,11... | collective-permute-start | bytes 7864328 | tf_op jit(solution)/shard_map/exchange/ppermute | solution.py:71
  6.5 17.3 %collective-permute-start = (bf16[2,2,2,80,512]{4,3,2,1,0:T(8,128)(2,1)}, bf16[2,2,2,80,512]{4,3,2,1,0:T(8,128)(2,1)S(1)}, u32[]{:S(2)}, u32[]{:S(2)}) collective-permute-start(bf16[2,2,2,80,512]{4,3,2,1,0:T(8,128)(2,1)} %pad_maximum_fusion), channel_id=1, source_target_pairs={{0,4},{4,0},{8,12},{12,8},{1,5},{5,1},{9,13},{13,9},{2,6},{6,2},{1... | collective-permute-start | bytes 1966088 | tf_op jit(solution)/shard_map/gradient_own/ppermute | solution.py:90
  7.2 28.7 %collective-permute-start.7 = (bf16[1024,512]{1,0:T(8,128)(2,1)S(1)}, bf16[1024,512]{1,0:T(8,128)(2,1)}, u32[]{:S(2)}, u32[]{:S(2)}) collective-permute-start(bf16[1024,512]{1,0:T(8,128)(2,1)S(1)} %bitcast.193), channel_id=1, source_target_pairs={{0,2},{2,0},{1,3},{3,1},{4,6},{6,4},{5,7},{7,5},{8,10},{10,8},{9,1... | collective-permute-start | bytes 3145736 | tf_op jit(solution)/shard_map/exchange/ppermute | solution.py:71
  23.8 2.2 %copy-start.3 = (bf16[2,2,2,80,512]{4,3,2,1,0:T(8,128)(2,1)}, bf16[2,2,2,80,512]{4,3,2,1,0:T(8,128)(2,1)S(1)}, u32[]{:S(2)}) copy-start(bf16[2,2,2,80,512]{4,3,2,1,0:T(8,128)(2,1)S(1)} %collective-permute-done) | copy-start | bytes 1966084
  23.9 10.8 %collective-permute-start.1 = (bf16[2,2,80,512]{3,2,1,0:T(8,128)(2,1)S(1)}, bf16[2,2,80,512]{3,2,1,0:T(8,128)(2,1)}, u32[]{:S(2)}, u32[]{:S(2)}) collective-permute-start(bf16[2,2,80,512]{3,2,1,0:T(8,128)(2,1)S(1)} %fusion.14), channel_id=1, source_target_pairs={{0,12},{12,0},{4,8},{8,4},{1,13},{13,1},{5,9},{9,5},{2,14},{14,2},... | collective-permute-start | bytes 983048 | tf_op jit(solution)/shard_map/gradient_own/ppermute | solution.py:93
  43.9 19.2 %collective-permute-start.4 = (bf16[2,2,2,80,512]{4,3,1,2,0:T(8,128)(2,1)}, bf16[2,2,2,80,512]{4,3,1,2,0:T(8,128)(2,1)}, u32[]{:S(2)}, u32[]{:S(2)}) collective-permute-start(bf16[2,2,2,80,512]{4,3,1,2,0:T(8,128)(2,1)} %pad_maximum_fusion.1), channel_id=1, source_target_pairs={{0,12},{12,0},{4,8},{8,4},{1,13},{13,1},{5,9},{9,5},{2,14},{14,2},... | collective-permute-start | bytes 1966088 | tf_op jit(solution)/shard_map/gradient_own/ppermute | solution.py:90
  50.7 18.0 %collective-permute-start.8 = (bf16[2,2,2,80,512]{4,3,1,2,0:T(8,128)(2,1)}, bf16[2,2,2,80,512]{4,3,1,2,0:T(8,128)(2,1)}, u32[]{:S(2)}, u32[]{:S(2)}) collective-permute-start(bf16[2,2,2,80,512]{4,3,1,2,0:T(8,128)(2,1)} %pad_maximum_fusion.2), channel_id=1, source_target_pairs={{0,4},{4,0},{8,12},{12,8},{1,5},{5,1},{9,13},{13,9},{2,6},{6,2},{1... | collective-permute-start | bytes 1966088 | tf_op jit(solution)/shard_map/gradient_other/ppermute | solution.py:90
  50.7 5.4 %collective-permute-start.2 = (bf16[2,80,512]{2,1,0:T(8,128)(2,1)S(1)}, bf16[2,80,512]{2,1,0:T(8,128)(2,1)S(1)}, u32[]{:S(2)}, u32[]{:S(2)}) collective-permute-start(bf16[2,80,512]{2,1,0:T(8,128)(2,1)S(1)} %dynamic-slice_bitcast_fusion.5), channel_id=1, source_target_pairs={{0,16},{16,0},{1,17},{17,1},{2,18},{18,2},{3,19},{19,3},{4,20},{20... | collective-permute-start | bytes 491528 | tf_op jit(solution)/shard_map/gradient_own/ppermute | solution.py:71
  50.9 26.1 %collective-permute-start.11 = (bf16[2,2,2,80,512]{4,3,1,2,0:T(8,128)(2,1)S(1)}, bf16[2,2,2,80,512]{4,3,1,2,0:T(8,128)(2,1)S(1)}, u32[]{:S(2)}, u32[]{:S(2)}) collective-permute-start(bf16[2,2,2,80,512]{4,3,1,2,0:T(8,128)(2,1)S(1)} %pad_maximum_fusion.3), channel_id=1, source_target_pairs={{0,12},{12,0},{4,8},{8,4},{1,13},{13,1},{5,9},{9,5},{2,14},{14,2},... | collective-permute-start | bytes 1966088 | tf_op jit(solution)/shard_map/gradient_other/ppermute | solution.py:90
  64.1 13.3 %collective-permute-start.5 = (bf16[2,2,80,512]{3,2,0,1:T(8,128)(2,1)S(1)}, bf16[2,2,80,512]{3,2,0,1:T(8,128)(2,1)S(1)}, u32[]{:S(2)}, u32[]{:S(2)}) collective-permute-start(bf16[2,2,80,512]{3,2,0,1:T(8,128)(2,1)S(1)} %fusion.11), channel_id=1, source_target_pairs={{0,4},{4,0},{8,12},{12,8},{1,5},{5,1},{9,13},{13,9},{2,6},{6,2},{1... | collective-permute-start | bytes 983048 | tf_op jit(solution)/shard_map/gradient_own/ppermute | solution.py:93
  69.7 12.2 %collective-permute-start.9 = (bf16[2,2,80,512]{3,2,0,1:T(8,128)(2,1)S(1)}, bf16[2,2,80,512]{3,2,0,1:T(8,128)(2,1)S(1)}, u32[]{:S(2)}, u32[]{:S(2)}) collective-permute-start(bf16[2,2,80,512]{3,2,0,1:T(8,128)(2,1)S(1)} %fusion.8), channel_id=1, source_target_pairs={{0,12},{12,0},{4,8},{8,4},{1,13},{13,1},{5,9},{9,5},{2,14},{14,2},... | collective-permute-start | bytes 983048 | tf_op jit(solution)/shard_map/gradient_other/ppermute | solution.py:93
  77.1 7.5 %collective-permute-start.12 = (bf16[2,2,80,512]{3,2,0,1:T(8,128)(2,1)S(1)}, bf16[2,2,80,512]{3,2,0,1:T(8,128)(2,1)S(1)}, u32[]{:S(2)}, u32[]{:S(2)}) collective-permute-start(bf16[2,2,80,512]{3,2,0,1:T(8,128)(2,1)S(1)} %fusion.5), channel_id=1, source_target_pairs={{0,4},{4,0},{8,12},{12,8},{1,5},{5,1},{9,13},{13,9},{2,6},{6,2},{1... | collective-permute-start | bytes 983048 | tf_op jit(solution)/shard_map/gradient_other/ppermute | solution.py:93
  78.5 7.7 %collective-permute-start.6 = (bf16[2,80,512]{2,1,0:T(8,128)(2,1)S(1)}, bf16[2,80,512]{2,1,0:T(8,128)(2,1)S(1)}, u32[]{:S(2)}, u32[]{:S(2)}) collective-permute-start(bf16[2,80,512]{2,1,0:T(8,128)(2,1)S(1)} %dynamic-slice_bitcast_fusion.4), channel_id=1, source_target_pairs={{0,16},{16,0},{1,17},{17,1},{2,18},{18,2},{3,19},{19,3},{4,20},{20... | collective-permute-start | bytes 491528 | tf_op jit(solution)/shard_map/gradient_own/ppermute | solution.py:71
  83.0 6.1 %collective-permute-start.10 = (bf16[2,80,512]{2,1,0:T(8,128)(2,1)S(1)}, bf16[2,80,512]{2,1,0:T(8,128)(2,1)S(1)}, u32[]{:S(2)}, u32[]{:S(2)}) collective-permute-start(bf16[2,80,512]{2,1,0:T(8,128)(2,1)S(1)} %dynamic-slice_bitcast_fusion.3), channel_id=1, source_target_pairs={{0,16},{16,0},{1,17},{17,1},{2,18},{18,2},{3,19},{19,3},{4,20},{20... | collective-permute-start | bytes 491528 | tf_op jit(solution)/shard_map/gradient_other/ppermute | solution.py:71
  84.8 6.2 %collective-permute-start.13 = (bf16[2,80,512]{2,1,0:T(8,128)(2,1)S(1)}, bf16[2,80,512]{2,1,0:T(8,128)(2,1)S(1)}, u32[]{:S(2)}, u32[]{:S(2)}) collective-permute-start(bf16[2,80,512]{2,1,0:T(8,128)(2,1)S(1)} %dynamic-slice_bitcast_fusion.2), channel_id=1, source_target_pairs={{0,16},{16,0},{1,17},{17,1},{2,18},{18,2},{3,19},{19,3},{4,20},{20... | collective-permute-start | bytes 491528 | tf_op jit(solution)/shard_map/gradient_other/ppermute | solution.py:71
  89.3 37.8 %copy-start.4 = (f32[80,2,256]{2,1,0:T(2,128)S(1)}, f32[80,2,256]{2,1,0:T(2,128)}, u32[]{:S(2)}) copy-start(f32[80,2,256]{2,1,0:T(2,128)} %param.14) | copy-start | bytes 491524
  91.0 36.8 %copy-start.5 = (f32[80,2,256]{2,1,0:T(2,128)S(1)}, f32[80,2,256]{2,1,0:T(2,128)}, u32[]{:S(2)}) copy-start(f32[80,2,256]{2,1,0:T(2,128)} %param.15) | copy-start | bytes 491524
  91.0 36.9 %copy-start.6 = (f32[80,2,256]{2,1,0:T(2,128)S(1)}, f32[80,2,256]{2,1,0:T(2,128)}, u32[]{:S(2)}) copy-start(f32[80,2,256]{2,1,0:T(2,128)} %param.13) | copy-start | bytes 491524
  91.1 37.0 %copy-start.7 = (bf16[4,4,5120]{2,1,0:T(4,128)(2,1)S(1)}, bf16[4,4,5120]{2,1,0:T(4,128)(2,1)}, u32[]{:S(2)}) copy-start(bf16[4,4,5120]{2,1,0:T(4,128)(2,1)} %param.16) | copy-start | bytes 491524
  119.4 19.1 %all-to-all-start.1 = ((f32[256,1,128]{2,1,0:T(1,128)}), f32[256,1,128]{2,1,0:T(1,128)S(1)}, u32[]{:S(2)}, u32[]{:S(2)}) async-start(f32[256,1,128]{2,1,0:T(1,128)} %broadcast_in_dim.14), calls=%async_computation.1 | async-start | bytes 262144 | tf_op jit(solution)/shard_map/squares/all_to_all | solution.py:203
  127.2 19.0 %collective-permute-start.14 = (f32[80,512]{1,0:T(8,128)S(1)}, f32[80,512]{1,0:T(8,128)S(1)}, u32[]{:S(2)}, u32[]{:S(2)}) collective-permute-start(f32[80,512]{1,0:T(8,128)S(1)} %get-tuple-element.30), channel_id=1, source_target_pairs={{0,0},{2,128},{32,32},{34,160},{64,64},{66,192},{96,96},{98,224},{... | collective-permute-start | bytes 491528 | tf_op jit(solution)/shard_map/place/ppermute | solution.py:200
  138.5 18.8 %all-to-all-start.2 = ((bf16[64,16,80]{2,1,0:T(8,128)(2,1)}), bf16[64,16,80]{2,1,0:T(8,128)(2,1)S(1)}, u32[]{:S(2)}, u32[]{:S(2)}) async-start(bf16[64,16,80]{2,1,0:T(8,128)(2,1)} %bitcast.177), calls=%async_computation.2 | async-start | bytes 524288 | tf_op jit(solution)/shard_map/hidden/all_to_all | solution.py:164
  157.4 7.6 %copy-start.8 = (bf16[4,4,2048]{2,1,0:T(4,128)(2,1)S(1)}, bf16[4,4,2048]{2,1,0:T(4,128)(2,1)}, u32[]{:S(2)}) copy-start(bf16[4,4,2048]{2,1,0:T(4,128)(2,1)} %param.17) | copy-start | bytes 196612
  157.4 7.7 %copy-start.2 = (s32[4]{0:T(128)S(1)}, s32[4]{0:T(128)}, u32[]{:S(2)}) copy-start(s32[4]{0:T(128)} %length_ref.1) | copy-start | bytes 52
  159.2 33.3 %all-to-all-start.3 = ((bf16[64,16,512]{2,1,0:T(8,128)(2,1)}), bf16[64,16,512]{2,1,0:T(8,128)(2,1)S(1)}, u32[]{:S(2)}, u32[]{:S(2)}) async-start(bf16[64,16,512]{2,1,0:T(8,128)(2,1)} %bitcast.39), calls=%async_computation.3 | async-start | bytes 2097152 | tf_op jit(solution)/shard_map/project/all_to_all | solution.py:217
  165.1 2.2 %copy-start = (bf16[4,2048,256]{2,1,0:T(8,128)(2,1)S(1)}, bf16[4,2048,256]{2,1,0:T(8,128)(2,1)}, u32[]{:S(2)}) copy-start(bf16[4,2048,256]{2,1,0:T(8,128)(2,1)} %key_ref.1) | copy-start | bytes 12582916
  167.2 2.2 %copy-start.1 = (bf16[4,2048,256]{2,1,0:T(8,128)(2,1)S(1)}, bf16[4,2048,256]{2,1,0:T(8,128)(2,1)}, u32[]{:S(2)}) copy-start(bf16[4,2048,256]{2,1,0:T(8,128)(2,1)} %value_ref.1) | copy-start | bytes 12582916
  169.4 23.4 %copy-start.9 = (f32[128]{0:T(128)S(1)}, f32[128]{0:T(128)}, u32[]{:S(2)}) copy-start(f32[128]{0:T(128)} %param.21) | copy-start | bytes 1540

commit v2 on v1

v2 whole, which is shorter than its diff:
```python
import functools
import math

import jax
import jax.numpy as jnp
from jax import lax
from jax.experimental import pallas as pl
from jax.experimental.pallas import tpu as pltpu
from jax.sharding import Mesh
from jax.sharding import PartitionSpec as P

QH = 64
KVH = 8
HD = 128

beta_one = 0.9
beta_two = 0.999
learn_rate = 0.001
decay_rate = 0.1
adam_eps = 1e-08
step_number = 10.0
clip_rms = 0.001
norm_eps = 1e-06
rope_base = 1000000.0

SIZES = {"z": 8, "xl": 2, "y": 4, "xh": 2, "core": 2}
FSDP = ("z", "xl", "y")
TP = ("xh", "core")
EVERY = FSDP + TP

BF16 = jnp.bfloat16
F32 = jnp.float32


def adamw_update(weight, gradient, moment_one, moment_two, factor):
    clipped = gradient * factor
    first_moment = beta_one * moment_one + (1.0 - beta_one) * clipped
    second_moment = beta_two * moment_two + (1.0 - beta_two) * clipped * clipped
    first_hat = first_moment / (1.0 - beta_one**step_number)
    second_hat = second_moment / (1.0 - beta_two**step_number)
    direction = first_hat / (jnp.sqrt(second_hat) + adam_eps) + decay_rate * weight
    return (weight - learn_rate * direction, direction)


def swap(values, axis):
    return lax.ppermute(values, axis, [(0, 1), (1, 0)])


PAIRING = ([(0, 1), (1, 0), (2, 3), (3, 2)], [(0, 3), (3, 0), (1, 2), (2, 1)])


def partner(position, pairing):
    return position ^ 1 if pairing == 0 else 3 - position


def in_hbm(values):
    return pltpu.with_memory_space_constraint(values, pltpu.HBM)


def product_kernel(order, left_ref, right_ref, away_ref, near_ref, mine_ref, total_ref):
    total_ref[...] = lax.dot_general(
        left_ref[...], right_ref[...], (((0,), (0,)), ((), ())), preferred_element_type=F32
    )
    rows = mine_ref.shape[2]
    for x in range(2):
        for slot in range(4):
            at = pl.multiple_of((x * 4 + order[slot]) * rows, rows)
            block = total_ref[pl.ds(at, rows), :].astype(BF16)
            if slot < 2:
                away_ref[slot, 0, x] = block
            elif slot == 2:
                near_ref[0, x] = block
            else:
                mine_ref[0, x] = block


def product(left, right, pairing, rows):
    tokens, columns = right.shape
    me = lax.axis_index("y")
    far = partner(me, pairing)
    near = partner(me, 1 - pairing)
    order = jnp.stack([partner(far, 1 - pairing), far, near, me]).astype(jnp.int32)
    part = pltpu.HBM((2, 2, rows, columns), BF16)
    part_spec = pl.BlockSpec((1, 2, rows, columns), lambda k, order: (k, 0, 0, 0))
    return pl.pallas_call(
        product_kernel,
        out_shape=(pltpu.HBM((2, 2, 2, rows, columns), BF16), part, part),
        grid_spec=pltpu.PrefetchScalarGridSpec(
            num_scalar_prefetch=1,
            grid=(2,),
            in_specs=[
                pl.BlockSpec((tokens, 8 * rows), lambda k, order: (0, k)),
                pl.BlockSpec((tokens, columns), lambda k, order: (0, 0)),
            ],
            out_specs=[
                pl.BlockSpec((2, 1, 2, rows, columns), lambda k, order: (0, k, 0, 0, 0)),
                part_spec,
                part_spec,
            ],
            scratch_shapes=[pltpu.VMEM((8 * rows, columns), F32)],
        ),
        compiler_params=pltpu.CompilerParams(vmem_limit_bytes=24 * 1024 * 1024),
        name="product",
    )(order, in_hbm(left), in_hbm(right))


def add(*values):
    total = values[0].astype(F32)
    for value in values[1:]:
        total = total + value.astype(F32)
    return total.astype(BF16)


def along_y(values, pairing):
    return lax.ppermute(values, "y", PAIRING[pairing])


def together(*values):
    return lax.optimization_barrier(values)


def old_attention_kernel(length_ref, query_ref, key_ref, value_ref, out_ref, top_ref, total_ref):
    length = length_ref[pl.program_id(0)]
    scores = lax.dot_general(
        query_ref[0, 0], key_ref[0], (((1,), (1,)), ((), ())), preferred_element_type=F32
    ) * (1.0 / math.sqrt(HD))
    slot = lax.broadcasted_iota(jnp.int32, scores.shape, 1)
    scores = jnp.where(slot < length, scores, -jnp.inf)
    top = jnp.max(scores, axis=-1, keepdims=True)
    weights = jnp.exp(scores - top)
    total = jnp.sum(weights, axis=-1, keepdims=True)
    out_ref[0, 0] = jnp.dot(weights.astype(BF16), value_ref[0], preferred_element_type=F32)
    top_ref[0, 0] = jnp.broadcast_to(top, top_ref.shape[2:])
    total_ref[0, 0] = jnp.broadcast_to(total, total_ref.shape[2:])


def old_attention(query_heads, cache_keys, cache_values, cache_lengths):
    heads, rows, queries, _ = query_heads.shape
    cache = cache_keys.shape[1]
    small = pl.BlockSpec((1, 1, queries, HD), lambda r, h, lengths: (h, r, 0, 0))
    large = pl.BlockSpec((1, cache, HD), lambda r, h, lengths: (r, 0, h))
    shape = jax.ShapeDtypeStruct((heads, rows, queries, HD), F32)
    return pl.pallas_call(
        old_attention_kernel,
        out_shape=(shape, shape, shape),
        grid_spec=pltpu.PrefetchScalarGridSpec(
            num_scalar_prefetch=1,
            grid=(rows, heads),
            in_specs=[small, large, large],
            out_specs=[small, small, small],
        ),
        compiler_params=pltpu.CompilerParams(vmem_limit_bytes=24 * 1024 * 1024),
        name="old_attention",
    )(cache_lengths, query_heads, in_hbm(cache_keys), in_hbm(cache_values))


def fresh_kernel(
    part_ref,
    query_ref,
    old_sum_ref,
    old_top_ref,
    old_total_ref,
    gain_ref,
    cosine_ref,
    sine_ref,
    keys_ref,
    values_ref,
    attended_ref,
    mixed_ref,
    *,
    steps,
):
    heads, queries, _ = query_ref.shape
    states = part_ref.shape[1]
    groups = queries // states
    projected = jnp.sum(part_ref[...].astype(F32), axis=0)
    query = lax.broadcasted_iota(jnp.int32, (queries, states), 0)
    key = lax.broadcasted_iota(jnp.int32, (queries, states), 1)
    row_queries = groups * steps
    valid = (query // row_queries == key // steps) & (query % steps >= key % steps)
    for head in range(heads):
        at = slice(head * HD, (head + 1) * HD)
        raw = projected[:, at]
        mean = jnp.mean(raw * raw, axis=-1, keepdims=True)
        normed = raw * lax.rsqrt(mean + norm_eps) * gain_ref[...]
        turned = normed * cosine_ref[...] + pltpu.roll(normed, HD // 2, 1) * sine_ref[...]
        keys = turned.astype(BF16)
        values = projected[:, heads * HD + head * HD : heads * HD + (head + 1) * HD].astype(BF16)
        keys_ref[:, at] = keys
        values_ref[:, at] = values
        scores = lax.dot_general(
            query_ref[head], keys, (((1,), (1,)), ((), ())), preferred_element_type=F32
        ) * (1.0 / math.sqrt(HD))
        scores = jnp.where(valid, scores, -jnp.inf)
        old_top = old_top_ref[head]
        top = jnp.maximum(old_top, jnp.max(scores, axis=-1, keepdims=True))
        exps = jnp.exp(scores - top[:, :1])
        old_scale = jnp.exp(old_top - top)
        inverse = 1.0 / (old_total_ref[head] * old_scale + jnp.sum(exps, axis=-1, keepdims=True))
        weights = (exps * inverse[:, :1]).astype(BF16)
        mixed = old_sum_ref[head] * (old_scale * inverse)
        mixed = mixed + jnp.dot(weights, values, preferred_element_type=F32)
        for row in range(states // steps):
            for group in range(groups):
                column = (head * groups + group) * HD
                source = row * row_queries + group * steps
                mixed_ref[row * steps : (row + 1) * steps, column : column + HD] = mixed[
                    source : source + steps
                ]
    attended_ref[...] = mixed_ref[...].astype(BF16)


def fresh_attention(parts, query_heads, old_sum, old_top, old_total, key_gain, cosine, sine, steps):
    heads, queries, _ = query_heads.shape
    states = parts.shape[1]
    return pl.pallas_call(
        functools.partial(fresh_kernel, steps=steps),
        out_shape=(
            jax.ShapeDtypeStruct((states, heads * HD), BF16),
            jax.ShapeDtypeStruct((states, heads * HD), BF16),
            jax.ShapeDtypeStruct((states, heads * queries // states * HD), BF16),
        ),
        scratch_shapes=[pltpu.VMEM((states, heads * queries // states * HD), F32)],
        compiler_params=pltpu.CompilerParams(vmem_limit_bytes=24 * 1024 * 1024),
        name="fresh_attention",
    )(parts, query_heads, old_sum, old_top, old_total, key_gain, cosine, sine)


def gradient_kernel(parts_ref, gradient_ref, squares_ref, *, total_tokens):
    gradient = jnp.sum(parts_ref[...].astype(F32), axis=0) / total_tokens
    gradient_ref[...] = gradient
    squares_ref[...] = jnp.broadcast_to(jnp.sum(gradient * gradient), squares_ref.shape)


def sum_gradient(parts, total_tokens, devices):
    return pl.pallas_call(
        functools.partial(gradient_kernel, total_tokens=total_tokens),
        out_shape=(
            jax.ShapeDtypeStruct(parts.shape[1:], F32),
            jax.ShapeDtypeStruct((devices, HD), F32),
        ),
        compiler_params=pltpu.CompilerParams(vmem_limit_bytes=24 * 1024 * 1024),
        name="sum_gradient",
    )(parts)


def update_kernel(
    squares_ref, gradient_ref, state_ref, weight_ref, step_ref, rollout_ref, *, entries
):
    squares = jnp.sum(squares_ref[...], axis=0, keepdims=True)[:, :1]
    factor = jnp.minimum(1.0, clip_rms / jnp.sqrt(squares / entries + norm_eps))
    rows = weight_ref.shape[0]
    new_weight, adam_step = adamw_update(
        state_ref[:rows],
        gradient_ref[...],
        state_ref[rows : 2 * rows],
        state_ref[2 * rows :],
        factor,
    )
    weight_ref[...] = new_weight
    step_ref[...] = adam_step
    rollout_ref[...] = new_weight.astype(BF16)


def update(squares, gradient, state, entries):
    own = jax.ShapeDtypeStruct(gradient.shape, F32)
    return pl.pallas_call(
        functools.partial(update_kernel, entries=entries),
        out_shape=(own, own, jax.ShapeDtypeStruct(gradient.shape, BF16)),
        compiler_params=pltpu.CompilerParams(vmem_limit_bytes=24 * 1024 * 1024),
        name="update",
    )(squares, gradient, state)


def project_kernel(hidden_ref, *refs):
    weights = jnp.concatenate([ref[...] for ref in refs[:-1]])
    partial = jnp.dot(hidden_ref[...], weights, preferred_element_type=F32)
    refs[-1][...] = partial.astype(BF16)


def project(hidden, weights):
    return pl.pallas_call(
        project_kernel,
        out_shape=jax.ShapeDtypeStruct((hidden.shape[0], weights[0].shape[1]), BF16),
        compiler_params=pltpu.CompilerParams(vmem_limit_bytes=24 * 1024 * 1024),
        name="project",
    )(hidden, *weights)


def local(
    tokens,
    grad_out,
    weight,
    moment_one,
    moment_two,
    rollout_hidden,
    queries,
    cache_keys,
    cache_values,
    cache_lengths,
    key_gain,
):
    token_count = tokens.shape[0]
    total_tokens = token_count * 64
    own_rows = weight.shape[0]
    columns = weight.shape[1] * weight.shape[2]
    entry_count = own_rows * 64 * columns * 4
    z = lax.axis_index("z")
    xl = lax.axis_index("xl")
    xh = lax.axis_index("xh")
    core = lax.axis_index("core")

    with jax.named_scope("exchange"):
        upstream_other = swap(grad_out, "xh")
        tokens_other = swap(tokens, "core")
        upstream = grad_out.reshape(token_count, columns)

    row_count, step_count, model_width = rollout_hidden.shape
    states = row_count * step_count
    head_count = weight.shape[2] // HD
    groups = QH // KVH

    def by_xl(first, second):
        block = jnp.stack([first, second])
        kept = lax.dynamic_index_in_dim(block, xl, axis=2, keepdims=False)
        sent = lax.dynamic_index_in_dim(block, 1 - xl, axis=2, keepdims=False)
        return kept, sent

    def in_order(block):
        return jnp.where(core == 0, block, block[::-1]).reshape(4, own_rows, columns)

    def from_y(values, step):
        return lax.ppermute(values, "y", [(a, a ^ step) for a in range(4)])

    with jax.named_scope("first_half"):
        away, one_near, one_mine = product(tokens, upstream, 0, own_rows)
        away, tokens_other, queries, rollout_hidden = together(
            away, tokens_other, queries, rollout_hidden
        )
        one_got = along_y(away, 0)
        away, two_near, two_mine = product(tokens_other, upstream, 1, own_rows)
        two_near, rollout_hidden, weight, moment_one, moment_two = together(
            two_near, rollout_hidden, weight, moment_one, moment_two
        )
        two_got = along_y(away, 1)
    def trade(block, axis, bit, partners):
        mesh_axis = "xl" if bit is None else "z"
        mine = xl if bit is None else (z >> bit) & 1
        kept = lax.dynamic_index_in_dim(block, mine, axis=axis, keepdims=False)
        sent = lax.dynamic_index_in_dim(block, 1 - mine, axis=axis, keepdims=False)
        got = lax.ppermute(sent, mesh_axis, partners)
        return jnp.where(
            mine == 0, jnp.stack([kept, got], axis=axis), jnp.stack([got, kept], axis=axis)
        )

    def trade_z(block, bit):
        return trade(block, 2 - bit, bit, [(a, a ^ (1 << bit)) for a in range(8)])

    with jax.named_scope("hidden"):
        hidden = rollout_hidden.reshape(states, 16, 4 * own_rows).transpose(1, 0, 2)
        hidden = hidden.reshape(2, 2, 2, 2, states, 4 * own_rows)
        hidden = trade(hidden, 3, None, [(0, 1), (1, 0)])
        hidden = trade_z(hidden, 0)
    with jax.named_scope("state"):
        query_heads = queries.reshape(row_count, step_count, head_count, groups, HD)
        query_heads = query_heads.transpose(2, 0, 3, 1, 4)
        query_heads = query_heads.reshape(head_count, row_count, groups * step_count, HD)
        state = jnp.concatenate([weight, moment_one, moment_two]).reshape(3 * own_rows, columns)
    with jax.named_scope("first_half"):
        one_got, two_near, hidden, query_heads, state, upstream_other = together(
            one_got, two_near, hidden, query_heads, state, upstream_other
        )
        one_passed = add(one_near, one_got[0])
        two_passed = add(two_near, two_got[0])
        one_passed, two_passed, upstream_other = together(one_passed, two_passed, upstream_other)
        one_last = along_y(one_passed, 1)
        two_last = along_y(two_passed, 0)
    with jax.named_scope("second_half"):
        upstream_other = upstream_other.reshape(token_count, columns)
        away, three_near, three_mine = product(tokens, upstream_other, 0, own_rows)
        away, tokens_other = together(away, tokens_other)
        three_got = along_y(away, 0)
        away, four_near, four_mine = product(tokens_other, upstream_other, 1, own_rows)
        away, one_last, two_last, hidden = together(away, one_last, two_last, hidden)
        four_got = along_y(away, 1)
    with jax.named_scope("first_half"):
        kept, sent = by_xl(add(one_mine, one_got[1], one_last), add(two_mine, two_got[1], two_last))
        arrived = swap(sent, "xl")
    with jax.named_scope("hidden"):
        hidden = trade_z(trade_z(hidden, 1), 2)
        y = lax.axis_index("y")
        hidden = hidden.reshape(16 * states, 4, own_rows)
        hidden = jnp.concatenate(
            [
                lax.dynamic_index_in_dim(hidden, y ^ step, axis=1, keepdims=False)
                for step in range(4)
            ],
            axis=1,
        )
    with jax.named_scope("second_half"):
        three_got, four_near, hidden = together(three_got, four_near, hidden)
        three_passed = add(three_near, three_got[0])
        four_passed = add(four_near, four_got[0])
        three_passed, four_passed, arrived = together(three_passed, four_passed, arrived)
        three_last = along_y(three_passed, 1)
        four_last = along_y(four_passed, 0)
    with jax.named_scope("first_half"):
        first = in_order(add(kept, arrived))
    with jax.named_scope("second_half"):
        three_last, first = together(three_last, first)
        kept, sent = by_xl(
            add(three_mine, three_got[1], three_last), add(four_mine, four_got[1], four_last)
        )
        second = in_order(add(kept, swap(sent, "xl")))
    with jax.named_scope("reduce_z"):
        parts = jnp.where(
            xh == 0, jnp.concatenate([first, second]), jnp.concatenate([second, first])
        )
        parts = lax.all_to_all(parts, "z", 0, 0)
        gradient, squares = sum_gradient(parts, total_tokens, 256)
    with jax.named_scope("squares"):
        squares = lax.all_to_all(squares, EVERY, 0, 0, tiled=True)
    with jax.named_scope("place"):
        pairs = [(a * 2 + b, (a + 4) % 8 * 2 + 1 - b) for a in range(8) for b in range(2) if a // 4 != b]
        placed = lax.ppermute(gradient, ("z", "xh"), pairs)
        gradient = jnp.where(z // 4 == xh, gradient, placed)
        gradient, squares = together(gradient, squares)
    with jax.named_scope("update"):
        new_weight, adam_step, rollout_weight = update(
            squares, gradient, state, float(entry_count)
        )
    with jax.named_scope("project"):
        weights = [rollout_weight] + [from_y(rollout_weight, step) for step in range(1, 4)]
        partial = project(hidden, weights)
        partial, query_heads = together(partial, query_heads)
        partial = lax.all_to_all(partial.reshape(16, states, columns), ("z", "xl"), 0, 0)
    with jax.named_scope("old"):
        old = old_attention(query_heads, cache_keys, cache_values, cache_lengths)

        def flat(values):
            return values.reshape(head_count, groups * states, HD)

        half_width = HD // 2
        frequency = rope_base ** (-2.0 * jnp.arange(half_width, dtype=F32) / HD)
        positions = cache_lengths[:, None] + jnp.arange(step_count, dtype=jnp.int32)[None, :]
        angles = positions.astype(F32).reshape(states, 1) * frequency
        cosine = jnp.cos(angles)
        sine = jnp.sin(angles)
        cosine = jnp.concatenate([cosine, cosine], axis=-1)
        sine = jnp.concatenate([-sine, sine], axis=-1)
    with jax.named_scope("fresh"):
        new_keys, new_values, attended = fresh_attention(
            partial,
            flat(query_heads),
            *[flat(values) for values in old],
            key_gain.reshape(1, HD),
            cosine,
            sine,
            step_count,
        )
        new_keys = new_keys.reshape(row_count, step_count, head_count * HD)
        new_values = new_values.reshape(row_count, step_count, head_count * HD)
        attended = attended.reshape(row_count, step_count, head_count * groups * HD)
    return (
        new_weight.reshape(own_rows, 2, columns // 2),
        adam_step.reshape(own_rows, 2, columns // 2),
        new_keys,
        new_values,
        attended,
    )


def solution(mesh):
    fine = Mesh(mesh.devices.reshape(tuple(SIZES.values())), tuple(SIZES))
    in_specs = (
        P(FSDP, TP),
        P(FSDP, None, TP),
        P(FSDP, None, TP),
        P(FSDP, None, TP),
        P(FSDP, None, TP),
        P(FSDP, None, None),
        P(FSDP, None, TP),
        P(FSDP, None, TP),
        P(FSDP, None, TP),
        P(FSDP),
        P(),
    )
    out_specs = (P(FSDP, None, TP),) * 5
    return jax.shard_map(local, mesh=fine, in_specs=in_specs, out_specs=out_specs, check_vma=False)
```

time: 197 us -> 174 us (0.88)
  waiting for transfers between devices: 83.5 us -> 44 us
  Pallas kernels: 6.55 us -> 31.7 us
  matrix products: 14.6 us -> 0 us
  starting transfers between devices: 37.1 us -> 50.1 us
  blocking collectives: 26.1 us -> 19.5 us
    pallas_call x0 -> x8, Pallas kernels: none -> 23.3 us  [the longest x4 19.8 us: product(): pl.pallas_call(product_kernel, out_shape=(pltpu.HBM((2, 2, 2, rows, colum...]
    all_to_all x3 -> x2, waiting for transfers between devices: 35.1 us -> 13.2 us  [the longest x1 11.4 us: local(): squares = lax.all_to_all(squares, EVERY, 0, 0, tiled=True)]
    ppermute x8 -> x15, waiting for transfers between devices: 41.5 us -> 23.8 us  [the longest x8 9.77 us: along_y(): return lax.ppermute(values, 'y', PAIRING[pairing])]
    ppermute x8 -> x15, starting transfers between devices: 9.27 us -> 26.5 us  [the longest x4 12.1 us: trade(): got = lax.ppermute(sent, mesh_axis, partners)]
    dot_general x7 -> x0, matrix products: 14.6 us -> none  [the longest x4 13.7 us: product(): lax.dot_general(left, right, (((0,), (0,)), ((), ())), preferred_element_...]
    all_to_all x1, blocking collectives: 26.1 us -> 19.5 us  [local(): parts = lax.all_to_all(parts, 'z', 0, 0)]
    all_to_all x3 -> x2, starting transfers between devices: 19.4 us -> 16.7 us  [the longest x1 13.2 us: local(): squares = lax.all_to_all(squares, EVERY, 0, 0, tiled=True)]
    optimization_barrier x0 -> x1, local copies, waits for them, and re-layouts: none -> 2.47 us  [together(): return lax.optimization_barrier(values)]
  transfers between devices with their start and end apart: 18 -> 22, of which waited for: 12 -> 13; matrix products, arithmetic and copies ran while one was open for 12% -> 13% of each run, Pallas kernels for 3% -> 16%
where the time goes in v2:
time: 174 us; the launch traced here: 173 us
  starting transfers between devices  50.1 us (29%)
  waiting for transfers between devices  44 us (25%)
  Pallas kernels  31.7 us (18%)
  blocking collectives  19.5 us (11%)
  local copies, waits for them, and re-layouts  14.8 us (9%)
  other arithmetic  11.9 us (7%)
    pallas_call x4, Pallas kernels, product(): pl.pallas_call(product_kernel, out_shape=(pltpu.HBM((2, 2, 2, rows, colum...  19.8 us
    all_to_all x1, blocking collectives, local(): parts = lax.all_to_all(parts, 'z', 0, 0)  19.5 us
    all_to_all x1, starting transfers between devices, local(): squares = lax.all_to_all(squares, EVERY, 0, 0, tiled=True)  13.2 us
    ppermute x4, starting transfers between devices, trade(): got = lax.ppermute(sent, mesh_axis, partners)  12.1 us
    all_to_all x1, waiting for transfers between devices, local(): squares = lax.all_to_all(squares, EVERY, 0, 0, tiled=True)  11.4 us
    ppermute x8, waiting for transfers between devices, along_y(): return lax.ppermute(values, 'y', PAIRING[pairing])  9.77 us
    ppermute x8, starting transfers between devices, along_y(): return lax.ppermute(values, 'y', PAIRING[pairing])  9.58 us
    ppermute x4, waiting for transfers between devices, trade(): got = lax.ppermute(sent, mesh_axis, partners)  9.41 us
  transfers between devices with their start and end apart: 22, of which 13 were waited for; matrix products, arithmetic and copies ran while one was open for 13% of the time, Pallas kernels for 16%

profile of v2, /device:TPU:24, one launch (start us, length us, event | category | flops | bytes accessed | tf_op | source)
XLA Modules:
  0.0 173.0 jit_solution(12756546492946416964)
XLA Ops:
  0.7 3.1 %collective-permute-start.4 = (bf16[1024,2,256]{2,1,0:T(2,128)(2,1)}, bf16[1024,2,256]{2,1,0:T(2,128)(2,1)}, u32[]{:S(2)}, u32[]{:S(2)}) collective-permute-start(bf16[1024,2,256]{2,1,0:T(2,128)(2,1)} %param.12), channel_id=1, source_target_pairs={{0,2},{2,0},{1,3},{3,1},{4,6},{6,4},{5,7},{7,5},{8,10},{10,8},{9,1... | collective-permute-start | bytes 3145736 | tf_op jit(solution)/shard_map/exchange/ppermute | solution.py:46
  3.8 2.5 %copy.89 = bf16[128,8,2,256]{3,1,2,0:T(8,128)(2,1)} copy(bf16[128,8,2,256]{3,2,1,0:T(2,128)(2,1)} %bitcast.129) | data formatting | bytes 2097152
  6.4 4.9 %product.4 = (bf16[2,2,2,80,512]{4,3,2,1,0:T(8,128)(2,1)}, bf16[2,2,80,512]{3,2,1,0:T(8,128)(2,1)}, bf16[2,2,80,512]{3,2,1,0:T(8,128)(2,1)}) custom-call(s32[4]{0:T(128)S(1)} %get-tuple-element.138.order, bf16[1024,1280]{1,0:T(8,128)(2,1)} %left_ref.3, bf16[1024,512]{1,0:T(8,128)(2,1)} %bitcast.122), custom_call_target="tpu_custom_call" | custom-call | tf_op jit(solution)/shard_map/first_half/product/pallas_call | solution.py:85
  11.3 2.5 %copy.67 = bf16[2,2,2,80,512]{4,3,1,2,0:T(8,128)(2,1)} copy(bf16[2,2,2,80,512]{4,3,2,1,0:T(8,128)(2,1)} %get-tuple-element.66) | data formatting | bytes 1310720 | tf_op jit(solution)/shard_map/first_half/optimization_barrier | solution.py:119
  14.6 5.0 %product.5 = (bf16[2,2,2,80,512]{4,3,2,1,0:T(8,128)(2,1)}, bf16[2,2,80,512]{3,2,1,0:T(8,128)(2,1)}, bf16[2,2,80,512]{3,2,1,0:T(8,128)(2,1)}) custom-call(s32[4]{0:T(128)S(1)} %get-tuple-element.139.order, bf16[1024,1280]{1,0:T(8,128)(2,1)} %copy-done.2, bf16[1024,512]{1,0:T(8,128)(2,1)} %bitcast.123), custom_call_target="tpu_custom_call" | custom-call | tf_op jit(solution)/shard_map/first_half/product/pallas_call | solution.py:85
  23.7 6.5 %collective-permute-done.2 = bf16[2,2,2,16,320]{4,3,2,1,0:T(8,128)(2,1)S(1)} collective-permute-done((bf16[2,2,2,16,320]{4,3,2,1,0:T(8,128)(2,1)S(1)}, bf16[2,2,2,16,320]{4,3,2,1,0:T(8,128)(2,1)S(1)}, u32[]{:S(2)}, u32[]{:S(2)}) %collective-permute-start.2) | collective-permute-done | bytes 81952 | tf_op jit(solution)/shard_map/hidden/ppermute | solution.py:351
  30.3 2.0 %collective-permute-start.3 = (bf16[2,2,2,16,320]{4,3,2,1,0:T(8,128)(2,1)S(1)}, bf16[2,2,2,16,320]{4,3,2,1,0:T(8,128)(2,1)S(1)}, u32[]{:S(2)}, u32[]{:S(2)}) collective-permute-start(bf16[2,2,2,16,320]{4,3,2,1,0:T(8,128)(2,1)S(1)} %get-tuple-element.132), channel_id=1, source_target_pairs={{0,32},{32,0},{64,96},{96,64},{128,160},{160,128},{192,224},{224,1... | collective-permute-start | bytes 245768 | tf_op jit(solution)/shard_map/hidden/ppermute | solution.py:351
  32.3 1.3 pad_maximum_fusion
  33.7 1.4 collective-permute-done.3
  36.2 3.9 %collective-permute-done.5 = bf16[2,2,2,80,512]{4,3,1,2,0:T(8,128)(2,1)S(1)} collective-permute-done((bf16[2,2,2,80,512]{4,3,1,2,0:T(8,128)(2,1)S(1)}, bf16[2,2,2,80,512]{4,3,1,2,0:T(8,128)(2,1)S(1)}, u32[]{:S(2)}, u32[]{:S(2)}) %collective-permute-start.5) | collective-permute-done | bytes 655392 | tf_op jit(solution)/shard_map/first_half/ppermute | solution.py:115
  41.3 2.4 %copy.91 = bf16[128,8,2,256]{3,1,2,0:T(8,128)(2,1)} copy(bf16[128,8,2,256]{3,2,1,0:T(2,128)(2,1)} %bitcast.70) | data formatting | bytes 2097152
  43.7 5.0 %product.6 = (bf16[2,2,2,80,512]{4,3,2,1,0:T(8,128)(2,1)}, bf16[2,2,80,512]{3,2,1,0:T(8,128)(2,1)}, bf16[2,2,80,512]{3,2,1,0:T(8,128)(2,1)}) custom-call(s32[4]{0:T(128)S(1)} %get-tuple-element.138.order, bf16[1024,1280]{1,0:T(8,128)(2,1)} %left_ref.3, bf16[1024,512]{1,0:T(8,128)(2,1)} %bitcast.124), custom_call_target="tpu_custom_call" | custom-call | tf_op jit(solution)/shard_map/second_half/product/pallas_call | solution.py:85
  48.7 2.0 %collective-permute-start.6 = (bf16[2,2,2,80,512]{4,3,2,1,0:T(8,128)(2,1)}, bf16[2,2,2,80,512]{4,3,2,1,0:T(8,128)(2,1)S(1)}, u32[]{:S(2)}, u32[]{:S(2)}) collective-permute-start(bf16[2,2,2,80,512]{4,3,2,1,0:T(8,128)(2,1)} %get-tuple-element.83), channel_id=1, source_target_pairs={{0,4},{4,0},{8,12},{12,8},{1,5},{5,1},{9,13},{13,9},{2,6},{6,2},{1... | collective-permute-start | bytes 1966088 | tf_op jit(solution)/shard_map/second_half/ppermute | solution.py:115
  50.7 5.0 %product.7 = (bf16[2,2,2,80,512]{4,3,2,1,0:T(8,128)(2,1)}, bf16[2,2,80,512]{3,2,1,0:T(8,128)(2,1)}, bf16[2,2,80,512]{3,2,1,0:T(8,128)(2,1)}) custom-call(s32[4]{0:T(128)S(1)} %get-tuple-element.139.order, bf16[1024,1280]{1,0:T(8,128)(2,1)} %copy-done.2, bf16[1024,512]{1,0:T(8,128)(2,1)} %bitcast.125), custom_call_target="tpu_custom_call" | custom-call | tf_op jit(solution)/shard_map/second_half/product/pallas_call | solution.py:85
  56.4 3.3 %collective-permute-start.9 = (bf16[2,2,2,16,320]{4,3,2,1,0:T(8,128)(2,1)S(1)}, bf16[2,2,2,16,320]{4,3,2,1,0:T(8,128)(2,1)S(1)}, u32[]{:S(2)}, u32[]{:S(2)}) collective-permute-start(bf16[2,2,2,16,320]{4,3,2,1,0:T(8,128)(2,1)S(1)} %get-tuple-element.130), channel_id=1, source_target_pairs={{0,64},{32,96},{64,0},{96,32},{128,192},{160,224},{192,128},{224,1... | collective-permute-start | bytes 245768 | tf_op jit(solution)/shard_map/hidden/ppermute | solution.py:351
  59.7 2.2 %collective-permute-start.11 = (bf16[2,2,2,80,512]{4,3,2,1,0:T(8,128)(2,1)}, bf16[2,2,2,80,512]{4,3,2,1,0:T(8,128)(2,1)S(1)}, u32[]{:S(2)}, u32[]{:S(2)}) collective-permute-start(bf16[2,2,2,80,512]{4,3,2,1,0:T(8,128)(2,1)} %get-tuple-element.93), channel_id=1, source_target_pairs={{0,12},{12,0},{4,8},{8,4},{1,13},{13,1},{5,9},{9,5},{2,14},{14,2},... | collective-permute-start | bytes 1966088 | tf_op jit(solution)/shard_map/second_half/ppermute | solution.py:115
  64.2 6.2 %collective-permute-start.10 = (bf16[2,2,2,16,320]{4,3,2,1,0:T(8,128)(2,1)S(1)}, bf16[2,2,2,16,320]{4,3,2,1,0:T(8,128)(2,1)S(1)}, u32[]{:S(2)}, u32[]{:S(2)}) collective-permute-start(bf16[2,2,2,16,320]{4,3,2,1,0:T(8,128)(2,1)S(1)} %get-tuple-element.128), channel_id=1, source_target_pairs={{0,128},{32,160},{64,192},{96,224},{128,0},{160,32},{192,64},{224,... | collective-permute-start | bytes 245768 | tf_op jit(solution)/shard_map/hidden/ppermute | solution.py:351
  71.1 1.4 collective-permute-start.12
  72.5 1.5 collective-permute-done.10
  78.5 2.3 %collective-permute-start.13 = (bf16[2,2,80,512]{3,2,1,0:T(8,128)(2,1)S(1)}, bf16[2,2,80,512]{3,2,1,0:T(8,128)(2,1)S(1)}, u32[]{:S(2)}, u32[]{:S(2)}) collective-permute-start(bf16[2,2,80,512]{3,2,1,0:T(8,128)(2,1)S(1)} %fusion.11), channel_id=1, source_target_pairs={{0,12},{12,0},{4,8},{8,4},{1,13},{13,1},{5,9},{9,5},{2,14},{14,2},... | collective-permute-start | bytes 983048 | tf_op jit(solution)/shard_map/second_half/ppermute | solution.py:115
  82.0 4.8 %collective-permute-done.13 = bf16[2,2,80,512]{3,2,1,0:T(8,128)(2,1)S(1)} collective-permute-done((bf16[2,2,80,512]{3,2,1,0:T(8,128)(2,1)S(1)}, bf16[2,2,80,512]{3,2,1,0:T(8,128)(2,1)S(1)}, u32[]{:S(2)}, u32[]{:S(2)}) %collective-permute-start.13) | collective-permute-done | bytes 327712 | tf_op jit(solution)/shard_map/second_half/ppermute | solution.py:115
  90.2 1.5 collective-permute-start.15
  91.7 5.6 %collective-permute-done.15 = bf16[2,2,80,512]{3,2,1,0:T(8,128)(2,1)S(1)} collective-permute-done((bf16[2,2,80,512]{3,2,1,0:T(8,128)(2,1)S(1)}, bf16[2,2,80,512]{3,2,1,0:T(8,128)(2,1)S(1)}, u32[]{:S(2)}, u32[]{:S(2)}) %collective-permute-start.15) | collective-permute-done | bytes 327712 | tf_op jit(solution)/shard_map/second_half/ppermute | solution.py:46
  97.6 19.5 %all_to_all.22.parts_ref = bf16[8,80,512]{2,1,0:T(8,128)(2,1)S(1)} all-to-all(bf16[8,80,512]{2,1,0:T(8,128)(2,1)S(1)} %maximum_select_fusion), channel_id=1, replica_groups=mesh['z'=8,'xl'=2,'y'=4,'xh'=2,'core'=2] {'z'}, dimensions={0} | all-to-all | bytes 1310720 | tf_op jit(solution)/shard_map/reduce_z/all_to_all | solution.py:419
  118.7 13.2 %all-to-all-start.1 = ((f32[256,1,128]{2,1,0:T(1,128)}), f32[256,1,128]{2,1,0:T(1,128)S(1)}, u32[]{:S(2)}, u32[]{:S(2)}) async-start(f32[256,1,128]{2,1,0:T(1,128)} %bitcast.46), calls=%async_computation.1 | async-start | bytes 262144 | tf_op jit(solution)/shard_map/squares/all_to_all | solution.py:422
  132.0 11.4 %all-to-all-done.1 = f32[256,1,128]{2,1,0:T(1,128)S(1)} async-done(((f32[256,1,128]{2,1,0:T(1,128)}), f32[256,1,128]{2,1,0:T(1,128)S(1)}, u32[]{:S(2)}, u32[]{:S(2)}) %all-to-all-start.1) | async-done | bytes 131104 | tf_op jit(solution)/shard_map/squares/all_to_all | solution.py:422
  144.6 2.7 %collective-permute-start.18 = (bf16[80,512]{1,0:T(8,128)(2,1)S(1)}, bf16[80,512]{1,0:T(8,128)(2,1)S(1)}, u32[]{:S(2)}, u32[]{:S(2)}) collective-permute-start(bf16[80,512]{1,0:T(8,128)(2,1)S(1)} %get-tuple-element.113.refs_0_), channel_id=1, source_target_pairs={{0,8},{4,12},{8,0},{12,4},{1,9},{5,13},{9,1},{13,5},{2,10},{6,14},... | collective-permute-start | bytes 245768 | tf_op jit(solution)/shard_map/project/ppermute | solution.py:333
  148.8 2.7 %collective-permute-done.18.refs_2_ = bf16[80,512]{1,0:T(8,128)(2,1)S(1)} collective-permute-done((bf16[80,512]{1,0:T(8,128)(2,1)S(1)}, bf16[80,512]{1,0:T(8,128)(2,1)S(1)}, u32[]{:S(2)}, u32[]{:S(2)}) %collective-permute-start.18) | collective-permute-done | bytes 81952 | tf_op jit(solution)/shard_map/project/ppermute | solution.py:333
  151.5 1.7 collective-permute-done.19.refs_3_
  154.2 3.5 %all-to-all-start.2 = ((bf16[16,16,512]{2,1,0:T(8,128)(2,1)}), bf16[16,16,512]{2,1,0:T(8,128)(2,1)S(1)}, u32[]{:S(2)}, u32[]{:S(2)}) async-start(bf16[16,16,512]{2,1,0:T(8,128)(2,1)} %bitcast.48), calls=%async_computation.2 | async-start | bytes 524288 | tf_op jit(solution)/shard_map/project/all_to_all | solution.py:436
  159.6 8.4 %old_attention.1 = (f32[2,4,32,128]{3,2,1,0:T(8,128)S(1)}, f32[2,4,32,128]{3,2,1,0:T(8,128)S(1)}, f32[2,4,32,128]{3,2,1,0:T(8,128)S(1)}) custom-call(s32[4]{0:T(128)S(1)} %copy-done, bf16[2,4,32,128]{3,2,1,0:T(8,128)(2,1)S(1)} %bitcast.115, bf16[4,2048,256]{2,1,0:T(8,128)(2,1)} %key_ref.1, bf16[4,2048,256]{2,1,0:T(8,128)(2,1)} %value_ref.1), custom_call_target="tpu_custom_call" | custom-call | tf_op jit(solution)/shard_map/old/old_attention/pallas_call | solution.py:143
  168.1 1.8 %all-to-all-done.2.part_ref = bf16[16,16,512]{2,1,0:T(8,128)(2,1)S(1)} async-done(((bf16[16,16,512]{2,1,0:T(8,128)(2,1)}), bf16[16,16,512]{2,1,0:T(8,128)(2,1)S(1)}, u32[]{:S(2)}, u32[]{:S(2)}) %all-to-all-start.2) | async-done | bytes 262176 | tf_op jit(solution)/shard_map/project/all_to_all | solution.py:436
  (92 shorter events, 30.9 us)
Async XLA Ops:
  0.6 10.7 %collective-permute-start = (bf16[1024,1280]{1,0:T(8,128)(2,1)}, bf16[1024,1280]{1,0:T(8,128)(2,1)S(1)}, u32[]{:S(2)}, u32[]{:S(2)}) collective-permute-start(bf16[1024,1280]{1,0:T(8,128)(2,1)} %left_ref.3), channel_id=1, source_target_pairs={{0,1},{1,0},{2,3},{3,2},{4,5},{5,4},{6,7},{7,6},{8,9},{9,8},{10,11... | collective-permute-start | bytes 7864328 | tf_op jit(solution)/shard_map/exchange/ppermute | solution.py:46
  0.7 34.4 %collective-permute-start.4 = (bf16[1024,2,256]{2,1,0:T(2,128)(2,1)}, bf16[1024,2,256]{2,1,0:T(2,128)(2,1)}, u32[]{:S(2)}, u32[]{:S(2)}) collective-permute-start(bf16[1024,2,256]{2,1,0:T(2,128)(2,1)} %param.12), channel_id=1, source_target_pairs={{0,2},{2,0},{1,3},{3,1},{4,6},{6,4},{5,7},{7,5},{8,10},{10,8},{9,1... | collective-permute-start | bytes 3145736 | tf_op jit(solution)/shard_map/exchange/ppermute | solution.py:46
  6.4 13.1 %copy-start.8 = (bf16[4,4,5120]{2,1,0:T(4,128)(2,1)S(1)}, bf16[4,4,5120]{2,1,0:T(4,128)(2,1)}, u32[]{:S(2)}) copy-start(bf16[4,4,5120]{2,1,0:T(4,128)(2,1)} %param.16) | copy-start | bytes 491524
  11.3 3.2 %copy-start.2 = (bf16[1024,1280]{1,0:T(8,128)(2,1)}, bf16[1024,1280]{1,0:T(8,128)(2,1)S(1)}, u32[]{:S(2)}) copy-start(bf16[1024,1280]{1,0:T(8,128)(2,1)S(1)} %collective-permute-done.left_ref) | copy-start | bytes 7864324
  13.8 21.3 %collective-permute-start.1 = (bf16[2,2,2,80,512]{4,3,1,2,0:T(8,128)(2,1)}, bf16[2,2,2,80,512]{4,3,1,2,0:T(8,128)(2,1)}, u32[]{:S(2)}, u32[]{:S(2)}) collective-permute-start(bf16[2,2,2,80,512]{4,3,1,2,0:T(8,128)(2,1)} %copy.67), channel_id=1, source_target_pairs={{0,4},{4,0},{8,12},{12,8},{1,5},{5,1},{9,13},{13,9},{2,6},{6,2},{1... | collective-permute-start | bytes 1966088 | tf_op jit(solution)/shard_map/first_half/ppermute | solution.py:115
  14.6 20.6 %copy-start.6 = (bf16[2,2,80,512]{3,2,1,0:T(8,128)(2,1)S(1)}, bf16[2,2,80,512]{3,2,1,0:T(8,128)(2,1)}, u32[]{:S(2)}) copy-start(bf16[2,2,80,512]{3,2,1,0:T(8,128)(2,1)} %get-tuple-element.64) | copy-start | bytes 983044
  19.5 20.5 %copy-start.7 = (bf16[2,2,80,512]{3,2,1,0:T(8,128)(2,1)S(1)}, bf16[2,2,80,512]{3,2,1,0:T(8,128)(2,1)}, u32[]{:S(2)}) copy-start(bf16[2,2,80,512]{3,2,1,0:T(8,128)(2,1)} %get-tuple-element.77) | copy-start | bytes 983044
  19.8 10.4 %collective-permute-start.2 = (bf16[2,2,2,16,320]{4,3,2,1,0:T(8,128)(2,1)S(1)}, bf16[2,2,2,16,320]{4,3,2,1,0:T(8,128)(2,1)S(1)}, u32[]{:S(2)}, u32[]{:S(2)}) collective-permute-start(bf16[2,2,2,16,320]{4,3,2,1,0:T(8,128)(2,1)S(1)} %get-tuple-element.134), channel_id=1, source_target_pairs={{0,16},{16,0},{1,17},{17,1},{2,18},{18,2},{3,19},{19,3},{4,20},{20... | collective-permute-start | bytes 245768 | tf_op jit(solution)/shard_map/hidden/ppermute | solution.py:351
  22.5 17.5 %collective-permute-start.5 = (bf16[2,2,2,80,512]{4,3,1,2,0:T(8,128)(2,1)S(1)}, bf16[2,2,2,80,512]{4,3,1,2,0:T(8,128)(2,1)S(1)}, u32[]{:S(2)}, u32[]{:S(2)}) collective-permute-start(bf16[2,2,2,80,512]{4,3,1,2,0:T(8,128)(2,1)S(1)} %copy.73), channel_id=1, source_target_pairs={{0,12},{12,0},{4,8},{8,4},{1,13},{13,1},{5,9},{9,5},{2,14},{14,2},... | collective-permute-start | bytes 1966088 | tf_op jit(solution)/shard_map/first_half/ppermute | solution.py:115
  30.3 4.7 %collective-permute-start.3 = (bf16[2,2,2,16,320]{4,3,2,1,0:T(8,128)(2,1)S(1)}, bf16[2,2,2,16,320]{4,3,2,1,0:T(8,128)(2,1)S(1)}, u32[]{:S(2)}, u32[]{:S(2)}) collective-permute-start(bf16[2,2,2,16,320]{4,3,2,1,0:T(8,128)(2,1)S(1)} %get-tuple-element.132), channel_id=1, source_target_pairs={{0,32},{32,0},{64,96},{96,64},{128,160},{160,128},{192,224},{224,1... | collective-permute-start | bytes 245768 | tf_op jit(solution)/shard_map/hidden/ppermute | solution.py:351
  40.1 15.5 %collective-permute-start.7 = (bf16[2,2,80,512]{3,2,0,1:T(8,128)(2,1)S(1)}, bf16[2,2,80,512]{3,2,0,1:T(8,128)(2,1)S(1)}, u32[]{:S(2)}, u32[]{:S(2)}) collective-permute-start(bf16[2,2,80,512]{3,2,0,1:T(8,128)(2,1)S(1)} %fusion.13), channel_id=1, source_target_pairs={{0,12},{12,0},{4,8},{8,4},{1,13},{13,1},{5,9},{9,5},{2,14},{14,2},... | collective-permute-start | bytes 983048 | tf_op jit(solution)/shard_map/first_half/ppermute | solution.py:115
  41.3 14.4 %collective-permute-start.8 = (bf16[2,2,80,512]{3,2,0,1:T(8,128)(2,1)S(1)}, bf16[2,2,80,512]{3,2,0,1:T(8,128)(2,1)S(1)}, u32[]{:S(2)}, u32[]{:S(2)}) collective-permute-start(bf16[2,2,80,512]{3,2,0,1:T(8,128)(2,1)S(1)} %fusion.12), channel_id=1, source_target_pairs={{0,4},{4,0},{8,12},{12,8},{1,5},{5,1},{9,13},{13,9},{2,6},{6,2},{1... | collective-permute-start | bytes 983048 | tf_op jit(solution)/shard_map/first_half/ppermute | solution.py:115
  43.7 18.1 %copy-start.3 = (bf16[2,2,80,512]{3,2,1,0:T(8,128)(2,1)S(1)}, bf16[2,2,80,512]{3,2,1,0:T(8,128)(2,1)}, u32[]{:S(2)}) copy-start(bf16[2,2,80,512]{3,2,1,0:T(8,128)(2,1)} %get-tuple-element.94) | copy-start | bytes 983044
  43.7 19.2 %copy-start.4 = (bf16[2,2,80,512]{3,2,1,0:T(8,128)(2,1)S(1)}, bf16[2,2,80,512]{3,2,1,0:T(8,128)(2,1)}, u32[]{:S(2)}) copy-start(bf16[2,2,80,512]{3,2,1,0:T(8,128)(2,1)} %get-tuple-element.96) | copy-start | bytes 983044
  48.7 26.4 %collective-permute-start.6 = (bf16[2,2,2,80,512]{4,3,2,1,0:T(8,128)(2,1)}, bf16[2,2,2,80,512]{4,3,2,1,0:T(8,128)(2,1)S(1)}, u32[]{:S(2)}, u32[]{:S(2)}) collective-permute-start(bf16[2,2,2,80,512]{4,3,2,1,0:T(8,128)(2,1)} %get-tuple-element.83), channel_id=1, source_target_pairs={{0,4},{4,0},{8,12},{12,8},{1,5},{5,1},{9,13},{13,9},{2,6},{6,2},{1... | collective-permute-start | bytes 1966088 | tf_op jit(solution)/shard_map/second_half/ppermute | solution.py:115
  55.7 0.7 copy-start.5
  56.4 7.7 %collective-permute-start.9 = (bf16[2,2,2,16,320]{4,3,2,1,0:T(8,128)(2,1)S(1)}, bf16[2,2,2,16,320]{4,3,2,1,0:T(8,128)(2,1)S(1)}, u32[]{:S(2)}, u32[]{:S(2)}) collective-permute-start(bf16[2,2,2,16,320]{4,3,2,1,0:T(8,128)(2,1)S(1)} %get-tuple-element.130), channel_id=1, source_target_pairs={{0,64},{32,96},{64,0},{96,32},{128,192},{160,224},{192,128},{224,1... | collective-permute-start | bytes 245768 | tf_op jit(solution)/shard_map/hidden/ppermute | solution.py:351
  59.7 16.5 %collective-permute-start.11 = (bf16[2,2,2,80,512]{4,3,2,1,0:T(8,128)(2,1)}, bf16[2,2,2,80,512]{4,3,2,1,0:T(8,128)(2,1)S(1)}, u32[]{:S(2)}, u32[]{:S(2)}) collective-permute-start(bf16[2,2,2,80,512]{4,3,2,1,0:T(8,128)(2,1)} %get-tuple-element.93), channel_id=1, source_target_pairs={{0,12},{12,0},{4,8},{8,4},{1,13},{13,1},{5,9},{9,5},{2,14},{14,2},... | collective-permute-start | bytes 1966088 | tf_op jit(solution)/shard_map/second_half/ppermute | solution.py:115
  64.2 9.8 %collective-permute-start.10 = (bf16[2,2,2,16,320]{4,3,2,1,0:T(8,128)(2,1)S(1)}, bf16[2,2,2,16,320]{4,3,2,1,0:T(8,128)(2,1)S(1)}, u32[]{:S(2)}, u32[]{:S(2)}) collective-permute-start(bf16[2,2,2,16,320]{4,3,2,1,0:T(8,128)(2,1)S(1)} %get-tuple-element.128), channel_id=1, source_target_pairs={{0,128},{32,160},{64,192},{96,224},{128,0},{160,32},{192,64},{224,... | collective-permute-start | bytes 245768 | tf_op jit(solution)/shard_map/hidden/ppermute | solution.py:351
  71.1 7.4 %collective-permute-start.12 = (bf16[2,2,80,512]{3,2,1,0:T(8,128)(2,1)}, bf16[2,2,80,512]{3,2,1,0:T(8,128)(2,1)}, u32[]{:S(2)}, u32[]{:S(2)}) collective-permute-start(bf16[2,2,80,512]{3,2,1,0:T(8,128)(2,1)} %fusion.25), channel_id=1, source_target_pairs={{0,16},{16,0},{1,17},{17,1},{2,18},{18,2},{3,19},{19,3},{4,20},{20... | collective-permute-start | bytes 983048 | tf_op jit(solution)/shard_map/first_half/ppermute | solution.py:46
  78.5 8.3 %collective-permute-start.13 = (bf16[2,2,80,512]{3,2,1,0:T(8,128)(2,1)S(1)}, bf16[2,2,80,512]{3,2,1,0:T(8,128)(2,1)S(1)}, u32[]{:S(2)}, u32[]{:S(2)}) collective-permute-start(bf16[2,2,80,512]{3,2,1,0:T(8,128)(2,1)S(1)} %fusion.11), channel_id=1, source_target_pairs={{0,12},{12,0},{4,8},{8,4},{1,13},{13,1},{5,9},{9,5},{2,14},{14,2},... | collective-permute-start | bytes 983048 | tf_op jit(solution)/shard_map/second_half/ppermute | solution.py:115
  81.8 7.2 %collective-permute-start.14 = (bf16[2,2,80,512]{3,2,1,0:T(8,128)(2,1)S(1)}, bf16[2,2,80,512]{3,2,1,0:T(8,128)(2,1)S(1)}, u32[]{:S(2)}, u32[]{:S(2)}) collective-permute-start(bf16[2,2,80,512]{3,2,1,0:T(8,128)(2,1)S(1)} %fusion.10), channel_id=1, source_target_pairs={{0,4},{4,0},{8,12},{12,8},{1,5},{5,1},{9,13},{13,9},{2,6},{6,2},{1... | collective-permute-start | bytes 983048 | tf_op jit(solution)/shard_map/second_half/ppermute | solution.py:115
  90.1 67.6 %copy-start = (s32[4]{0:T(128)S(1)}, s32[4]{0:T(128)}, u32[]{:S(2)}) copy-start(s32[4]{0:T(128)} %length_ref.1) | copy-start | bytes 52
  90.2 7.2 %collective-permute-start.15 = (bf16[2,2,80,512]{3,2,1,0:T(8,128)(2,1)S(1)}, bf16[2,2,80,512]{3,2,1,0:T(8,128)(2,1)S(1)}, u32[]{:S(2)}, u32[]{:S(2)}) collective-permute-start(bf16[2,2,80,512]{3,2,1,0:T(8,128)(2,1)S(1)} %fusion.19), channel_id=1, source_target_pairs={{0,16},{16,0},{1,17},{17,1},{2,18},{18,2},{3,19},{19,3},{4,20},{20... | collective-permute-start | bytes 983048 | tf_op jit(solution)/shard_map/second_half/ppermute | solution.py:46
  118.0 13.9 %collective-permute-start.16 = (f32[80,512]{1,0:T(8,128)S(1)}, f32[80,512]{1,0:T(8,128)S(1)}, u32[]{:S(2)}, u32[]{:S(2)}) collective-permute-start(f32[80,512]{1,0:T(8,128)S(1)} %get-tuple-element.105), channel_id=1, source_target_pairs={{2,128},{34,160},{66,192},{98,224},{128,2},{160,34},{192,66},{224,... | collective-permute-start | bytes 491528 | tf_op jit(solution)/shard_map/place/ppermute | solution.py:425
  118.7 24.7 %all-to-all-start.1 = ((f32[256,1,128]{2,1,0:T(1,128)}), f32[256,1,128]{2,1,0:T(1,128)S(1)}, u32[]{:S(2)}, u32[]{:S(2)}) async-start(f32[256,1,128]{2,1,0:T(1,128)} %bitcast.46), calls=%async_computation.1 | async-start | bytes 262144 | tf_op jit(solution)/shard_map/squares/all_to_all | solution.py:422
  143.7 5.1 %collective-permute-start.17 = (bf16[80,512]{1,0:T(8,128)(2,1)S(1)}, bf16[80,512]{1,0:T(8,128)(2,1)S(1)}, u32[]{:S(2)}, u32[]{:S(2)}) collective-permute-start(bf16[80,512]{1,0:T(8,128)(2,1)S(1)} %get-tuple-element.113.refs_0_), channel_id=1, source_target_pairs={{0,4},{4,0},{8,12},{12,8},{1,5},{5,1},{9,13},{13,9},{2,6},{6,2},{1... | collective-permute-start | bytes 245768 | tf_op jit(solution)/shard_map/project/ppermute | solution.py:333
  144.6 6.9 %collective-permute-start.18 = (bf16[80,512]{1,0:T(8,128)(2,1)S(1)}, bf16[80,512]{1,0:T(8,128)(2,1)S(1)}, u32[]{:S(2)}, u32[]{:S(2)}) collective-permute-start(bf16[80,512]{1,0:T(8,128)(2,1)S(1)} %get-tuple-element.113.refs_0_), channel_id=1, source_target_pairs={{0,8},{4,12},{8,0},{12,4},{1,9},{5,13},{9,1},{13,5},{2,10},{6,14},... | collective-permute-start | bytes 245768 | tf_op jit(solution)/shard_map/project/ppermute | solution.py:333
  147.3 5.9 %collective-permute-start.19 = (bf16[80,512]{1,0:T(8,128)(2,1)S(1)}, bf16[80,512]{1,0:T(8,128)(2,1)S(1)}, u32[]{:S(2)}, u32[]{:S(2)}) collective-permute-start(bf16[80,512]{1,0:T(8,128)(2,1)S(1)} %get-tuple-element.113.refs_0_), channel_id=1, source_target_pairs={{0,12},{4,8},{8,4},{12,0},{1,13},{5,9},{9,5},{13,1},{2,14},{6,10},... | collective-permute-start | bytes 245768 | tf_op jit(solution)/shard_map/project/ppermute | solution.py:333
  154.2 15.7 %all-to-all-start.2 = ((bf16[16,16,512]{2,1,0:T(8,128)(2,1)}), bf16[16,16,512]{2,1,0:T(8,128)(2,1)S(1)}, u32[]{:S(2)}, u32[]{:S(2)}) async-start(bf16[16,16,512]{2,1,0:T(8,128)(2,1)} %bitcast.48), calls=%async_computation.2 | async-start | bytes 524288 | tf_op jit(solution)/shard_map/project/all_to_all | solution.py:436
  159.6 10.2 %copy-start.1 = (f32[128]{0:T(128)S(1)}, f32[128]{0:T(128)}, u32[]{:S(2)}) copy-start(f32[128]{0:T(128)} %param.21) | copy-start | bytes 1540

commit v3 on v2

--- a/solution.py
+++ b/solution.py
@@ -67,11 +67,11 @@
             at = pl.multiple_of((x * 4 + order[slot]) * rows, rows)
             block = total_ref[pl.ds(at, rows), :].astype(BF16)
             if slot < 2:
-                away_ref[slot, 0, x] = block
+                away_ref[slot, x, 0] = block
             elif slot == 2:
-                near_ref[0, x] = block
+                near_ref[x, 0] = block
             else:
-                mine_ref[0, x] = block
+                mine_ref[x, 0] = block
 
 
 def product(left, right, pairing, rows):
@@ -81,7 +81,7 @@
     near = partner(me, 1 - pairing)
     order = jnp.stack([partner(far, 1 - pairing), far, near, me]).astype(jnp.int32)
     part = pltpu.HBM((2, 2, rows, columns), BF16)
-    part_spec = pl.BlockSpec((1, 2, rows, columns), lambda k, order: (k, 0, 0, 0))
+    part_spec = pl.BlockSpec((2, 1, rows, columns), lambda k, order: (0, k, 0, 0))
     return pl.pallas_call(
         product_kernel,
         out_shape=(pltpu.HBM((2, 2, 2, rows, columns), BF16), part, part),
@@ -93,7 +93,7 @@
                 pl.BlockSpec((tokens, columns), lambda k, order: (0, 0)),
             ],
             out_specs=[
-                pl.BlockSpec((2, 1, 2, rows, columns), lambda k, order: (0, k, 0, 0, 0)),
+                pl.BlockSpec((2, 2, 1, rows, columns), lambda k, order: (0, 0, k, 0, 0)),
                 part_spec,
                 part_spec,
             ],
@@ -185,9 +185,12 @@
         normed = raw * lax.rsqrt(mean + norm_eps) * gain_ref[...]
         turned = normed * cosine_ref[...] + pltpu.roll(normed, HD // 2, 1) * sine_ref[...]
         keys = turned.astype(BF16)
-        values = projected[:, heads * HD + head * HD : heads * HD + (head + 1) * HD].astype(BF16)
-        keys_ref[:, at] = keys
-        values_ref[:, at] = values
+        raw_values = projected[:, heads * HD + head * HD : heads * HD + (head + 1) * HD]
+        values = raw_values.astype(BF16)
+        for row in range(states // steps):
+            own = slice(row * steps, (row + 1) * steps)
+            keys_ref[row, :, at] = turned[own].astype(BF16)
+            values_ref[row, :, at] = raw_values[own].astype(BF16)
         scores = lax.dot_general(
             query_ref[head], keys, (((1,), (1,)), ((), ())), preferred_element_type=F32
         ) * (1.0 / math.sqrt(HD))
@@ -207,7 +210,8 @@
                 mixed_ref[row * steps : (row + 1) * steps, column : column + HD] = mixed[
                     source : source + steps
                 ]
-    attended_ref[...] = mixed_ref[...].astype(BF16)
+    for row in range(states // steps):
+        attended_ref[row] = mixed_ref[row * steps : (row + 1) * steps].astype(BF16)
 
 
 def fresh_attention(parts, query_heads, old_sum, old_top, old_total, key_gain, cosine, sine, steps):
@@ -216,9 +220,9 @@
     return pl.pallas_call(
         functools.partial(fresh_kernel, steps=steps),
         out_shape=(
-            jax.ShapeDtypeStruct((states, heads * HD), BF16),
-            jax.ShapeDtypeStruct((states, heads * HD), BF16),
-            jax.ShapeDtypeStruct((states, heads * queries // states * HD), BF16),
+            jax.ShapeDtypeStruct((states // steps, steps, heads * HD), BF16),
+            jax.ShapeDtypeStruct((states // steps, steps, heads * HD), BF16),
+            jax.ShapeDtypeStruct((states // steps, steps, heads * queries // states * HD), BF16),
         ),
         scratch_shapes=[pltpu.VMEM((states, heads * queries // states * HD), F32)],
         compiler_params=pltpu.CompilerParams(vmem_limit_bytes=24 * 1024 * 1024),
@@ -321,10 +325,12 @@
     groups = QH // KVH
 
     def by_xl(first, second):
-        block = jnp.stack([first, second])
-        kept = lax.dynamic_index_in_dim(block, xl, axis=2, keepdims=False)
-        sent = lax.dynamic_index_in_dim(block, 1 - xl, axis=2, keepdims=False)
-        return kept, sent
+        def slots(at):
+            return jnp.stack(
+                [lax.dynamic_index_in_dim(block, at, keepdims=False) for block in (first, second)]
+            )
+
+        return slots(xl), slots(1 - xl)
 
     def in_order(block):
         return jnp.where(core == 0, block, block[::-1]).reshape(4, own_rows, columns)
@@ -359,46 +365,38 @@
     with jax.named_scope("hidden"):
         hidden = rollout_hidden.reshape(states, 16, 4 * own_rows).transpose(1, 0, 2)
         hidden = hidden.reshape(2, 2, 2, 2, states, 4 * own_rows)
-        hidden = trade(hidden, 3, None, [(0, 1), (1, 0)])
-        hidden = trade_z(hidden, 0)
+        hidden = trade_z(trade_z(hidden, 0), 1)
+        hidden, upstream_other = together(hidden, upstream_other)
+        hidden = trade_z(hidden, 2)
     with jax.named_scope("state"):
         query_heads = queries.reshape(row_count, step_count, head_count, groups, HD)
         query_heads = query_heads.transpose(2, 0, 3, 1, 4)
         query_heads = query_heads.reshape(head_count, row_count, groups * step_count, HD)
         state = jnp.concatenate([weight, moment_one, moment_two]).reshape(3 * own_rows, columns)
     with jax.named_scope("first_half"):
-        one_got, two_near, hidden, query_heads, state, upstream_other = together(
-            one_got, two_near, hidden, query_heads, state, upstream_other
+        upstream_other = upstream_other.reshape(token_count, columns)
+        one_got, two_got, hidden, query_heads, state, upstream_other = together(
+            one_got, two_got, hidden, query_heads, state, upstream_other
         )
         one_passed = add(one_near, one_got[0])
+        one_passed, upstream_other = together(one_passed, upstream_other)
+        one_last = along_y(one_passed, 1)
+    with jax.named_scope("second_half"):
+        away, three_near, three_mine = product(tokens, upstream_other, 0, own_rows)
+        away, tokens_other, two_near = together(away, tokens_other, two_near)
+        three_got = along_y(away, 0)
+    with jax.named_scope("first_half"):
         two_passed = add(two_near, two_got[0])
-        one_passed, two_passed, upstream_other = together(one_passed, two_passed, upstream_other)
-        one_last = along_y(one_passed, 1)
+        two_passed, tokens_other = together(two_passed, tokens_other)
         two_last = along_y(two_passed, 0)
     with jax.named_scope("second_half"):
-        upstream_other = upstream_other.reshape(token_count, columns)
-        away, three_near, three_mine = product(tokens, upstream_other, 0, own_rows)
-        away, tokens_other = together(away, tokens_other)
-        three_got = along_y(away, 0)
         away, four_near, four_mine = product(tokens_other, upstream_other, 1, own_rows)
-        away, one_last, two_last, hidden = together(away, one_last, two_last, hidden)
+        away, one_last, two_last = together(away, one_last, two_last)
         four_got = along_y(away, 1)
     with jax.named_scope("first_half"):
         kept, sent = by_xl(add(one_mine, one_got[1], one_last), add(two_mine, two_got[1], two_last))
         arrived = swap(sent, "xl")
-    with jax.named_scope("hidden"):
-        hidden = trade_z(trade_z(hidden, 1), 2)
-        y = lax.axis_index("y")
-        hidden = hidden.reshape(16 * states, 4, own_rows)
-        hidden = jnp.concatenate(
-            [
-                lax.dynamic_index_in_dim(hidden, y ^ step, axis=1, keepdims=False)
-                for step in range(4)
-            ],
-            axis=1,
-        )
     with jax.named_scope("second_half"):
-        three_got, four_near, hidden = together(three_got, four_near, hidden)
         three_passed = add(three_near, three_got[0])
         four_passed = add(four_near, four_got[0])
         three_passed, four_passed, arrived = together(three_passed, four_passed, arrived)
@@ -418,13 +416,25 @@
         )
         parts = lax.all_to_all(parts, "z", 0, 0)
         gradient, squares = sum_gradient(parts, total_tokens, 256)
+        gradient, squares, hidden = together(gradient, squares, hidden)
+    with jax.named_scope("hidden"):
+        hidden = trade(hidden, 3, None, [(0, 1), (1, 0)])
+        y = lax.axis_index("y")
+        hidden = hidden.reshape(16 * states, 4, own_rows)
+        hidden = jnp.concatenate(
+            [
+                lax.dynamic_index_in_dim(hidden, y ^ step, axis=1, keepdims=False)
+                for step in range(4)
+            ],
+            axis=1,
+        )
     with jax.named_scope("squares"):
         squares = lax.all_to_all(squares, EVERY, 0, 0, tiled=True)
     with jax.named_scope("place"):
         pairs = [(a * 2 + b, (a + 4) % 8 * 2 + 1 - b) for a in range(8) for b in range(2) if a // 4 != b]
         placed = lax.ppermute(gradient, ("z", "xh"), pairs)
         gradient = jnp.where(z // 4 == xh, gradient, placed)
-        gradient, squares = together(gradient, squares)
+        gradient, squares, hidden = together(gradient, squares, hidden)
     with jax.named_scope("update"):
         new_weight, adam_step, rollout_weight = update(
             squares, gradient, state, float(entry_count)
@@ -458,9 +468,6 @@
             sine,
             step_count,
         )
-        new_keys = new_keys.reshape(row_count, step_count, head_count * HD)
-        new_values = new_values.reshape(row_count, step_count, head_count * HD)
-        attended = attended.reshape(row_count, step_count, head_count * groups * HD)
     return (
         new_weight.reshape(own_rows, 2, columns // 2),
         adam_step.reshape(own_rows, 2, columns // 2),

time: 174 us -> 169 us (0.971)
  other arithmetic: 11.9 us -> 4.76 us
  waiting for transfers between devices: 44 us -> 50 us
  local copies, waits for them, and re-layouts: 14.8 us -> 9.42 us
    ppermute x8, waiting for transfers between devices: 9.77 us -> 20.4 us  [along_y(): return lax.ppermute(values, 'y', PAIRING[pairing])]
    another operation x4 -> x2, other arithmetic: 4.39 us -> 0.07 us  [slots(): jnp.stack([lax.dynamic_index_in_dim(block, at, keepdims=False) for block...]
    all_to_all x1, starting transfers between devices: 13.2 us -> 15.8 us  [local(): squares = lax.all_to_all(squares, EVERY, 0, 0, tiled=True)]
    ppermute x4, waiting for transfers between devices: 9.41 us -> 6.83 us  [trade(): got = lax.ppermute(sent, mesh_axis, partners)]
    optimization_barrier x1 -> x0, local copies, waits for them, and re-layouts: 2.47 us -> none  [together(): return lax.optimization_barrier(values)]
    reshape x3 -> x0, local copies, waits for them, and re-layouts: 1.88 us -> none  [the longest x1 0.66 us: local(): attended = attended.reshape(row_count, step_count, head_count * groups * HD)]
    convert_element_type x6 -> x10, other arithmetic: 4.44 us -> 3.46 us  [add(): return total.astype(BF16)]
    unnamed x21 -> x35, local copies, waits for them, and re-layouts: 5.65 us -> 6.49 us
  transfers between devices with their start and end apart: 22 -> 22, of which waited for: 13 -> 15; matrix products, arithmetic and copies ran while one was open for 13% -> 6% of each run, Pallas kernels for 16% -> 14%
where the time goes in v3:
time: 169 us; the launch traced here: 168 us
  starting transfers between devices  50.3 us (30%)
  waiting for transfers between devices  50 us (30%)
  Pallas kernels  32.4 us (19%)
  blocking collectives  20.5 us (12%)
  local copies, waits for them, and re-layouts  9.42 us (6%)
  other arithmetic  4.76 us (3%)
    all_to_all x1, blocking collectives, local(): parts = lax.all_to_all(parts, 'z', 0, 0)  20.5 us
    ppermute x8, waiting for transfers between devices, along_y(): return lax.ppermute(values, 'y', PAIRING[pairing])  20.4 us
    pallas_call x4, Pallas kernels, product(): pl.pallas_call(product_kernel, out_shape=(pltpu.HBM((2, 2, 2, rows, colum...  19.8 us
    all_to_all x1, starting transfers between devices, local(): squares = lax.all_to_all(squares, EVERY, 0, 0, tiled=True)  15.8 us
    ppermute x4, starting transfers between devices, trade(): got = lax.ppermute(sent, mesh_axis, partners)  12.5 us
    all_to_all x1, waiting for transfers between devices, local(): squares = lax.all_to_all(squares, EVERY, 0, 0, tiled=True)  10.3 us
    ppermute x8, starting transfers between devices, along_y(): return lax.ppermute(values, 'y', PAIRING[pairing])  8.5 us
    pallas_call x1, Pallas kernels, old_attention(): pl.pallas_call(old_attention_kernel, out_shape=(shape, shape, shape), gri...  8.41 us
  transfers between devices with their start and end apart: 22, of which 15 were waited for; matrix products, arithmetic and copies ran while one was open for 6% of the time, Pallas kernels for 14%

profile of v3, /device:TPU:24, one launch (start us, length us, event | category | flops | bytes accessed | tf_op | source)
XLA Modules:
  0.0 168.5 jit_solution(2223744588382652723)
XLA Ops:
  0.7 3.1 %collective-permute-start.5 = (bf16[1024,2,256]{2,1,0:T(2,128)(2,1)}, bf16[1024,2,256]{2,1,0:T(2,128)(2,1)}, u32[]{:S(2)}, u32[]{:S(2)}) collective-permute-start(bf16[1024,2,256]{2,1,0:T(2,128)(2,1)} %param.12), channel_id=1, source_target_pairs={{0,2},{2,0},{1,3},{3,1},{4,6},{6,4},{5,7},{7,5},{8,10},{10,8},{9,1... | collective-permute-start | bytes 3145736 | tf_op jit(solution)/shard_map/exchange/ppermute | solution.py:46
  3.8 2.5 %copy.59 = bf16[128,8,2,256]{3,1,2,0:T(8,128)(2,1)} copy(bf16[128,8,2,256]{3,2,1,0:T(2,128)(2,1)} %bitcast.107) | data formatting | bytes 2097152
  6.4 5.0 %product.4 = (bf16[2,2,2,80,512]{4,3,2,1,0:T(8,128)(2,1)}, bf16[2,2,80,512]{3,2,1,0:T(8,128)(2,1)}, bf16[2,2,80,512]{3,2,1,0:T(8,128)(2,1)}) custom-call(s32[4]{0:T(128)S(1)} %get-tuple-element.154.order, bf16[1024,1280]{1,0:T(8,128)(2,1)} %left_ref.3, bf16[1024,512]{1,0:T(8,128)(2,1)} %bitcast.102), custom_call_target="tpu_custom_call" | custom-call | tf_op jit(solution)/shard_map/first_half/product/pallas_call | solution.py:85
  11.4 1.5 copy-done.2
  12.9 5.0 %product.5 = (bf16[2,2,2,80,512]{4,3,2,1,0:T(8,128)(2,1)}, bf16[2,2,80,512]{3,2,1,0:T(8,128)(2,1)}, bf16[2,2,80,512]{3,2,1,0:T(8,128)(2,1)}) custom-call(s32[4]{0:T(128)S(1)} %get-tuple-element.155.order, bf16[1024,1280]{1,0:T(8,128)(2,1)} %copy-done.2, bf16[1024,512]{1,0:T(8,128)(2,1)} %bitcast.103), custom_call_target="tpu_custom_call" | custom-call | tf_op jit(solution)/shard_map/first_half/product/pallas_call | solution.py:85
  18.1 2.0 %collective-permute-start.3 = (bf16[2,2,2,16,320]{4,3,2,1,0:T(8,128)(2,1)S(1)}, bf16[2,2,2,16,320]{4,3,2,1,0:T(8,128)(2,1)S(1)}, u32[]{:S(2)}, u32[]{:S(2)}) collective-permute-start(bf16[2,2,2,16,320]{4,3,2,1,0:T(8,128)(2,1)S(1)} %get-tuple-element.150), channel_id=1, source_target_pairs={{0,32},{32,0},{64,96},{96,64},{128,160},{160,128},{192,224},{224,1... | collective-permute-start | bytes 245768 | tf_op jit(solution)/shard_map/hidden/ppermute | solution.py:357
  21.9 1.3 collective-permute-done.3
  23.3 3.4 %collective-permute-start.4 = (bf16[2,2,2,16,320]{4,3,2,1,0:T(8,128)(2,1)S(1)}, bf16[2,2,2,16,320]{4,3,2,1,0:T(8,128)(2,1)S(1)}, u32[]{:S(2)}, u32[]{:S(2)}) collective-permute-start(bf16[2,2,2,16,320]{4,3,2,1,0:T(8,128)(2,1)S(1)} %get-tuple-element.148), channel_id=1, source_target_pairs={{0,64},{32,96},{64,0},{96,32},{128,192},{160,224},{192,128},{224,1... | collective-permute-start | bytes 245768 | tf_op jit(solution)/shard_map/hidden/ppermute | solution.py:357
  26.8 4.6 %collective-permute-done.4 = bf16[2,2,2,16,320]{4,3,2,1,0:T(8,128)(2,1)S(1)} collective-permute-done((bf16[2,2,2,16,320]{4,3,2,1,0:T(8,128)(2,1)S(1)}, bf16[2,2,2,16,320]{4,3,2,1,0:T(8,128)(2,1)S(1)}, u32[]{:S(2)}, u32[]{:S(2)}) %collective-permute-start.4) | collective-permute-done | bytes 81952 | tf_op jit(solution)/shard_map/hidden/ppermute | solution.py:357
  31.5 6.3 %collective-permute-start.6 = (bf16[2,2,2,16,320]{4,3,2,1,0:T(8,128)(2,1)S(1)}, bf16[2,2,2,16,320]{4,3,2,1,0:T(8,128)(2,1)S(1)}, u32[]{:S(2)}, u32[]{:S(2)}) collective-permute-start(bf16[2,2,2,16,320]{4,3,2,1,0:T(8,128)(2,1)S(1)} %get-tuple-element.146), channel_id=1, source_target_pairs={{0,128},{32,160},{64,192},{96,224},{128,0},{160,32},{192,64},{224,... | collective-permute-start | bytes 245768 | tf_op jit(solution)/shard_map/hidden/ppermute | solution.py:357
  38.0 2.5 %copy.61 = bf16[128,8,2,256]{3,1,2,0:T(8,128)(2,1)} copy(bf16[128,8,2,256]{3,2,1,0:T(2,128)(2,1)} %bitcast.60) | data formatting | bytes 2097152
  42.3 4.9 %product.6 = (bf16[2,2,2,80,512]{4,3,2,1,0:T(8,128)(2,1)}, bf16[2,2,80,512]{3,2,1,0:T(8,128)(2,1)}, bf16[2,2,80,512]{3,2,1,0:T(8,128)(2,1)}) custom-call(s32[4]{0:T(128)S(1)} %get-tuple-element.154.order, bf16[1024,1280]{1,0:T(8,128)(2,1)} %left_ref.3, bf16[1024,512]{1,0:T(8,128)(2,1)} %bitcast.100), custom_call_target="tpu_custom_call" | custom-call | tf_op jit(solution)/shard_map/second_half/product/pallas_call | solution.py:85
  50.4 5.0 %product.7 = (bf16[2,2,2,80,512]{4,3,2,1,0:T(8,128)(2,1)}, bf16[2,2,80,512]{3,2,1,0:T(8,128)(2,1)}, bf16[2,2,80,512]{3,2,1,0:T(8,128)(2,1)}) custom-call(s32[4]{0:T(128)S(1)} %get-tuple-element.155.order, bf16[1024,1280]{1,0:T(8,128)(2,1)} %copy-done.2, bf16[1024,512]{1,0:T(8,128)(2,1)} %bitcast.101), custom_call_target="tpu_custom_call" | custom-call | tf_op jit(solution)/shard_map/second_half/product/pallas_call | solution.py:85
  55.4 2.1 %collective-permute-done.8 = bf16[2,2,80,512]{3,2,1,0:T(8,128)(2,1)S(1)} collective-permute-done((bf16[2,2,80,512]{3,2,1,0:T(8,128)(2,1)}, bf16[2,2,80,512]{3,2,1,0:T(8,128)(2,1)S(1)}, u32[]{:S(2)}, u32[]{:S(2)}) %collective-permute-start.8) | collective-permute-done | bytes 327712 | tf_op jit(solution)/shard_map/first_half/ppermute | solution.py:115
  57.4 1.9 %collective-permute-done.9 = bf16[2,2,80,512]{3,2,1,0:T(8,128)(2,1)} collective-permute-done((bf16[2,2,80,512]{3,2,1,0:T(8,128)(2,1)}, bf16[2,2,80,512]{3,2,1,0:T(8,128)(2,1)}, u32[]{:S(2)}, u32[]{:S(2)}) %collective-permute-start.9) | collective-permute-done | bytes 327712 | tf_op jit(solution)/shard_map/first_half/ppermute | solution.py:115
  59.3 2.9 %collective-permute-start.10 = (bf16[2,2,2,80,512]{4,3,2,1,0:T(8,128)(2,1)}, bf16[2,2,2,80,512]{4,3,2,1,0:T(8,128)(2,1)S(1)}, u32[]{:S(2)}, u32[]{:S(2)}) collective-permute-start(bf16[2,2,2,80,512]{4,3,2,1,0:T(8,128)(2,1)} %get-tuple-element.97), channel_id=1, source_target_pairs={{0,12},{12,0},{4,8},{8,4},{1,13},{13,1},{5,9},{9,5},{2,14},{14,2},... | collective-permute-start | bytes 1966088 | tf_op jit(solution)/shard_map/second_half/ppermute | solution.py:115
  63.8 6.5 %collective-permute-done.7 = bf16[2,2,2,80,512]{4,3,2,1,0:T(8,128)(2,1)S(1)} collective-permute-done((bf16[2,2,2,80,512]{4,3,2,1,0:T(8,128)(2,1)}, bf16[2,2,2,80,512]{4,3,2,1,0:T(8,128)(2,1)S(1)}, u32[]{:S(2)}, u32[]{:S(2)}) %collective-permute-start.7) | collective-permute-done | bytes 655392 | tf_op jit(solution)/shard_map/second_half/ppermute | solution.py:115
  70.4 3.0 %collective-permute-done.10 = bf16[2,2,2,80,512]{4,3,2,1,0:T(8,128)(2,1)S(1)} collective-permute-done((bf16[2,2,2,80,512]{4,3,2,1,0:T(8,128)(2,1)}, bf16[2,2,2,80,512]{4,3,2,1,0:T(8,128)(2,1)S(1)}, u32[]{:S(2)}, u32[]{:S(2)}) %collective-permute-start.10) | collective-permute-done | bytes 655392 | tf_op jit(solution)/shard_map/second_half/ppermute | solution.py:115
  73.7 1.2 collective-permute-start.12
  75.1 5.7 %collective-permute-done.13 = bf16[2,2,80,512]{3,2,1,0:T(8,128)(2,1)S(1)} collective-permute-done((bf16[2,2,80,512]{3,2,1,0:T(8,128)(2,1)S(1)}, bf16[2,2,80,512]{3,2,1,0:T(8,128)(2,1)S(1)}, u32[]{:S(2)}, u32[]{:S(2)}) %collective-permute-start.13) | collective-permute-done | bytes 327712 | tf_op jit(solution)/shard_map/second_half/ppermute | solution.py:115
  83.5 6.0 %collective-permute-done.14 = bf16[2,2,80,512]{3,2,1,0:T(8,128)(2,1)S(1)} collective-permute-done((bf16[2,2,80,512]{3,2,1,0:T(8,128)(2,1)S(1)}, bf16[2,2,80,512]{3,2,1,0:T(8,128)(2,1)S(1)}, u32[]{:S(2)}, u32[]{:S(2)}) %collective-permute-start.14) | collective-permute-done | bytes 327712 | tf_op jit(solution)/shard_map/second_half/ppermute | solution.py:46
  89.8 20.5 %all_to_all.22.parts_ref = bf16[8,80,512]{2,1,0:T(8,128)(2,1)S(1)} all-to-all(bf16[8,80,512]{2,1,0:T(8,128)(2,1)S(1)} %maximum_select_fusion), channel_id=1, replica_groups=mesh['z'=8,'xl'=2,'y'=4,'xh'=2,'core'=2] {'z'}, dimensions={0} | all-to-all | bytes 1310720 | tf_op jit(solution)/shard_map/reduce_z/all_to_all | solution.py:417
  112.8 15.8 %all-to-all-start.1 = ((f32[256,1,128]{2,1,0:T(1,128)}), f32[256,1,128]{2,1,0:T(1,128)S(1)}, u32[]{:S(2)}, u32[]{:S(2)}) async-start(f32[256,1,128]{2,1,0:T(1,128)} %bitcast.26), calls=%async_computation.1 | async-start | bytes 262144 | tf_op jit(solution)/shard_map/squares/all_to_all | solution.py:432
  129.8 10.3 %all-to-all-done.1 = f32[256,1,128]{2,1,0:T(1,128)S(1)} async-done(((f32[256,1,128]{2,1,0:T(1,128)}), f32[256,1,128]{2,1,0:T(1,128)S(1)}, u32[]{:S(2)}, u32[]{:S(2)}) %all-to-all-start.1) | async-done | bytes 131104 | tf_op jit(solution)/shard_map/squares/all_to_all | solution.py:432
  141.4 2.7 %collective-permute-start.18 = (bf16[80,512]{1,0:T(8,128)(2,1)S(1)}, bf16[80,512]{1,0:T(8,128)(2,1)S(1)}, u32[]{:S(2)}, u32[]{:S(2)}) collective-permute-start(bf16[80,512]{1,0:T(8,128)(2,1)S(1)} %get-tuple-element.121.refs_0_), channel_id=1, source_target_pairs={{0,8},{4,12},{8,0},{12,4},{1,9},{5,13},{9,1},{13,5},{2,10},{6,14},... | collective-permute-start | bytes 245768 | tf_op jit(solution)/shard_map/project/ppermute | solution.py:339
  144.0 1.2 collective-permute-start.19
  145.6 2.7 %collective-permute-done.18.refs_2_ = bf16[80,512]{1,0:T(8,128)(2,1)S(1)} collective-permute-done((bf16[80,512]{1,0:T(8,128)(2,1)S(1)}, bf16[80,512]{1,0:T(8,128)(2,1)S(1)}, u32[]{:S(2)}, u32[]{:S(2)}) %collective-permute-start.18) | collective-permute-done | bytes 81952 | tf_op jit(solution)/shard_map/project/ppermute | solution.py:339
  148.3 1.7 collective-permute-done.19.refs_3_
  150.9 3.5 %all-to-all-start.2 = ((bf16[16,16,512]{2,1,0:T(8,128)(2,1)}), bf16[16,16,512]{2,1,0:T(8,128)(2,1)S(1)}, u32[]{:S(2)}, u32[]{:S(2)}) async-start(bf16[16,16,512]{2,1,0:T(8,128)(2,1)} %bitcast.40), calls=%async_computation.2 | async-start | bytes 524288 | tf_op jit(solution)/shard_map/project/all_to_all | solution.py:446
  156.4 8.4 %old_attention.1 = (f32[2,4,32,128]{3,2,1,0:T(8,128)S(1)}, f32[2,4,32,128]{3,2,1,0:T(8,128)S(1)}, f32[2,4,32,128]{3,2,1,0:T(8,128)S(1)}) custom-call(s32[4]{0:T(128)S(1)} %copy-done, bf16[2,4,32,128]{3,2,1,0:T(8,128)(2,1)S(1)} %bitcast.93, bf16[4,2048,256]{2,1,0:T(8,128)(2,1)} %key_ref.1, bf16[4,2048,256]{2,1,0:T(8,128)(2,1)} %value_ref.1), custom_call_target="tpu_custom_call" | custom-call | tf_op jit(solution)/shard_map/old/old_attention/pallas_call | solution.py:143
  164.8 1.8 %all-to-all-done.2.part_ref = bf16[16,16,512]{2,1,0:T(8,128)(2,1)S(1)} async-done(((bf16[16,16,512]{2,1,0:T(8,128)(2,1)}), bf16[16,16,512]{2,1,0:T(8,128)(2,1)S(1)}, u32[]{:S(2)}, u32[]{:S(2)}) %all-to-all-start.2) | async-done | bytes 262176 | tf_op jit(solution)/shard_map/project/all_to_all | solution.py:446
  166.6 1.9 %fresh_attention.1 = (bf16[4,4,256]{2,1,0:T(4,128)(2,1)}, bf16[4,4,256]{2,1,0:T(4,128)(2,1)}, bf16[4,4,2048]{2,1,0:T(4,128)(2,1)}) custom-call(bf16[16,16,512]{2,1,0:T(8,128)(2,1)S(1)} %all-to-all-done.2.part_ref, bf16[2,128,128]{2,1,0:T(8,128)(2,1)S(1)} %bitcast.94, f32[2,128,128]{2,1,0:T(8,128)S(1)} %bitcast.96, f32[2,128,128]{2,1,0:T(8,128)S(1)} %bitcast.97, ...), custom_call_target="tpu_custom_call" | custom-call | tf_op jit(solution)/shard_map/fresh/fresh_attention/pallas_call | solution.py:220
  (105 shorter events, 20.6 us)
Async XLA Ops:
  0.6 10.7 %collective-permute-start = (bf16[1024,1280]{1,0:T(8,128)(2,1)}, bf16[1024,1280]{1,0:T(8,128)(2,1)S(1)}, u32[]{:S(2)}, u32[]{:S(2)}) collective-permute-start(bf16[1024,1280]{1,0:T(8,128)(2,1)} %left_ref.3), channel_id=1, source_target_pairs={{0,1},{1,0},{2,3},{3,2},{4,5},{5,4},{6,7},{7,6},{8,9},{9,8},{10,11... | collective-permute-start | bytes 7864328 | tf_op jit(solution)/shard_map/exchange/ppermute | solution.py:46
  0.7 30.7 %collective-permute-start.5 = (bf16[1024,2,256]{2,1,0:T(2,128)(2,1)}, bf16[1024,2,256]{2,1,0:T(2,128)(2,1)}, u32[]{:S(2)}, u32[]{:S(2)}) collective-permute-start(bf16[1024,2,256]{2,1,0:T(2,128)(2,1)} %param.12), channel_id=1, source_target_pairs={{0,2},{2,0},{1,3},{3,1},{4,6},{6,4},{5,7},{7,5},{8,10},{10,8},{9,1... | collective-permute-start | bytes 3145736 | tf_op jit(solution)/shard_map/exchange/ppermute | solution.py:46
  6.4 20.3 %copy-start.15 = (bf16[4,4,2048]{2,1,0:T(4,128)(2,1)S(1)}, bf16[4,4,2048]{2,1,0:T(4,128)(2,1)}, u32[]{:S(2)}) copy-start(bf16[4,4,2048]{2,1,0:T(4,128)(2,1)} %param.17) | copy-start | bytes 196612
  11.4 26.4 %copy-start.12 = (f32[80,2,256]{2,1,0:T(2,128)S(1)}, f32[80,2,256]{2,1,0:T(2,128)}, u32[]{:S(2)}) copy-start(f32[80,2,256]{2,1,0:T(2,128)} %param.15) | copy-start | bytes 491524
  11.4 26.4 %copy-start.13 = (f32[80,2,256]{2,1,0:T(2,128)S(1)}, f32[80,2,256]{2,1,0:T(2,128)}, u32[]{:S(2)}) copy-start(f32[80,2,256]{2,1,0:T(2,128)} %param.14) | copy-start | bytes 491524
  11.4 26.4 %copy-start.14 = (f32[80,2,256]{2,1,0:T(2,128)S(1)}, f32[80,2,256]{2,1,0:T(2,128)}, u32[]{:S(2)}) copy-start(f32[80,2,256]{2,1,0:T(2,128)} %param.13) | copy-start | bytes 491524
  17.8 23.7 %copy-start.7 = (bf16[2,2,80,512]{3,2,1,0:T(8,128)(2,1)S(1)}, bf16[2,2,80,512]{3,2,1,0:T(8,128)(2,1)}, u32[]{:S(2)}) copy-start(bf16[2,2,80,512]{3,2,1,0:T(8,128)(2,1)} %get-tuple-element.68) | copy-start | bytes 983044
  18.1 5.1 %collective-permute-start.3 = (bf16[2,2,2,16,320]{4,3,2,1,0:T(8,128)(2,1)S(1)}, bf16[2,2,2,16,320]{4,3,2,1,0:T(8,128)(2,1)S(1)}, u32[]{:S(2)}, u32[]{:S(2)}) collective-permute-start(bf16[2,2,2,16,320]{4,3,2,1,0:T(8,128)(2,1)S(1)} %get-tuple-element.150), channel_id=1, source_target_pairs={{0,32},{32,0},{64,96},{96,64},{128,160},{160,128},{192,224},{224,1... | collective-permute-start | bytes 245768 | tf_op jit(solution)/shard_map/hidden/ppermute | solution.py:357
  20.1 21.4 %collective-permute-start.1 = (bf16[2,2,2,80,512]{4,3,2,1,0:T(8,128)(2,1)}, bf16[2,2,2,80,512]{4,3,2,1,0:T(8,128)(2,1)S(1)}, u32[]{:S(2)}, u32[]{:S(2)}) collective-permute-start(bf16[2,2,2,80,512]{4,3,2,1,0:T(8,128)(2,1)} %get-tuple-element.70), channel_id=1, source_target_pairs={{0,4},{4,0},{8,12},{12,8},{1,5},{5,1},{9,13},{13,9},{2,6},{6,2},{1... | collective-permute-start | bytes 1966088 | tf_op jit(solution)/shard_map/first_half/ppermute | solution.py:115
  20.8 20.6 %collective-permute-start.2 = (bf16[2,2,2,80,512]{4,3,2,1,0:T(8,128)(2,1)}, bf16[2,2,2,80,512]{4,3,2,1,0:T(8,128)(2,1)S(1)}, u32[]{:S(2)}, u32[]{:S(2)}) collective-permute-start(bf16[2,2,2,80,512]{4,3,2,1,0:T(8,128)(2,1)} %get-tuple-element.72), channel_id=1, source_target_pairs={{0,12},{12,0},{4,8},{8,4},{1,13},{13,1},{5,9},{9,5},{2,14},{14,2},... | collective-permute-start | bytes 1966088 | tf_op jit(solution)/shard_map/first_half/ppermute | solution.py:115
  23.3 8.1 %collective-permute-start.4 = (bf16[2,2,2,16,320]{4,3,2,1,0:T(8,128)(2,1)S(1)}, bf16[2,2,2,16,320]{4,3,2,1,0:T(8,128)(2,1)S(1)}, u32[]{:S(2)}, u32[]{:S(2)}) collective-permute-start(bf16[2,2,2,16,320]{4,3,2,1,0:T(8,128)(2,1)S(1)} %get-tuple-element.148), channel_id=1, source_target_pairs={{0,64},{32,96},{64,0},{96,32},{128,192},{160,224},{192,128},{224,1... | collective-permute-start | bytes 245768 | tf_op jit(solution)/shard_map/hidden/ppermute | solution.py:357
  31.5 9.9 %collective-permute-start.6 = (bf16[2,2,2,16,320]{4,3,2,1,0:T(8,128)(2,1)S(1)}, bf16[2,2,2,16,320]{4,3,2,1,0:T(8,128)(2,1)S(1)}, u32[]{:S(2)}, u32[]{:S(2)}) collective-permute-start(bf16[2,2,2,16,320]{4,3,2,1,0:T(8,128)(2,1)S(1)} %get-tuple-element.146), channel_id=1, source_target_pairs={{0,128},{32,160},{64,192},{96,224},{128,0},{160,32},{192,64},{224,... | collective-permute-start | bytes 245768 | tf_op jit(solution)/shard_map/hidden/ppermute | solution.py:357
  42.3 20.0 %copy-start.4 = (bf16[2,2,80,512]{3,2,1,0:T(8,128)(2,1)S(1)}, bf16[2,2,80,512]{3,2,1,0:T(8,128)(2,1)}, u32[]{:S(2)}) copy-start(bf16[2,2,80,512]{3,2,1,0:T(8,128)(2,1)} %get-tuple-element.100) | copy-start | bytes 983044
  42.3 21.1 %copy-start.3 = (bf16[2,2,80,512]{3,2,1,0:T(8,128)(2,1)S(1)}, bf16[2,2,80,512]{3,2,1,0:T(8,128)(2,1)}, u32[]{:S(2)}) copy-start(bf16[2,2,80,512]{3,2,1,0:T(8,128)(2,1)} %get-tuple-element.98) | copy-start | bytes 983044
  48.1 22.2 %copy-start.9 = (bf16[2,2,80,512]{3,2,1,0:T(8,128)(2,1)S(1)}, bf16[2,2,80,512]{3,2,1,0:T(8,128)(2,1)}, u32[]{:S(2)}) copy-start(bf16[2,2,80,512]{3,2,1,0:T(8,128)(2,1)} %get-tuple-element.85) | copy-start | bytes 983044
  48.1 9.3 %collective-permute-start.8 = (bf16[2,2,80,512]{3,2,1,0:T(8,128)(2,1)}, bf16[2,2,80,512]{3,2,1,0:T(8,128)(2,1)S(1)}, u32[]{:S(2)}, u32[]{:S(2)}) collective-permute-start(bf16[2,2,80,512]{3,2,1,0:T(8,128)(2,1)} %fusion.11), channel_id=1, source_target_pairs={{0,12},{12,0},{4,8},{8,4},{1,13},{13,1},{5,9},{9,5},{2,14},{14,2},... | collective-permute-start | bytes 983048 | tf_op jit(solution)/shard_map/first_half/ppermute | solution.py:115
  48.4 11.0 %collective-permute-start.9 = (bf16[2,2,80,512]{3,2,1,0:T(8,128)(2,1)}, bf16[2,2,80,512]{3,2,1,0:T(8,128)(2,1)}, u32[]{:S(2)}, u32[]{:S(2)}) collective-permute-start(bf16[2,2,80,512]{3,2,1,0:T(8,128)(2,1)} %fusion.9), channel_id=1, source_target_pairs={{0,4},{4,0},{8,12},{12,8},{1,5},{5,1},{9,13},{13,9},{2,6},{6,2},{1... | collective-permute-start | bytes 983048 | tf_op jit(solution)/shard_map/first_half/ppermute | solution.py:115
  49.3 21.0 %collective-permute-start.7 = (bf16[2,2,2,80,512]{4,3,2,1,0:T(8,128)(2,1)}, bf16[2,2,2,80,512]{4,3,2,1,0:T(8,128)(2,1)S(1)}, u32[]{:S(2)}, u32[]{:S(2)}) collective-permute-start(bf16[2,2,2,80,512]{4,3,2,1,0:T(8,128)(2,1)} %get-tuple-element.88), channel_id=1, source_target_pairs={{0,4},{4,0},{8,12},{12,8},{1,5},{5,1},{9,13},{13,9},{2,6},{6,2},{1... | collective-permute-start | bytes 1966088 | tf_op jit(solution)/shard_map/second_half/ppermute | solution.py:115
  55.4 25.4 %copy-start.6 = (bf16[2,2,80,512]{3,2,1,0:T(8,128)(2,1)S(1)}, bf16[2,2,80,512]{3,2,1,0:T(8,128)(2,1)}, u32[]{:S(2)}) copy-start(bf16[2,2,80,512]{3,2,1,0:T(8,128)(2,1)} %get-tuple-element.107) | copy-start | bytes 983044
  59.3 14.0 %collective-permute-start.10 = (bf16[2,2,2,80,512]{4,3,2,1,0:T(8,128)(2,1)}, bf16[2,2,2,80,512]{4,3,2,1,0:T(8,128)(2,1)S(1)}, u32[]{:S(2)}, u32[]{:S(2)}) collective-permute-start(bf16[2,2,2,80,512]{4,3,2,1,0:T(8,128)(2,1)} %get-tuple-element.97), channel_id=1, source_target_pairs={{0,12},{12,0},{4,8},{8,4},{1,13},{13,1},{5,9},{9,5},{2,14},{14,2},... | collective-permute-start | bytes 1966088 | tf_op jit(solution)/shard_map/second_half/ppermute | solution.py:115
  63.7 9.8 %collective-permute-start.11 = (bf16[2,2,80,512]{3,2,1,0:T(8,128)(2,1)S(1)}, bf16[2,2,80,512]{3,2,1,0:T(8,128)(2,1)S(1)}, u32[]{:S(2)}, u32[]{:S(2)}) collective-permute-start(bf16[2,2,80,512]{3,2,1,0:T(8,128)(2,1)S(1)} %pad_maximum_fusion.1), channel_id=1, source_target_pairs={{0,16},{16,0},{1,17},{17,1},{2,18},{18,2},{3,19},{19,3},{4,20},{20... | collective-permute-start | bytes 983048 | tf_op jit(solution)/shard_map/first_half/ppermute | solution.py:46
  73.5 7.3 %collective-permute-start.13 = (bf16[2,2,80,512]{3,2,1,0:T(8,128)(2,1)S(1)}, bf16[2,2,80,512]{3,2,1,0:T(8,128)(2,1)S(1)}, u32[]{:S(2)}, u32[]{:S(2)}) collective-permute-start(bf16[2,2,80,512]{3,2,1,0:T(8,128)(2,1)S(1)} %fusion.8), channel_id=1, source_target_pairs={{0,4},{4,0},{8,12},{12,8},{1,5},{5,1},{9,13},{13,9},{2,6},{6,2},{1... | collective-permute-start | bytes 983048 | tf_op jit(solution)/shard_map/second_half/ppermute | solution.py:115
  73.7 8.4 %collective-permute-start.12 = (bf16[2,2,80,512]{3,2,1,0:T(8,128)(2,1)S(1)}, bf16[2,2,80,512]{3,2,1,0:T(8,128)(2,1)S(1)}, u32[]{:S(2)}, u32[]{:S(2)}) collective-permute-start(bf16[2,2,80,512]{3,2,1,0:T(8,128)(2,1)S(1)} %fusion.10), channel_id=1, source_target_pairs={{0,12},{12,0},{4,8},{8,4},{1,13},{13,1},{5,9},{9,5},{2,14},{14,2},... | collective-permute-start | bytes 983048 | tf_op jit(solution)/shard_map/second_half/ppermute | solution.py:115
  82.3 7.2 %collective-permute-start.14 = (bf16[2,2,80,512]{3,2,1,0:T(8,128)(2,1)S(1)}, bf16[2,2,80,512]{3,2,1,0:T(8,128)(2,1)S(1)}, u32[]{:S(2)}, u32[]{:S(2)}) collective-permute-start(bf16[2,2,80,512]{3,2,1,0:T(8,128)(2,1)S(1)} %pad_maximum_fusion.2), channel_id=1, source_target_pairs={{0,16},{16,0},{1,17},{17,1},{2,18},{18,2},{3,19},{19,3},{4,20},{20... | collective-permute-start | bytes 983048 | tf_op jit(solution)/shard_map/second_half/ppermute | solution.py:46
  89.8 64.7 %copy-start = (s32[4]{0:T(128)S(1)}, s32[4]{0:T(128)}, u32[]{:S(2)}) copy-start(s32[4]{0:T(128)} %length_ref.1) | copy-start | bytes 52
  111.3 17.4 %collective-permute-start.16 = (bf16[2,2,2,16,320]{4,3,2,1,0:T(8,128)(2,1)S(1)}, bf16[2,2,2,16,320]{4,3,2,1,0:T(8,128)(2,1)S(1)}, u32[]{:S(2)}, u32[]{:S(2)}) collective-permute-start(bf16[2,2,2,16,320]{4,3,2,1,0:T(8,128)(2,1)S(1)} %get-tuple-element.144), channel_id=1, source_target_pairs={{0,16},{16,0},{1,17},{17,1},{2,18},{18,2},{3,19},{19,3},{4,20},{20... | collective-permute-start | bytes 245768 | tf_op jit(solution)/shard_map/hidden/ppermute | solution.py:357
  112.2 17.6 %collective-permute-start.15 = (f32[80,512]{1,0:T(8,128)S(1)}, f32[80,512]{1,0:T(8,128)S(1)}, u32[]{:S(2)}, u32[]{:S(2)}) collective-permute-start(f32[80,512]{1,0:T(8,128)S(1)} %get-tuple-element.112), channel_id=1, source_target_pairs={{2,128},{34,160},{66,192},{98,224},{128,2},{160,34},{192,66},{224,... | collective-permute-start | bytes 491528 | tf_op jit(solution)/shard_map/place/ppermute | solution.py:435
  112.8 27.3 %all-to-all-start.1 = ((f32[256,1,128]{2,1,0:T(1,128)}), f32[256,1,128]{2,1,0:T(1,128)S(1)}, u32[]{:S(2)}, u32[]{:S(2)}) async-start(f32[256,1,128]{2,1,0:T(1,128)} %bitcast.26), calls=%async_computation.1 | async-start | bytes 262144 | tf_op jit(solution)/shard_map/squares/all_to_all | solution.py:432
  140.5 5.1 %collective-permute-start.17 = (bf16[80,512]{1,0:T(8,128)(2,1)S(1)}, bf16[80,512]{1,0:T(8,128)(2,1)S(1)}, u32[]{:S(2)}, u32[]{:S(2)}) collective-permute-start(bf16[80,512]{1,0:T(8,128)(2,1)S(1)} %get-tuple-element.121.refs_0_), channel_id=1, source_target_pairs={{0,4},{4,0},{8,12},{12,8},{1,5},{5,1},{9,13},{13,9},{2,6},{6,2},{1... | collective-permute-start | bytes 245768 | tf_op jit(solution)/shard_map/project/ppermute | solution.py:339
  141.4 6.9 %collective-permute-start.18 = (bf16[80,512]{1,0:T(8,128)(2,1)S(1)}, bf16[80,512]{1,0:T(8,128)(2,1)S(1)}, u32[]{:S(2)}, u32[]{:S(2)}) collective-permute-start(bf16[80,512]{1,0:T(8,128)(2,1)S(1)} %get-tuple-element.121.refs_0_), channel_id=1, source_target_pairs={{0,8},{4,12},{8,0},{12,4},{1,9},{5,13},{9,1},{13,5},{2,10},{6,14},... | collective-permute-start | bytes 245768 | tf_op jit(solution)/shard_map/project/ppermute | solution.py:339
  144.0 5.9 %collective-permute-start.19 = (bf16[80,512]{1,0:T(8,128)(2,1)S(1)}, bf16[80,512]{1,0:T(8,128)(2,1)S(1)}, u32[]{:S(2)}, u32[]{:S(2)}) collective-permute-start(bf16[80,512]{1,0:T(8,128)(2,1)S(1)} %get-tuple-element.121.refs_0_), channel_id=1, source_target_pairs={{0,12},{4,8},{8,4},{12,0},{1,13},{5,9},{9,5},{13,1},{2,14},{6,10},... | collective-permute-start | bytes 245768 | tf_op jit(solution)/shard_map/project/ppermute | solution.py:339
  150.9 15.7 %all-to-all-start.2 = ((bf16[16,16,512]{2,1,0:T(8,128)(2,1)}), bf16[16,16,512]{2,1,0:T(8,128)(2,1)S(1)}, u32[]{:S(2)}, u32[]{:S(2)}) async-start(bf16[16,16,512]{2,1,0:T(8,128)(2,1)} %bitcast.40), calls=%async_computation.2 | async-start | bytes 524288 | tf_op jit(solution)/shard_map/project/all_to_all | solution.py:446
  (6 other events, 69.2 us)

commit v4 on v3

--- a/solution.py
+++ b/solution.py
@@ -338,17 +338,6 @@
     def from_y(values, step):
         return lax.ppermute(values, "y", [(a, a ^ step) for a in range(4)])
 
-    with jax.named_scope("first_half"):
-        away, one_near, one_mine = product(tokens, upstream, 0, own_rows)
-        away, tokens_other, queries, rollout_hidden = together(
-            away, tokens_other, queries, rollout_hidden
-        )
-        one_got = along_y(away, 0)
-        away, two_near, two_mine = product(tokens_other, upstream, 1, own_rows)
-        two_near, rollout_hidden, weight, moment_one, moment_two = together(
-            two_near, rollout_hidden, weight, moment_one, moment_two
-        )
-        two_got = along_y(away, 1)
     def trade(block, axis, bit, partners):
         mesh_axis = "xl" if bit is None else "z"
         mine = xl if bit is None else (z >> bit) & 1
@@ -362,12 +351,25 @@
     def trade_z(block, bit):
         return trade(block, 2 - bit, bit, [(a, a ^ (1 << bit)) for a in range(8)])
 
+    with jax.named_scope("first_half"):
+        away, one_near, one_mine = product(tokens, upstream, 0, own_rows)
+        away, tokens_other, queries, rollout_hidden = together(
+            away, tokens_other, queries, rollout_hidden
+        )
+        one_got = along_y(away, 0)
     with jax.named_scope("hidden"):
         hidden = rollout_hidden.reshape(states, 16, 4 * own_rows).transpose(1, 0, 2)
         hidden = hidden.reshape(2, 2, 2, 2, states, 4 * own_rows)
-        hidden = trade_z(trade_z(hidden, 0), 1)
+        hidden = trade_z(hidden, 0)
+    with jax.named_scope("first_half"):
+        away, two_near, two_mine = product(tokens_other, upstream, 1, own_rows)
+        two_near, hidden, weight, moment_one, moment_two = together(
+            two_near, hidden, weight, moment_one, moment_two
+        )
+        two_got = along_y(away, 1)
+    with jax.named_scope("hidden"):
+        hidden = trade_z(trade_z(hidden, 1), 2)
         hidden, upstream_other = together(hidden, upstream_other)
-        hidden = trade_z(hidden, 2)
     with jax.named_scope("state"):
         query_heads = queries.reshape(row_count, step_count, head_count, groups, HD)
         query_heads = query_heads.transpose(2, 0, 3, 1, 4)
@@ -395,7 +397,11 @@
         four_got = along_y(away, 1)
     with jax.named_scope("first_half"):
         kept, sent = by_xl(add(one_mine, one_got[1], one_last), add(two_mine, two_got[1], two_last))
+        sent, query_heads = together(sent, query_heads)
         arrived = swap(sent, "xl")
+    with jax.named_scope("old"):
+        old = old_attention(query_heads, cache_keys, cache_values, cache_lengths)
+        three_got, *old = together(three_got, *old)
     with jax.named_scope("second_half"):
         three_passed = add(three_near, three_got[0])
         four_passed = add(four_near, four_got[0])
@@ -442,14 +448,8 @@
     with jax.named_scope("project"):
         weights = [rollout_weight] + [from_y(rollout_weight, step) for step in range(1, 4)]
         partial = project(hidden, weights)
-        partial, query_heads = together(partial, query_heads)
         partial = lax.all_to_all(partial.reshape(16, states, columns), ("z", "xl"), 0, 0)
-    with jax.named_scope("old"):
-        old = old_attention(query_heads, cache_keys, cache_values, cache_lengths)
-
-        def flat(values):
-            return values.reshape(head_count, groups * states, HD)
-
+    with jax.named_scope("angles"):
         half_width = HD // 2
         frequency = rope_base ** (-2.0 * jnp.arange(half_width, dtype=F32) / HD)
         positions = cache_lengths[:, None] + jnp.arange(step_count, dtype=jnp.int32)[None, :]
@@ -461,8 +461,10 @@
     with jax.named_scope("fresh"):
         new_keys, new_values, attended = fresh_attention(
             partial,
-            flat(query_heads),
-            *[flat(values) for values in old],
+            *[
+                values.reshape(head_count, groups * states, HD)
+                for values in (query_heads, *old)
+            ],
             key_gain.reshape(1, HD),
             cosine,
             sine,

time: 169 us -> 166 us (0.982)
  waiting for transfers between devices: 50 us -> 47.6 us
  starting transfers between devices: 50.3 us -> 48.5 us
    ppermute x8, waiting for transfers between devices: 20.4 us -> 10.4 us  [along_y(): return lax.ppermute(values, 'y', PAIRING[pairing])]
    all_to_all x1, waiting for transfers between devices: 1.8 us -> 10.2 us  [local(): lax.all_to_all(partial.reshape(16, states, columns), ('z', 'xl'), 0, 0)]
    all_to_all x1, starting transfers between devices: 15.8 us -> 13.3 us  [local(): squares = lax.all_to_all(squares, EVERY, 0, 0, tiled=True)]
    unnamed x35 -> x27, local copies, waits for them, and re-layouts: 6.49 us -> 4.94 us
  transfers between devices with their start and end apart: 22 -> 22, of which waited for: 15 -> 12; matrix products, arithmetic and copies ran while one was open for 6% -> 7% of each run, Pallas kernels for 14% -> 14%
where the time goes in v4:
time: 166 us; the launch traced here: 165 us
  starting transfers between devices  48.5 us (29%)
  waiting for transfers between devices  47.6 us (29%)
  Pallas kernels  32.4 us (20%)
  blocking collectives  21.7 us (13%)
  local copies, waits for them, and re-layouts  8.71 us (5%)
  other arithmetic  5.31 us (3%)
    all_to_all x1, blocking collectives, local(): parts = lax.all_to_all(parts, 'z', 0, 0)  21.7 us
    pallas_call x4, Pallas kernels, product(): pl.pallas_call(product_kernel, out_shape=(pltpu.HBM((2, 2, 2, rows, colum...  19.8 us
    all_to_all x1, starting transfers between devices, local(): squares = lax.all_to_all(squares, EVERY, 0, 0, tiled=True)  13.3 us
    ppermute x4, starting transfers between devices, trade(): got = lax.ppermute(sent, mesh_axis, partners)  12 us
    ppermute x8, waiting for transfers between devices, along_y(): return lax.ppermute(values, 'y', PAIRING[pairing])  10.4 us
    all_to_all x1, waiting for transfers between devices, local(): squares = lax.all_to_all(squares, EVERY, 0, 0, tiled=True)  10.3 us
    all_to_all x1, waiting for transfers between devices, local(): lax.all_to_all(partial.reshape(16, states, columns), ('z', 'xl'), 0, 0)  10.2 us
    ppermute x8, starting transfers between devices, along_y(): return lax.ppermute(values, 'y', PAIRING[pairing])  9.2 us
  transfers between devices with their start and end apart: 22, of which 12 were waited for; matrix products, arithmetic and copies ran while one was open for 7% of the time, Pallas kernels for 14%

profile of v4, /device:TPU:24, one launch (start us, length us, event | category | flops | bytes accessed | tf_op | source)
XLA Modules:
  0.0 165.2 jit_solution(15074517783945889452)
XLA Ops:
  0.7 3.1 %collective-permute-start.6 = (bf16[1024,2,256]{2,1,0:T(2,128)(2,1)}, bf16[1024,2,256]{2,1,0:T(2,128)(2,1)}, u32[]{:S(2)}, u32[]{:S(2)}) collective-permute-start(bf16[1024,2,256]{2,1,0:T(2,128)(2,1)} %param.12), channel_id=1, source_target_pairs={{0,2},{2,0},{1,3},{3,1},{4,6},{6,4},{5,7},{7,5},{8,10},{10,8},{9,1... | collective-permute-start | bytes 3145736 | tf_op jit(solution)/shard_map/exchange/ppermute | solution.py:46
  3.9 2.4 %copy.59 = bf16[128,8,2,256]{3,1,2,0:T(8,128)(2,1)} copy(bf16[128,8,2,256]{3,2,1,0:T(2,128)(2,1)} %bitcast.103) | data formatting | bytes 2097152
  6.4 5.0 %product.4 = (bf16[2,2,2,80,512]{4,3,2,1,0:T(8,128)(2,1)}, bf16[2,2,80,512]{3,2,1,0:T(8,128)(2,1)}, bf16[2,2,80,512]{3,2,1,0:T(8,128)(2,1)}) custom-call(s32[4]{0:T(128)S(1)} %get-tuple-element.162.order, bf16[1024,1280]{1,0:T(8,128)(2,1)} %left_ref.3, bf16[1024,512]{1,0:T(8,128)(2,1)} %bitcast.96), custom_call_target="tpu_custom_call" | custom-call | tf_op jit(solution)/shard_map/first_half/product/pallas_call | solution.py:85
  11.6 2.0 %collective-permute-start.3 = (bf16[2,2,2,16,320]{4,3,2,1,0:T(8,128)(2,1)S(1)}, bf16[2,2,2,16,320]{4,3,2,1,0:T(8,128)(2,1)S(1)}, u32[]{:S(2)}, u32[]{:S(2)}) collective-permute-start(bf16[2,2,2,16,320]{4,3,2,1,0:T(8,128)(2,1)S(1)} %get-tuple-element.158), channel_id=1, source_target_pairs={{0,32},{32,0},{64,96},{96,64},{128,160},{160,128},{192,224},{224,1... | collective-permute-start | bytes 245768 | tf_op jit(solution)/shard_map/hidden/ppermute | solution.py:346
  14.4 4.9 %product.5 = (bf16[2,2,2,80,512]{4,3,2,1,0:T(8,128)(2,1)}, bf16[2,2,80,512]{3,2,1,0:T(8,128)(2,1)}, bf16[2,2,80,512]{3,2,1,0:T(8,128)(2,1)}) custom-call(s32[4]{0:T(128)S(1)} %get-tuple-element.163.order, bf16[1024,1280]{1,0:T(8,128)(2,1)} %copy-done.2, bf16[1024,512]{1,0:T(8,128)(2,1)} %bitcast.97), custom_call_target="tpu_custom_call" | custom-call | tf_op jit(solution)/shard_map/first_half/product/pallas_call | solution.py:85
  20.5 3.4 %collective-permute-start.4 = (bf16[2,2,2,16,320]{4,3,2,1,0:T(8,128)(2,1)S(1)}, bf16[2,2,2,16,320]{4,3,2,1,0:T(8,128)(2,1)S(1)}, u32[]{:S(2)}, u32[]{:S(2)}) collective-permute-start(bf16[2,2,2,16,320]{4,3,2,1,0:T(8,128)(2,1)S(1)} %get-tuple-element.156), channel_id=1, source_target_pairs={{0,64},{32,96},{64,0},{96,32},{128,192},{160,224},{192,128},{224,1... | collective-permute-start | bytes 245768 | tf_op jit(solution)/shard_map/hidden/ppermute | solution.py:346
  24.8 3.3 %collective-permute-done.4 = bf16[2,2,2,16,320]{4,3,2,1,0:T(8,128)(2,1)S(1)} collective-permute-done((bf16[2,2,2,16,320]{4,3,2,1,0:T(8,128)(2,1)S(1)}, bf16[2,2,2,16,320]{4,3,2,1,0:T(8,128)(2,1)S(1)}, u32[]{:S(2)}, u32[]{:S(2)}) %collective-permute-start.4) | collective-permute-done | bytes 81952 | tf_op jit(solution)/shard_map/hidden/ppermute | solution.py:346
  28.1 6.0 %collective-permute-start.5 = (bf16[2,2,2,16,320]{4,3,2,1,0:T(8,128)(2,1)S(1)}, bf16[2,2,2,16,320]{4,3,2,1,0:T(8,128)(2,1)S(1)}, u32[]{:S(2)}, u32[]{:S(2)}) collective-permute-start(bf16[2,2,2,16,320]{4,3,2,1,0:T(8,128)(2,1)S(1)} %get-tuple-element.154), channel_id=1, source_target_pairs={{0,128},{32,160},{64,192},{96,224},{128,0},{160,32},{192,64},{224,... | collective-permute-start | bytes 245768 | tf_op jit(solution)/shard_map/hidden/ppermute | solution.py:346
  34.1 1.3 pad_maximum_fusion
  35.5 2.6 %collective-permute-done.5 = bf16[2,2,2,16,320]{4,3,2,1,0:T(8,128)(2,1)S(1)} collective-permute-done((bf16[2,2,2,16,320]{4,3,2,1,0:T(8,128)(2,1)S(1)}, bf16[2,2,2,16,320]{4,3,2,1,0:T(8,128)(2,1)S(1)}, u32[]{:S(2)}, u32[]{:S(2)}) %collective-permute-start.5) | collective-permute-done | bytes 81952 | tf_op jit(solution)/shard_map/hidden/ppermute | solution.py:346
  38.1 2.4 %copy.61 = bf16[128,8,2,256]{3,1,2,0:T(8,128)(2,1)} copy(bf16[128,8,2,256]{3,2,1,0:T(2,128)(2,1)} %bitcast.60) | data formatting | bytes 2097152
  41.6 5.0 %product.6 = (bf16[2,2,2,80,512]{4,3,2,1,0:T(8,128)(2,1)}, bf16[2,2,80,512]{3,2,1,0:T(8,128)(2,1)}, bf16[2,2,80,512]{3,2,1,0:T(8,128)(2,1)}) custom-call(s32[4]{0:T(128)S(1)} %get-tuple-element.162.order, bf16[1024,1280]{1,0:T(8,128)(2,1)} %left_ref.3, bf16[1024,512]{1,0:T(8,128)(2,1)} %bitcast.98), custom_call_target="tpu_custom_call" | custom-call | tf_op jit(solution)/shard_map/second_half/product/pallas_call | solution.py:85
  46.7 2.2 %collective-permute-start.8 = (bf16[2,2,80,512]{3,2,1,0:T(8,128)(2,1)S(1)}, bf16[2,2,80,512]{3,2,1,0:T(8,128)(2,1)S(1)}, u32[]{:S(2)}, u32[]{:S(2)}) collective-permute-start(bf16[2,2,80,512]{3,2,1,0:T(8,128)(2,1)S(1)} %fusion.11), channel_id=1, source_target_pairs={{0,12},{12,0},{4,8},{8,4},{1,13},{13,1},{5,9},{9,5},{2,14},{14,2},... | collective-permute-start | bytes 983048 | tf_op jit(solution)/shard_map/first_half/ppermute | solution.py:115
  48.9 2.0 %collective-permute-start.7 = (bf16[2,2,2,80,512]{4,3,2,1,0:T(8,128)(2,1)}, bf16[2,2,2,80,512]{4,3,2,1,0:T(8,128)(2,1)S(1)}, u32[]{:S(2)}, u32[]{:S(2)}) collective-permute-start(bf16[2,2,2,80,512]{4,3,2,1,0:T(8,128)(2,1)} %get-tuple-element.92), channel_id=1, source_target_pairs={{0,4},{4,0},{8,12},{12,8},{1,5},{5,1},{9,13},{13,9},{2,6},{6,2},{1... | collective-permute-start | bytes 1966088 | tf_op jit(solution)/shard_map/second_half/ppermute | solution.py:115
  50.9 4.9 %product.7 = (bf16[2,2,2,80,512]{4,3,2,1,0:T(8,128)(2,1)}, bf16[2,2,80,512]{3,2,1,0:T(8,128)(2,1)}, bf16[2,2,80,512]{3,2,1,0:T(8,128)(2,1)}) custom-call(s32[4]{0:T(128)S(1)} %get-tuple-element.163.order, bf16[1024,1280]{1,0:T(8,128)(2,1)} %copy-done.2, bf16[1024,512]{1,0:T(8,128)(2,1)} %bitcast.99), custom_call_target="tpu_custom_call" | custom-call | tf_op jit(solution)/shard_map/second_half/product/pallas_call | solution.py:85
  55.9 3.7 %collective-permute-done.9 = bf16[2,2,80,512]{3,2,1,0:T(8,128)(2,1)S(1)} collective-permute-done((bf16[2,2,80,512]{3,2,1,0:T(8,128)(2,1)S(1)}, bf16[2,2,80,512]{3,2,1,0:T(8,128)(2,1)S(1)}, u32[]{:S(2)}, u32[]{:S(2)}) %collective-permute-start.9) | collective-permute-done | bytes 327712 | tf_op jit(solution)/shard_map/first_half/ppermute | solution.py:115
  59.5 1.1 collective-permute-start.10
  62.7 8.4 %old_attention.1 = (f32[2,4,32,128]{3,2,1,0:T(8,128)S(1)}, f32[2,4,32,128]{3,2,1,0:T(8,128)S(1)}, f32[2,4,32,128]{3,2,1,0:T(8,128)S(1)}) custom-call(s32[4]{0:T(128)S(1)} %copy-done, bf16[2,4,32,128]{3,2,1,0:T(8,128)(2,1)S(1)} %bitcast.89, bf16[4,2048,256]{2,1,0:T(8,128)(2,1)} %key_ref.1, bf16[4,2048,256]{2,1,0:T(8,128)(2,1)} %value_ref.1), custom_call_target="tpu_custom_call" | custom-call | tf_op jit(solution)/shard_map/old/old_attention/pallas_call | solution.py:143
  72.1 1.8 %collective-permute-start.12 = (bf16[2,2,80,512]{3,2,1,0:T(8,128)(2,1)S(1)}, bf16[2,2,80,512]{3,2,1,0:T(8,128)(2,1)S(1)}, u32[]{:S(2)}, u32[]{:S(2)}) collective-permute-start(bf16[2,2,80,512]{3,2,1,0:T(8,128)(2,1)S(1)} %fusion.5), channel_id=1, source_target_pairs={{0,12},{12,0},{4,8},{8,4},{1,13},{13,1},{5,9},{9,5},{2,14},{14,2},... | collective-permute-start | bytes 983048 | tf_op jit(solution)/shard_map/second_half/ppermute | solution.py:115
  74.0 5.1 %collective-permute-done.13 = bf16[2,2,80,512]{3,2,1,0:T(8,128)(2,1)S(1)} collective-permute-done((bf16[2,2,80,512]{3,2,1,0:T(8,128)(2,1)S(1)}, bf16[2,2,80,512]{3,2,1,0:T(8,128)(2,1)S(1)}, u32[]{:S(2)}, u32[]{:S(2)}) %collective-permute-start.13) | collective-permute-done | bytes 327712 | tf_op jit(solution)/shard_map/second_half/ppermute | solution.py:115
  79.3 1.1 collective-permute-done.12
  81.8 6.1 %collective-permute-done.14 = bf16[2,2,80,512]{3,2,1,0:T(8,128)(2,1)S(1)} collective-permute-done((bf16[2,2,80,512]{3,2,1,0:T(8,128)(2,1)S(1)}, bf16[2,2,80,512]{3,2,1,0:T(8,128)(2,1)S(1)}, u32[]{:S(2)}, u32[]{:S(2)}) %collective-permute-start.14) | collective-permute-done | bytes 327712 | tf_op jit(solution)/shard_map/second_half/ppermute | solution.py:46
  88.1 21.7 %all_to_all.22.parts_ref = bf16[8,80,512]{2,1,0:T(8,128)(2,1)S(1)} all-to-all(bf16[8,80,512]{2,1,0:T(8,128)(2,1)S(1)} %maximum_select_fusion), channel_id=1, replica_groups=mesh['z'=8,'xl'=2,'y'=4,'xh'=2,'core'=2] {'z'}, dimensions={0} | all-to-all | bytes 1310720 | tf_op jit(solution)/shard_map/reduce_z/all_to_all | solution.py:423
  112.1 13.3 %all-to-all-start.1 = ((f32[256,1,128]{2,1,0:T(1,128)}), f32[256,1,128]{2,1,0:T(1,128)S(1)}, u32[]{:S(2)}, u32[]{:S(2)}) async-start(f32[256,1,128]{2,1,0:T(1,128)} %bitcast.26), calls=%async_computation.1 | async-start | bytes 262144 | tf_op jit(solution)/shard_map/squares/all_to_all | solution.py:438
  126.5 10.3 %all-to-all-done.1 = f32[256,1,128]{2,1,0:T(1,128)S(1)} async-done(((f32[256,1,128]{2,1,0:T(1,128)}), f32[256,1,128]{2,1,0:T(1,128)S(1)}, u32[]{:S(2)}, u32[]{:S(2)}) %all-to-all-start.1) | async-done | bytes 131104 | tf_op jit(solution)/shard_map/squares/all_to_all | solution.py:438
  138.1 2.7 %collective-permute-start.18 = (bf16[80,512]{1,0:T(8,128)(2,1)S(1)}, bf16[80,512]{1,0:T(8,128)(2,1)S(1)}, u32[]{:S(2)}, u32[]{:S(2)}) collective-permute-start(bf16[80,512]{1,0:T(8,128)(2,1)S(1)} %get-tuple-element.132.refs_0_), channel_id=1, source_target_pairs={{0,8},{4,12},{8,0},{12,4},{1,9},{5,13},{9,1},{13,5},{2,10},{6,14},... | collective-permute-start | bytes 245768 | tf_op jit(solution)/shard_map/project/ppermute | solution.py:339
  140.8 1.2 collective-permute-start.19
  142.3 2.7 %collective-permute-done.18.refs_2_ = bf16[80,512]{1,0:T(8,128)(2,1)S(1)} collective-permute-done((bf16[80,512]{1,0:T(8,128)(2,1)S(1)}, bf16[80,512]{1,0:T(8,128)(2,1)S(1)}, u32[]{:S(2)}, u32[]{:S(2)}) %collective-permute-start.18) | collective-permute-done | bytes 81952 | tf_op jit(solution)/shard_map/project/ppermute | solution.py:339
  145.0 1.7 %collective-permute-done.19.refs_3_ = bf16[80,512]{1,0:T(8,128)(2,1)S(1)} collective-permute-done((bf16[80,512]{1,0:T(8,128)(2,1)S(1)}, bf16[80,512]{1,0:T(8,128)(2,1)S(1)}, u32[]{:S(2)}, u32[]{:S(2)}) %collective-permute-start.19) | collective-permute-done | bytes 81952 | tf_op jit(solution)/shard_map/project/ppermute | solution.py:339
  147.7 3.5 %all-to-all-start.2 = ((bf16[16,16,512]{2,1,0:T(8,128)(2,1)}), bf16[16,16,512]{2,1,0:T(8,128)(2,1)S(1)}, u32[]{:S(2)}, u32[]{:S(2)}) async-start(bf16[16,16,512]{2,1,0:T(8,128)(2,1)} %bitcast.40), calls=%async_computation.2 | async-start | bytes 524288 | tf_op jit(solution)/shard_map/project/all_to_all | solution.py:451
  153.1 10.2 %all-to-all-done.2.part_ref = bf16[16,16,512]{2,1,0:T(8,128)(2,1)S(1)} async-done(((bf16[16,16,512]{2,1,0:T(8,128)(2,1)}), bf16[16,16,512]{2,1,0:T(8,128)(2,1)S(1)}, u32[]{:S(2)}, u32[]{:S(2)}) %all-to-all-start.2) | async-done | bytes 262176 | tf_op jit(solution)/shard_map/project/all_to_all | solution.py:451
  163.4 1.9 %fresh_attention.1 = (bf16[4,4,256]{2,1,0:T(4,128)(2,1)}, bf16[4,4,256]{2,1,0:T(4,128)(2,1)}, bf16[4,4,2048]{2,1,0:T(4,128)(2,1)}) custom-call(bf16[16,16,512]{2,1,0:T(8,128)(2,1)S(1)} %all-to-all-done.2.part_ref, bf16[2,128,128]{2,1,0:T(8,128)(2,1)S(1)} %bitcast.90, f32[2,128,128]{2,1,0:T(8,128)S(1)} %bitcast.92, f32[2,128,128]{2,1,0:T(8,128)S(1)} %bitcast.93, ...), custom_call_target="tpu_custom_call" | custom-call | tf_op jit(solution)/shard_map/fresh/fresh_attention/pallas_call | solution.py:220
  (97 shorter events, 17.1 us)
Async XLA Ops:
  0.6 10.7 %copy-start.11 = (bf16[4,4,5120]{2,1,0:T(4,128)(2,1)S(1)}, bf16[4,4,5120]{2,1,0:T(4,128)(2,1)}, u32[]{:S(2)}) copy-start(bf16[4,4,5120]{2,1,0:T(4,128)(2,1)} %param.16) | copy-start | bytes 491524
  0.6 10.7 %collective-permute-start = (bf16[1024,1280]{1,0:T(8,128)(2,1)}, bf16[1024,1280]{1,0:T(8,128)(2,1)S(1)}, u32[]{:S(2)}, u32[]{:S(2)}) collective-permute-start(bf16[1024,1280]{1,0:T(8,128)(2,1)} %left_ref.3), channel_id=1, source_target_pairs={{0,1},{1,0},{2,3},{3,2},{4,5},{5,4},{6,7},{7,6},{8,9},{9,8},{10,11... | collective-permute-start | bytes 7864328 | tf_op jit(solution)/shard_map/exchange/ppermute | solution.py:46
  0.7 37.4 %collective-permute-start.6 = (bf16[1024,2,256]{2,1,0:T(2,128)(2,1)}, bf16[1024,2,256]{2,1,0:T(2,128)(2,1)}, u32[]{:S(2)}, u32[]{:S(2)}) collective-permute-start(bf16[1024,2,256]{2,1,0:T(2,128)(2,1)} %param.12), channel_id=1, source_target_pairs={{0,2},{2,0},{1,3},{3,1},{4,6},{6,4},{5,7},{7,5},{8,10},{10,8},{9,1... | collective-permute-start | bytes 3145736 | tf_op jit(solution)/shard_map/exchange/ppermute | solution.py:46
  11.6 8.8 %collective-permute-start.3 = (bf16[2,2,2,16,320]{4,3,2,1,0:T(8,128)(2,1)S(1)}, bf16[2,2,2,16,320]{4,3,2,1,0:T(8,128)(2,1)S(1)}, u32[]{:S(2)}, u32[]{:S(2)}) collective-permute-start(bf16[2,2,2,16,320]{4,3,2,1,0:T(8,128)(2,1)S(1)} %get-tuple-element.158), channel_id=1, source_target_pairs={{0,32},{32,0},{64,96},{96,64},{128,160},{160,128},{192,224},{224,1... | collective-permute-start | bytes 245768 | tf_op jit(solution)/shard_map/hidden/ppermute | solution.py:346
  13.6 26.9 %collective-permute-start.1 = (bf16[2,2,2,80,512]{4,3,2,1,0:T(8,128)(2,1)}, bf16[2,2,2,80,512]{4,3,2,1,0:T(8,128)(2,1)}, u32[]{:S(2)}, u32[]{:S(2)}) collective-permute-start(bf16[2,2,2,80,512]{4,3,2,1,0:T(8,128)(2,1)} %get-tuple-element.74), channel_id=1, source_target_pairs={{0,4},{4,0},{8,12},{12,8},{1,5},{5,1},{9,13},{13,9},{2,6},{6,2},{1... | collective-permute-start | bytes 1966088 | tf_op jit(solution)/shard_map/first_half/ppermute | solution.py:115
  14.4 26.2 %copy-start.7 = (bf16[2,2,80,512]{3,2,1,0:T(8,128)(2,1)S(1)}, bf16[2,2,80,512]{3,2,1,0:T(8,128)(2,1)}, u32[]{:S(2)}) copy-start(bf16[2,2,80,512]{3,2,1,0:T(8,128)(2,1)} %get-tuple-element.72) | copy-start | bytes 983044
  19.3 21.2 %collective-permute-start.2 = (bf16[2,2,2,80,512]{4,3,2,1,0:T(8,128)(2,1)}, bf16[2,2,2,80,512]{4,3,2,1,0:T(8,128)(2,1)S(1)}, u32[]{:S(2)}, u32[]{:S(2)}) collective-permute-start(bf16[2,2,2,80,512]{4,3,2,1,0:T(8,128)(2,1)} %get-tuple-element.76), channel_id=1, source_target_pairs={{0,12},{12,0},{4,8},{8,4},{1,13},{13,1},{5,9},{9,5},{2,14},{14,2},... | collective-permute-start | bytes 1966088 | tf_op jit(solution)/shard_map/first_half/ppermute | solution.py:115
  20.5 7.6 %collective-permute-start.4 = (bf16[2,2,2,16,320]{4,3,2,1,0:T(8,128)(2,1)S(1)}, bf16[2,2,2,16,320]{4,3,2,1,0:T(8,128)(2,1)S(1)}, u32[]{:S(2)}, u32[]{:S(2)}) collective-permute-start(bf16[2,2,2,16,320]{4,3,2,1,0:T(8,128)(2,1)S(1)} %get-tuple-element.156), channel_id=1, source_target_pairs={{0,64},{32,96},{64,0},{96,32},{128,192},{160,224},{192,128},{224,1... | collective-permute-start | bytes 245768 | tf_op jit(solution)/shard_map/hidden/ppermute | solution.py:346
  28.1 9.9 %collective-permute-start.5 = (bf16[2,2,2,16,320]{4,3,2,1,0:T(8,128)(2,1)S(1)}, bf16[2,2,2,16,320]{4,3,2,1,0:T(8,128)(2,1)S(1)}, u32[]{:S(2)}, u32[]{:S(2)}) collective-permute-start(bf16[2,2,2,16,320]{4,3,2,1,0:T(8,128)(2,1)S(1)} %get-tuple-element.154), channel_id=1, source_target_pairs={{0,128},{32,160},{64,192},{96,224},{128,0},{160,32},{192,64},{224,... | collective-permute-start | bytes 245768 | tf_op jit(solution)/shard_map/hidden/ppermute | solution.py:346
  35.4 11.2 %copy-start.8 = (bf16[2,2,80,512]{3,2,1,0:T(8,128)(2,1)S(1)}, bf16[2,2,80,512]{3,2,1,0:T(8,128)(2,1)}, u32[]{:S(2)}) copy-start(bf16[2,2,80,512]{3,2,1,0:T(8,128)(2,1)} %get-tuple-element.94) | copy-start | bytes 983044
  41.6 19.1 %copy-start.4 = (bf16[2,2,80,512]{3,2,1,0:T(8,128)(2,1)S(1)}, bf16[2,2,80,512]{3,2,1,0:T(8,128)(2,1)}, u32[]{:S(2)}) copy-start(bf16[2,2,80,512]{3,2,1,0:T(8,128)(2,1)} %get-tuple-element.102) | copy-start | bytes 983044
  41.6 19.2 %copy-start.3 = (bf16[2,2,80,512]{3,2,1,0:T(8,128)(2,1)S(1)}, bf16[2,2,80,512]{3,2,1,0:T(8,128)(2,1)}, u32[]{:S(2)}) copy-start(bf16[2,2,80,512]{3,2,1,0:T(8,128)(2,1)} %get-tuple-element.93) | copy-start | bytes 983044
  46.7 16.1 %copy-start = (s32[4]{0:T(128)S(1)}, s32[4]{0:T(128)}, u32[]{:S(2)}) copy-start(s32[4]{0:T(128)} %length_ref.1) | copy-start | bytes 52
  46.7 9.2 %collective-permute-start.8 = (bf16[2,2,80,512]{3,2,1,0:T(8,128)(2,1)S(1)}, bf16[2,2,80,512]{3,2,1,0:T(8,128)(2,1)S(1)}, u32[]{:S(2)}, u32[]{:S(2)}) collective-permute-start(bf16[2,2,80,512]{3,2,1,0:T(8,128)(2,1)S(1)} %fusion.11), channel_id=1, source_target_pairs={{0,12},{12,0},{4,8},{8,4},{1,13},{13,1},{5,9},{9,5},{2,14},{14,2},... | collective-permute-start | bytes 983048 | tf_op jit(solution)/shard_map/first_half/ppermute | solution.py:115
  48.9 10.6 %collective-permute-start.9 = (bf16[2,2,80,512]{3,2,1,0:T(8,128)(2,1)S(1)}, bf16[2,2,80,512]{3,2,1,0:T(8,128)(2,1)S(1)}, u32[]{:S(2)}, u32[]{:S(2)}) collective-permute-start(bf16[2,2,80,512]{3,2,1,0:T(8,128)(2,1)S(1)} %fusion.8), channel_id=1, source_target_pairs={{0,4},{4,0},{8,12},{12,8},{1,5},{5,1},{9,13},{13,9},{2,6},{6,2},{1... | collective-permute-start | bytes 983048 | tf_op jit(solution)/shard_map/first_half/ppermute | solution.py:115
  48.9 22.3 %collective-permute-start.7 = (bf16[2,2,2,80,512]{4,3,2,1,0:T(8,128)(2,1)}, bf16[2,2,2,80,512]{4,3,2,1,0:T(8,128)(2,1)S(1)}, u32[]{:S(2)}, u32[]{:S(2)}) collective-permute-start(bf16[2,2,2,80,512]{4,3,2,1,0:T(8,128)(2,1)} %get-tuple-element.92), channel_id=1, source_target_pairs={{0,4},{4,0},{8,12},{12,8},{1,5},{5,1},{9,13},{13,9},{2,6},{6,2},{1... | collective-permute-start | bytes 1966088 | tf_op jit(solution)/shard_map/second_half/ppermute | solution.py:115
  59.5 12.2 %collective-permute-start.10 = (bf16[2,2,2,80,512]{4,3,2,1,0:T(8,128)(2,1)}, bf16[2,2,2,80,512]{4,3,2,1,0:T(8,128)(2,1)S(1)}, u32[]{:S(2)}, u32[]{:S(2)}) collective-permute-start(bf16[2,2,2,80,512]{4,3,2,1,0:T(8,128)(2,1)} %get-tuple-element.111), channel_id=1, source_target_pairs={{0,12},{12,0},{4,8},{8,4},{1,13},{13,1},{5,9},{9,5},{2,14},{14,2},... | collective-permute-start | bytes 1966088 | tf_op jit(solution)/shard_map/second_half/ppermute | solution.py:115
  62.0 9.7 %copy-start.10 = (bf16[2,2,80,512]{3,2,1,0:T(8,128)(2,1)S(1)}, bf16[2,2,80,512]{3,2,1,0:T(8,128)(2,1)}, u32[]{:S(2)}) copy-start(bf16[2,2,80,512]{3,2,1,0:T(8,128)(2,1)} %get-tuple-element.110) | copy-start | bytes 983044
  62.1 17.1 %copy-start.6 = (bf16[2,2,80,512]{3,2,1,0:T(8,128)(2,1)S(1)}, bf16[2,2,80,512]{3,2,1,0:T(8,128)(2,1)}, u32[]{:S(2)}) copy-start(bf16[2,2,80,512]{3,2,1,0:T(8,128)(2,1)} %get-tuple-element.118) | copy-start | bytes 983044
  62.1 9.8 %collective-permute-start.11 = (bf16[2,2,80,512]{3,2,1,0:T(8,128)(2,1)S(1)}, bf16[2,2,80,512]{3,2,1,0:T(8,128)(2,1)S(1)}, u32[]{:S(2)}, u32[]{:S(2)}) collective-permute-start(bf16[2,2,80,512]{3,2,1,0:T(8,128)(2,1)S(1)} %pad_maximum_fusion.1), channel_id=1, source_target_pairs={{0,16},{16,0},{1,17},{17,1},{2,18},{18,2},{3,19},{19,3},{4,20},{20... | collective-permute-start | bytes 983048 | tf_op jit(solution)/shard_map/first_half/ppermute | solution.py:46
  71.2 9.3 %copy-start.5 = (bf16[2,2,80,512]{3,2,1,0:T(8,128)(2,1)S(1)}, bf16[2,2,80,512]{3,2,1,0:T(8,128)(2,1)}, u32[]{:S(2)}) copy-start(bf16[2,2,80,512]{3,2,1,0:T(8,128)(2,1)} %get-tuple-element.116) | copy-start | bytes 983044
  71.8 7.3 %collective-permute-start.13 = (bf16[2,2,80,512]{3,2,1,0:T(8,128)(2,1)S(1)}, bf16[2,2,80,512]{3,2,1,0:T(8,128)(2,1)S(1)}, u32[]{:S(2)}, u32[]{:S(2)}) collective-permute-start(bf16[2,2,80,512]{3,2,1,0:T(8,128)(2,1)S(1)} %fusion.4), channel_id=1, source_target_pairs={{0,4},{4,0},{8,12},{12,8},{1,5},{5,1},{9,13},{13,9},{2,6},{6,2},{1... | collective-permute-start | bytes 983048 | tf_op jit(solution)/shard_map/second_half/ppermute | solution.py:115
  72.1 8.4 %collective-permute-start.12 = (bf16[2,2,80,512]{3,2,1,0:T(8,128)(2,1)S(1)}, bf16[2,2,80,512]{3,2,1,0:T(8,128)(2,1)S(1)}, u32[]{:S(2)}, u32[]{:S(2)}) collective-permute-start(bf16[2,2,80,512]{3,2,1,0:T(8,128)(2,1)S(1)} %fusion.5), channel_id=1, source_target_pairs={{0,12},{12,0},{4,8},{8,4},{1,13},{13,1},{5,9},{9,5},{2,14},{14,2},... | collective-permute-start | bytes 983048 | tf_op jit(solution)/shard_map/second_half/ppermute | solution.py:115
  80.7 7.2 %collective-permute-start.14 = (bf16[2,2,80,512]{3,2,1,0:T(8,128)(2,1)S(1)}, bf16[2,2,80,512]{3,2,1,0:T(8,128)(2,1)S(1)}, u32[]{:S(2)}, u32[]{:S(2)}) collective-permute-start(bf16[2,2,80,512]{3,2,1,0:T(8,128)(2,1)S(1)} %pad_maximum_fusion.2), channel_id=1, source_target_pairs={{0,16},{16,0},{1,17},{17,1},{2,18},{18,2},{3,19},{19,3},{4,20},{20... | collective-permute-start | bytes 983048 | tf_op jit(solution)/shard_map/second_half/ppermute | solution.py:46
  109.8 53.6 %copy-start.1 = (f32[128]{0:T(128)S(1)}, f32[128]{0:T(128)}, u32[]{:S(2)}) copy-start(f32[128]{0:T(128)} %param.21) | copy-start | bytes 1540
  110.8 14.7 %collective-permute-start.16 = (bf16[2,2,2,16,320]{4,3,2,1,0:T(8,128)(2,1)S(1)}, bf16[2,2,2,16,320]{4,3,2,1,0:T(8,128)(2,1)S(1)}, u32[]{:S(2)}, u32[]{:S(2)}) collective-permute-start(bf16[2,2,2,16,320]{4,3,2,1,0:T(8,128)(2,1)S(1)} %get-tuple-element.152), channel_id=1, source_target_pairs={{0,16},{16,0},{1,17},{17,1},{2,18},{18,2},{3,19},{19,3},{4,20},{20... | collective-permute-start | bytes 245768 | tf_op jit(solution)/shard_map/hidden/ppermute | solution.py:346
  111.4 15.1 %collective-permute-start.15 = (f32[80,512]{1,0:T(8,128)S(1)}, f32[80,512]{1,0:T(8,128)S(1)}, u32[]{:S(2)}, u32[]{:S(2)}) collective-permute-start(f32[80,512]{1,0:T(8,128)S(1)} %get-tuple-element.123), channel_id=1, source_target_pairs={{2,128},{34,160},{66,192},{98,224},{128,2},{160,34},{192,66},{224,... | collective-permute-start | bytes 491528 | tf_op jit(solution)/shard_map/place/ppermute | solution.py:441
  112.1 24.8 %all-to-all-start.1 = ((f32[256,1,128]{2,1,0:T(1,128)}), f32[256,1,128]{2,1,0:T(1,128)S(1)}, u32[]{:S(2)}, u32[]{:S(2)}) async-start(f32[256,1,128]{2,1,0:T(1,128)} %bitcast.26), calls=%async_computation.1 | async-start | bytes 262144 | tf_op jit(solution)/shard_map/squares/all_to_all | solution.py:438
  137.2 5.1 %collective-permute-start.17 = (bf16[80,512]{1,0:T(8,128)(2,1)S(1)}, bf16[80,512]{1,0:T(8,128)(2,1)S(1)}, u32[]{:S(2)}, u32[]{:S(2)}) collective-permute-start(bf16[80,512]{1,0:T(8,128)(2,1)S(1)} %get-tuple-element.132.refs_0_), channel_id=1, source_target_pairs={{0,4},{4,0},{8,12},{12,8},{1,5},{5,1},{9,13},{13,9},{2,6},{6,2},{1... | collective-permute-start | bytes 245768 | tf_op jit(solution)/shard_map/project/ppermute | solution.py:339
  138.1 6.9 %collective-permute-start.18 = (bf16[80,512]{1,0:T(8,128)(2,1)S(1)}, bf16[80,512]{1,0:T(8,128)(2,1)S(1)}, u32[]{:S(2)}, u32[]{:S(2)}) collective-permute-start(bf16[80,512]{1,0:T(8,128)(2,1)S(1)} %get-tuple-element.132.refs_0_), channel_id=1, source_target_pairs={{0,8},{4,12},{8,0},{12,4},{1,9},{5,13},{9,1},{13,5},{2,10},{6,14},... | collective-permute-start | bytes 245768 | tf_op jit(solution)/shard_map/project/ppermute | solution.py:339
  140.8 5.9 %collective-permute-start.19 = (bf16[80,512]{1,0:T(8,128)(2,1)S(1)}, bf16[80,512]{1,0:T(8,128)(2,1)S(1)}, u32[]{:S(2)}, u32[]{:S(2)}) collective-permute-start(bf16[80,512]{1,0:T(8,128)(2,1)S(1)} %get-tuple-element.132.refs_0_), channel_id=1, source_target_pairs={{0,12},{4,8},{8,4},{12,0},{1,13},{5,9},{9,5},{13,1},{2,14},{6,10},... | collective-permute-start | bytes 245768 | tf_op jit(solution)/shard_map/project/ppermute | solution.py:339
  147.7 15.7 %all-to-all-start.2 = ((bf16[16,16,512]{2,1,0:T(8,128)(2,1)}), bf16[16,16,512]{2,1,0:T(8,128)(2,1)S(1)}, u32[]{:S(2)}, u32[]{:S(2)}) async-start(bf16[16,16,512]{2,1,0:T(8,128)(2,1)} %bitcast.40), calls=%async_computation.2 | async-start | bytes 524288 | tf_op jit(solution)/shard_map/project/all_to_all | solution.py:451
  (2 other events, 12.2 us)

commit v5 on v4

--- a/solution.py
+++ b/solution.py
@@ -101,7 +101,7 @@
         ),
         compiler_params=pltpu.CompilerParams(vmem_limit_bytes=24 * 1024 * 1024),
         name="product",
-    )(order, in_hbm(left), in_hbm(right))
+    )(order, in_hbm(left), right)
 
 
 def add(*values):

time: 166 us -> 165 us (level)
  other arithmetic: 5.31 us -> 8.85 us
  local copies, waits for them, and re-layouts: 8.71 us -> 5.56 us
    convert_element_type x10, other arithmetic: 2.95 us -> 6.48 us  [add(): return total.astype(BF16)]
    unnamed x27 -> x23, local copies, waits for them, and re-layouts: 4.94 us -> 1.79 us
  transfers between devices with their start and end apart: 22 -> 22, of which waited for: 12 -> 12; matrix products, arithmetic and copies ran while one was open for 7% -> 6% of each run, Pallas kernels for 14% -> 14%
where the time goes in v5:
time: 165 us; the launch traced here: 164 us
  starting transfers between devices  49.6 us (30%)
  waiting for transfers between devices  46.8 us (28%)
  Pallas kernels  31.2 us (19%)
  blocking collectives  21.3 us (13%)
  other arithmetic  8.85 us (5%)
  local copies, waits for them, and re-layouts  5.56 us (3%)
    all_to_all x1, blocking collectives, local(): parts = lax.all_to_all(parts, 'z', 0, 0)  21.3 us
    pallas_call x4, Pallas kernels, product(): pl.pallas_call(product_kernel, out_shape=(pltpu.HBM((2, 2, 2, rows, colum...  18.6 us
    ppermute x4, starting transfers between devices, trade(): got = lax.ppermute(sent, mesh_axis, partners)  12.9 us
    all_to_all x1, starting transfers between devices, local(): squares = lax.all_to_all(squares, EVERY, 0, 0, tiled=True)  12.7 us
    all_to_all x1, waiting for transfers between devices, local(): squares = lax.all_to_all(squares, EVERY, 0, 0, tiled=True)  10.3 us
    all_to_all x1, waiting for transfers between devices, local(): lax.all_to_all(partial.reshape(16, states, columns), ('z', 'xl'), 0, 0)  10.2 us
    ppermute x8, waiting for transfers between devices, along_y(): return lax.ppermute(values, 'y', PAIRING[pairing])  10.1 us
    ppermute x8, starting transfers between devices, along_y(): return lax.ppermute(values, 'y', PAIRING[pairing])  9.6 us
  transfers between devices with their start and end apart: 22, of which 12 were waited for; matrix products, arithmetic and copies ran while one was open for 6% of the time, Pallas kernels for 14%

profile of v5, /device:TPU:24, one launch (start us, length us, event | category | flops | bytes accessed | tf_op | source)
XLA Modules:
  0.0 164.4 jit_solution(9733162795376368554)
XLA Ops:
  0.7 3.1 %collective-permute-start.6 = (bf16[1024,2,256]{2,1,0:T(2,128)(2,1)}, bf16[1024,2,256]{2,1,0:T(2,128)(2,1)S(1)}, u32[]{:S(2)}, u32[]{:S(2)}) collective-permute-start(bf16[1024,2,256]{2,1,0:T(2,128)(2,1)} %param.12), channel_id=1, source_target_pairs={{0,2},{2,0},{1,3},{3,1},{4,6},{6,4},{5,7},{7,5},{8,10},{10,8},{9,1... | collective-permute-start | bytes 3145736 | tf_op jit(solution)/shard_map/exchange/ppermute | solution.py:46
  3.9 1.5 copy.59
  5.4 4.7 %product.4 = (bf16[2,2,2,80,512]{4,3,2,1,0:T(8,128)(2,1)}, bf16[2,2,80,512]{3,2,1,0:T(8,128)(2,1)}, bf16[2,2,80,512]{3,2,1,0:T(8,128)(2,1)}) custom-call(s32[4]{0:T(128)S(1)} %get-tuple-element.162.order, bf16[1024,1280]{1,0:T(8,128)(2,1)} %left_ref.3, bf16[1024,512]{1,0:T(8,128)(2,1)S(1)} %bitcast.88), custom_call_target="tpu_custom_call" | custom-call | tf_op jit(solution)/shard_map/first_half/product/pallas_call | solution.py:85
  10.4 2.0 %collective-permute-start.3 = (bf16[2,2,2,16,320]{4,3,2,1,0:T(8,128)(2,1)S(1)}, bf16[2,2,2,16,320]{4,3,2,1,0:T(8,128)(2,1)S(1)}, u32[]{:S(2)}, u32[]{:S(2)}) collective-permute-start(bf16[2,2,2,16,320]{4,3,2,1,0:T(8,128)(2,1)S(1)} %get-tuple-element.158), channel_id=1, source_target_pairs={{0,32},{32,0},{64,96},{96,64},{128,160},{160,128},{192,224},{224,1... | collective-permute-start | bytes 245768 | tf_op jit(solution)/shard_map/hidden/ppermute | solution.py:346
  13.1 4.7 %product.5 = (bf16[2,2,2,80,512]{4,3,2,1,0:T(8,128)(2,1)}, bf16[2,2,80,512]{3,2,1,0:T(8,128)(2,1)}, bf16[2,2,80,512]{3,2,1,0:T(8,128)(2,1)}) custom-call(s32[4]{0:T(128)S(1)} %get-tuple-element.163.order, bf16[1024,1280]{1,0:T(8,128)(2,1)} %collective-permute-done.left_ref, bf16[1024,512]{1,0:T(8,128)(2,1)S(1)} %bitcast.89), custom_call_target="tpu_custom_call" | custom-call | tf_op jit(solution)/shard_map/first_half/product/pallas_call | solution.py:85
  18.9 3.4 %collective-permute-start.4 = (bf16[2,2,2,16,320]{4,3,2,1,0:T(8,128)(2,1)S(1)}, bf16[2,2,2,16,320]{4,3,2,1,0:T(8,128)(2,1)S(1)}, u32[]{:S(2)}, u32[]{:S(2)}) collective-permute-start(bf16[2,2,2,16,320]{4,3,2,1,0:T(8,128)(2,1)S(1)} %get-tuple-element.156), channel_id=1, source_target_pairs={{0,64},{32,96},{64,0},{96,32},{128,192},{160,224},{192,128},{224,1... | collective-permute-start | bytes 245768 | tf_op jit(solution)/shard_map/hidden/ppermute | solution.py:346
  23.2 3.3 %collective-permute-done.4 = bf16[2,2,2,16,320]{4,3,2,1,0:T(8,128)(2,1)S(1)} collective-permute-done((bf16[2,2,2,16,320]{4,3,2,1,0:T(8,128)(2,1)S(1)}, bf16[2,2,2,16,320]{4,3,2,1,0:T(8,128)(2,1)S(1)}, u32[]{:S(2)}, u32[]{:S(2)}) %collective-permute-start.4) | collective-permute-done | bytes 81952 | tf_op jit(solution)/shard_map/hidden/ppermute | solution.py:346
  26.6 6.0 %collective-permute-start.5 = (bf16[2,2,2,16,320]{4,3,2,1,0:T(8,128)(2,1)S(1)}, bf16[2,2,2,16,320]{4,3,2,1,0:T(8,128)(2,1)S(1)}, u32[]{:S(2)}, u32[]{:S(2)}) collective-permute-start(bf16[2,2,2,16,320]{4,3,2,1,0:T(8,128)(2,1)S(1)} %get-tuple-element.154), channel_id=1, source_target_pairs={{0,128},{32,160},{64,192},{96,224},{128,0},{160,32},{192,64},{224,... | collective-permute-start | bytes 245768 | tf_op jit(solution)/shard_map/hidden/ppermute | solution.py:346
  32.6 1.3 pad_maximum_fusion
  33.9 2.6 %collective-permute-done.5 = bf16[2,2,2,16,320]{4,3,2,1,0:T(8,128)(2,1)S(1)} collective-permute-done((bf16[2,2,2,16,320]{4,3,2,1,0:T(8,128)(2,1)S(1)}, bf16[2,2,2,16,320]{4,3,2,1,0:T(8,128)(2,1)S(1)}, u32[]{:S(2)}, u32[]{:S(2)}) %collective-permute-start.5) | collective-permute-done | bytes 81952 | tf_op jit(solution)/shard_map/hidden/ppermute | solution.py:346
  36.8 1.8 %fusion.11 = bf16[2,2,80,512]{3,2,1,0:T(8,128)(2,1)} fusion(bf16[2,2,80,512]{3,2,1,0:T(8,128)(2,1)} %get-tuple-element.72, bf16[2,2,2,80,512]{4,3,2,1,0:T(8,128)(2,1)S(1)} %collective-permute-done.1), kind=kLoop, calls=%fused_computation.20 | loop fusion | flops 655360 | bytes 983040 | tf_op jit(solution)/shard_map/first_half/convert_element_type | solution.py:111
  38.6 4.6 %product.6 = (bf16[2,2,2,80,512]{4,3,2,1,0:T(8,128)(2,1)}, bf16[2,2,80,512]{3,2,1,0:T(8,128)(2,1)}, bf16[2,2,80,512]{3,2,1,0:T(8,128)(2,1)}) custom-call(s32[4]{0:T(128)S(1)} %get-tuple-element.162.order, bf16[1024,1280]{1,0:T(8,128)(2,1)} %left_ref.3, bf16[1024,512]{1,0:T(8,128)(2,1)S(1)} %bitcast.90), custom_call_target="tpu_custom_call" | custom-call | tf_op jit(solution)/shard_map/second_half/product/pallas_call | solution.py:85
  43.3 1.8 %fusion.8 = bf16[2,2,80,512]{3,2,1,0:T(8,128)(2,1)} fusion(bf16[2,2,80,512]{3,2,1,0:T(8,128)(2,1)S(1)} %copy-done.6, bf16[2,2,2,80,512]{4,3,2,1,0:T(8,128)(2,1)} %collective-permute-done.2), kind=kLoop, calls=%fused_computation.15 | loop fusion | flops 655360 | bytes 983040 | tf_op jit(solution)/shard_map/first_half/convert_element_type | solution.py:111
  45.1 2.2 %collective-permute-start.8 = (bf16[2,2,80,512]{3,2,1,0:T(8,128)(2,1)}, bf16[2,2,80,512]{3,2,1,0:T(8,128)(2,1)}, u32[]{:S(2)}, u32[]{:S(2)}) collective-permute-start(bf16[2,2,80,512]{3,2,1,0:T(8,128)(2,1)} %fusion.11), channel_id=1, source_target_pairs={{0,12},{12,0},{4,8},{8,4},{1,13},{13,1},{5,9},{9,5},{2,14},{14,2},... | collective-permute-start | bytes 983048 | tf_op jit(solution)/shard_map/first_half/ppermute | solution.py:115
  47.3 2.0 %collective-permute-start.7 = (bf16[2,2,2,80,512]{4,3,2,1,0:T(8,128)(2,1)}, bf16[2,2,2,80,512]{4,3,2,1,0:T(8,128)(2,1)S(1)}, u32[]{:S(2)}, u32[]{:S(2)}) collective-permute-start(bf16[2,2,2,80,512]{4,3,2,1,0:T(8,128)(2,1)} %get-tuple-element.92), channel_id=1, source_target_pairs={{0,4},{4,0},{8,12},{12,8},{1,5},{5,1},{9,13},{13,9},{2,6},{6,2},{1... | collective-permute-start | bytes 1966088 | tf_op jit(solution)/shard_map/second_half/ppermute | solution.py:115
  49.3 4.7 %product.7 = (bf16[2,2,2,80,512]{4,3,2,1,0:T(8,128)(2,1)}, bf16[2,2,80,512]{3,2,1,0:T(8,128)(2,1)}, bf16[2,2,80,512]{3,2,1,0:T(8,128)(2,1)}) custom-call(s32[4]{0:T(128)S(1)} %get-tuple-element.163.order, bf16[1024,1280]{1,0:T(8,128)(2,1)} %collective-permute-done.left_ref, bf16[1024,512]{1,0:T(8,128)(2,1)S(1)} %bitcast.91), custom_call_target="tpu_custom_call" | custom-call | tf_op jit(solution)/shard_map/second_half/product/pallas_call | solution.py:85
  54.4 3.8 %collective-permute-done.9 = bf16[2,2,80,512]{3,2,1,0:T(8,128)(2,1)} collective-permute-done((bf16[2,2,80,512]{3,2,1,0:T(8,128)(2,1)}, bf16[2,2,80,512]{3,2,1,0:T(8,128)(2,1)}, u32[]{:S(2)}, u32[]{:S(2)}) %collective-permute-start.9) | collective-permute-done | bytes 327712 | tf_op jit(solution)/shard_map/first_half/ppermute | solution.py:115
  62.4 8.4 %old_attention.1 = (f32[2,4,32,128]{3,2,1,0:T(8,128)S(1)}, f32[2,4,32,128]{3,2,1,0:T(8,128)S(1)}, f32[2,4,32,128]{3,2,1,0:T(8,128)S(1)}) custom-call(s32[4]{0:T(128)S(1)} %copy-done, bf16[2,4,32,128]{3,2,1,0:T(8,128)(2,1)S(1)} %bitcast.93, bf16[4,2048,256]{2,1,0:T(8,128)(2,1)} %key_ref.1, bf16[4,2048,256]{2,1,0:T(8,128)(2,1)} %value_ref.1), custom_call_target="tpu_custom_call" | custom-call | tf_op jit(solution)/shard_map/old/old_attention/pallas_call | solution.py:143
  71.4 2.3 %collective-permute-start.12 = (bf16[2,2,80,512]{3,2,1,0:T(8,128)(2,1)S(1)}, bf16[2,2,80,512]{3,2,1,0:T(8,128)(2,1)S(1)}, u32[]{:S(2)}, u32[]{:S(2)}) collective-permute-start(bf16[2,2,80,512]{3,2,1,0:T(8,128)(2,1)S(1)} %fusion.5), channel_id=1, source_target_pairs={{0,12},{12,0},{4,8},{8,4},{1,13},{13,1},{5,9},{9,5},{2,14},{14,2},... | collective-permute-start | bytes 983048 | tf_op jit(solution)/shard_map/second_half/ppermute | solution.py:115
  73.8 4.6 %collective-permute-done.13 = bf16[2,2,80,512]{3,2,1,0:T(8,128)(2,1)S(1)} collective-permute-done((bf16[2,2,80,512]{3,2,1,0:T(8,128)(2,1)S(1)}, bf16[2,2,80,512]{3,2,1,0:T(8,128)(2,1)S(1)}, u32[]{:S(2)}, u32[]{:S(2)}) %collective-permute-start.13) | collective-permute-done | bytes 327712 | tf_op jit(solution)/shard_map/second_half/ppermute | solution.py:115
  80.0 1.5 collective-permute-start.14
  81.5 5.6 %collective-permute-done.14 = bf16[2,2,80,512]{3,2,1,0:T(8,128)(2,1)S(1)} collective-permute-done((bf16[2,2,80,512]{3,2,1,0:T(8,128)(2,1)S(1)}, bf16[2,2,80,512]{3,2,1,0:T(8,128)(2,1)S(1)}, u32[]{:S(2)}, u32[]{:S(2)}) %collective-permute-start.14) | collective-permute-done | bytes 327712 | tf_op jit(solution)/shard_map/second_half/ppermute | solution.py:46
  87.4 21.3 %all_to_all.22.parts_ref = bf16[8,80,512]{2,1,0:T(8,128)(2,1)S(1)} all-to-all(bf16[8,80,512]{2,1,0:T(8,128)(2,1)S(1)} %maximum_select_fusion), channel_id=1, replica_groups=mesh['z'=8,'xl'=2,'y'=4,'xh'=2,'core'=2] {'z'}, dimensions={0} | all-to-all | bytes 1310720 | tf_op jit(solution)/shard_map/reduce_z/all_to_all | solution.py:423
  109.7 1.6 collective-permute-start.16
  111.9 12.7 %all-to-all-start.1 = ((f32[256,1,128]{2,1,0:T(1,128)}), f32[256,1,128]{2,1,0:T(1,128)S(1)}, u32[]{:S(2)}, u32[]{:S(2)}) async-start(f32[256,1,128]{2,1,0:T(1,128)} %bitcast.26), calls=%async_computation.1 | async-start | bytes 262144 | tf_op jit(solution)/shard_map/squares/all_to_all | solution.py:438
  125.7 10.3 %all-to-all-done.1 = f32[256,1,128]{2,1,0:T(1,128)S(1)} async-done(((f32[256,1,128]{2,1,0:T(1,128)}), f32[256,1,128]{2,1,0:T(1,128)S(1)}, u32[]{:S(2)}, u32[]{:S(2)}) %all-to-all-start.1) | async-done | bytes 131104 | tf_op jit(solution)/shard_map/squares/all_to_all | solution.py:438
  137.3 2.7 %collective-permute-start.18 = (bf16[80,512]{1,0:T(8,128)(2,1)S(1)}, bf16[80,512]{1,0:T(8,128)(2,1)S(1)}, u32[]{:S(2)}, u32[]{:S(2)}) collective-permute-start(bf16[80,512]{1,0:T(8,128)(2,1)S(1)} %get-tuple-element.132.refs_0_), channel_id=1, source_target_pairs={{0,8},{4,12},{8,0},{12,4},{1,9},{5,13},{9,1},{13,5},{2,10},{6,14},... | collective-permute-start | bytes 245768 | tf_op jit(solution)/shard_map/project/ppermute | solution.py:339
  141.5 2.7 %collective-permute-done.18.refs_2_ = bf16[80,512]{1,0:T(8,128)(2,1)S(1)} collective-permute-done((bf16[80,512]{1,0:T(8,128)(2,1)S(1)}, bf16[80,512]{1,0:T(8,128)(2,1)S(1)}, u32[]{:S(2)}, u32[]{:S(2)}) %collective-permute-start.18) | collective-permute-done | bytes 81952 | tf_op jit(solution)/shard_map/project/ppermute | solution.py:339
  144.2 1.7 %collective-permute-done.19.refs_3_ = bf16[80,512]{1,0:T(8,128)(2,1)S(1)} collective-permute-done((bf16[80,512]{1,0:T(8,128)(2,1)S(1)}, bf16[80,512]{1,0:T(8,128)(2,1)S(1)}, u32[]{:S(2)}, u32[]{:S(2)}) %collective-permute-start.19) | collective-permute-done | bytes 81952 | tf_op jit(solution)/shard_map/project/ppermute | solution.py:339
  146.9 3.5 %all-to-all-start.2 = ((bf16[16,16,512]{2,1,0:T(8,128)(2,1)}), bf16[16,16,512]{2,1,0:T(8,128)(2,1)S(1)}, u32[]{:S(2)}, u32[]{:S(2)}) async-start(bf16[16,16,512]{2,1,0:T(8,128)(2,1)} %bitcast.40), calls=%async_computation.2 | async-start | bytes 524288 | tf_op jit(solution)/shard_map/project/all_to_all | solution.py:451
  152.3 10.2 %all-to-all-done.2.part_ref = bf16[16,16,512]{2,1,0:T(8,128)(2,1)S(1)} async-done(((bf16[16,16,512]{2,1,0:T(8,128)(2,1)}), bf16[16,16,512]{2,1,0:T(8,128)(2,1)S(1)}, u32[]{:S(2)}, u32[]{:S(2)}) %all-to-all-start.2) | async-done | bytes 262176 | tf_op jit(solution)/shard_map/project/all_to_all | solution.py:451
  162.5 1.9 %fresh_attention.1 = (bf16[4,4,256]{2,1,0:T(4,128)(2,1)}, bf16[4,4,256]{2,1,0:T(4,128)(2,1)}, bf16[4,4,2048]{2,1,0:T(4,128)(2,1)}) custom-call(bf16[16,16,512]{2,1,0:T(8,128)(2,1)S(1)} %all-to-all-done.2.part_ref, bf16[2,128,128]{2,1,0:T(8,128)(2,1)S(1)} %bitcast.94, f32[2,128,128]{2,1,0:T(8,128)S(1)} %bitcast.96, f32[2,128,128]{2,1,0:T(8,128)S(1)} %bitcast.97, ...), custom_call_target="tpu_custom_call" | custom-call | tf_op jit(solution)/shard_map/fresh/fresh_attention/pallas_call | solution.py:220
  (93 shorter events, 19.0 us)
Async XLA Ops:
  0.6 9.5 %copy-start.9 = (bf16[4,4,5120]{2,1,0:T(4,128)(2,1)S(1)}, bf16[4,4,5120]{2,1,0:T(4,128)(2,1)}, u32[]{:S(2)}) copy-start(bf16[4,4,5120]{2,1,0:T(4,128)(2,1)} %param.16) | copy-start | bytes 491524
  0.6 9.4 %collective-permute-start = (bf16[1024,1280]{1,0:T(8,128)(2,1)}, bf16[1024,1280]{1,0:T(8,128)(2,1)}, u32[]{:S(2)}, u32[]{:S(2)}) collective-permute-start(bf16[1024,1280]{1,0:T(8,128)(2,1)} %left_ref.3), channel_id=1, source_target_pairs={{0,1},{1,0},{2,3},{3,2},{4,5},{5,4},{6,7},{7,6},{8,9},{9,8},{10,11... | collective-permute-start | bytes 7864328 | tf_op jit(solution)/shard_map/exchange/ppermute | solution.py:46
  0.7 35.8 %collective-permute-start.6 = (bf16[1024,2,256]{2,1,0:T(2,128)(2,1)}, bf16[1024,2,256]{2,1,0:T(2,128)(2,1)S(1)}, u32[]{:S(2)}, u32[]{:S(2)}) collective-permute-start(bf16[1024,2,256]{2,1,0:T(2,128)(2,1)} %param.12), channel_id=1, source_target_pairs={{0,2},{2,0},{1,3},{3,1},{4,6},{6,4},{5,7},{7,5},{8,10},{10,8},{9,1... | collective-permute-start | bytes 3145736 | tf_op jit(solution)/shard_map/exchange/ppermute | solution.py:46
  10.4 8.5 %collective-permute-start.3 = (bf16[2,2,2,16,320]{4,3,2,1,0:T(8,128)(2,1)S(1)}, bf16[2,2,2,16,320]{4,3,2,1,0:T(8,128)(2,1)S(1)}, u32[]{:S(2)}, u32[]{:S(2)}) collective-permute-start(bf16[2,2,2,16,320]{4,3,2,1,0:T(8,128)(2,1)S(1)} %get-tuple-element.158), channel_id=1, source_target_pairs={{0,32},{32,0},{64,96},{96,64},{128,160},{160,128},{192,224},{224,1... | collective-permute-start | bytes 245768 | tf_op jit(solution)/shard_map/hidden/ppermute | solution.py:346
  12.4 24.4 %collective-permute-start.1 = (bf16[2,2,2,80,512]{4,3,2,1,0:T(8,128)(2,1)}, bf16[2,2,2,80,512]{4,3,2,1,0:T(8,128)(2,1)S(1)}, u32[]{:S(2)}, u32[]{:S(2)}) collective-permute-start(bf16[2,2,2,80,512]{4,3,2,1,0:T(8,128)(2,1)} %get-tuple-element.74), channel_id=1, source_target_pairs={{0,4},{4,0},{8,12},{12,8},{1,5},{5,1},{9,13},{13,9},{2,6},{6,2},{1... | collective-permute-start | bytes 1966088 | tf_op jit(solution)/shard_map/first_half/ppermute | solution.py:115
  17.8 19.1 %collective-permute-start.2 = (bf16[2,2,2,80,512]{4,3,2,1,0:T(8,128)(2,1)}, bf16[2,2,2,80,512]{4,3,2,1,0:T(8,128)(2,1)}, u32[]{:S(2)}, u32[]{:S(2)}) collective-permute-start(bf16[2,2,2,80,512]{4,3,2,1,0:T(8,128)(2,1)} %get-tuple-element.76), channel_id=1, source_target_pairs={{0,12},{12,0},{4,8},{8,4},{1,13},{13,1},{5,9},{9,5},{2,14},{14,2},... | collective-permute-start | bytes 1966088 | tf_op jit(solution)/shard_map/first_half/ppermute | solution.py:115
  18.9 7.6 %collective-permute-start.4 = (bf16[2,2,2,16,320]{4,3,2,1,0:T(8,128)(2,1)S(1)}, bf16[2,2,2,16,320]{4,3,2,1,0:T(8,128)(2,1)S(1)}, u32[]{:S(2)}, u32[]{:S(2)}) collective-permute-start(bf16[2,2,2,16,320]{4,3,2,1,0:T(8,128)(2,1)S(1)} %get-tuple-element.156), channel_id=1, source_target_pairs={{0,64},{32,96},{64,0},{96,32},{128,192},{160,224},{192,128},{224,1... | collective-permute-start | bytes 245768 | tf_op jit(solution)/shard_map/hidden/ppermute | solution.py:346
  26.6 9.9 %collective-permute-start.5 = (bf16[2,2,2,16,320]{4,3,2,1,0:T(8,128)(2,1)S(1)}, bf16[2,2,2,16,320]{4,3,2,1,0:T(8,128)(2,1)S(1)}, u32[]{:S(2)}, u32[]{:S(2)}) collective-permute-start(bf16[2,2,2,16,320]{4,3,2,1,0:T(8,128)(2,1)S(1)} %get-tuple-element.154), channel_id=1, source_target_pairs={{0,128},{32,160},{64,192},{96,224},{128,0},{160,32},{192,64},{224,... | collective-permute-start | bytes 245768 | tf_op jit(solution)/shard_map/hidden/ppermute | solution.py:346
  33.9 9.4 %copy-start.6 = (bf16[2,2,80,512]{3,2,1,0:T(8,128)(2,1)S(1)}, bf16[2,2,80,512]{3,2,1,0:T(8,128)(2,1)}, u32[]{:S(2)}) copy-start(bf16[2,2,80,512]{3,2,1,0:T(8,128)(2,1)} %get-tuple-element.94) | copy-start | bytes 983044
  38.6 20.7 %copy-start.3 = (bf16[2,2,80,512]{3,2,1,0:T(8,128)(2,1)S(1)}, bf16[2,2,80,512]{3,2,1,0:T(8,128)(2,1)}, u32[]{:S(2)}) copy-start(bf16[2,2,80,512]{3,2,1,0:T(8,128)(2,1)} %get-tuple-element.102) | copy-start | bytes 983044
  38.6 21.9 %copy-start.2 = (bf16[2,2,80,512]{3,2,1,0:T(8,128)(2,1)S(1)}, bf16[2,2,80,512]{3,2,1,0:T(8,128)(2,1)}, u32[]{:S(2)}) copy-start(bf16[2,2,80,512]{3,2,1,0:T(8,128)(2,1)} %get-tuple-element.93) | copy-start | bytes 983044
  45.1 17.4 %copy-start = (s32[4]{0:T(128)S(1)}, s32[4]{0:T(128)}, u32[]{:S(2)}) copy-start(s32[4]{0:T(128)} %length_ref.1) | copy-start | bytes 52
  45.1 9.3 %collective-permute-start.8 = (bf16[2,2,80,512]{3,2,1,0:T(8,128)(2,1)}, bf16[2,2,80,512]{3,2,1,0:T(8,128)(2,1)}, u32[]{:S(2)}, u32[]{:S(2)}) collective-permute-start(bf16[2,2,80,512]{3,2,1,0:T(8,128)(2,1)} %fusion.11), channel_id=1, source_target_pairs={{0,12},{12,0},{4,8},{8,4},{1,13},{13,1},{5,9},{9,5},{2,14},{14,2},... | collective-permute-start | bytes 983048 | tf_op jit(solution)/shard_map/first_half/ppermute | solution.py:115
  47.3 11.0 %collective-permute-start.9 = (bf16[2,2,80,512]{3,2,1,0:T(8,128)(2,1)}, bf16[2,2,80,512]{3,2,1,0:T(8,128)(2,1)}, u32[]{:S(2)}, u32[]{:S(2)}) collective-permute-start(bf16[2,2,80,512]{3,2,1,0:T(8,128)(2,1)} %fusion.8), channel_id=1, source_target_pairs={{0,4},{4,0},{8,12},{12,8},{1,5},{5,1},{9,13},{13,9},{2,6},{6,2},{1... | collective-permute-start | bytes 983048 | tf_op jit(solution)/shard_map/first_half/ppermute | solution.py:115
  47.3 23.6 %collective-permute-start.7 = (bf16[2,2,2,80,512]{4,3,2,1,0:T(8,128)(2,1)}, bf16[2,2,2,80,512]{4,3,2,1,0:T(8,128)(2,1)S(1)}, u32[]{:S(2)}, u32[]{:S(2)}) collective-permute-start(bf16[2,2,2,80,512]{4,3,2,1,0:T(8,128)(2,1)} %get-tuple-element.92), channel_id=1, source_target_pairs={{0,4},{4,0},{8,12},{12,8},{1,5},{5,1},{9,13},{13,9},{2,6},{6,2},{1... | collective-permute-start | bytes 1966088 | tf_op jit(solution)/shard_map/second_half/ppermute | solution.py:115
  58.2 12.8 %collective-permute-start.10 = (bf16[2,2,2,80,512]{4,3,2,1,0:T(8,128)(2,1)}, bf16[2,2,2,80,512]{4,3,2,1,0:T(8,128)(2,1)S(1)}, u32[]{:S(2)}, u32[]{:S(2)}) collective-permute-start(bf16[2,2,2,80,512]{4,3,2,1,0:T(8,128)(2,1)} %get-tuple-element.111), channel_id=1, source_target_pairs={{0,12},{12,0},{4,8},{8,4},{1,13},{13,1},{5,9},{9,5},{2,14},{14,2},... | collective-permute-start | bytes 1966088 | tf_op jit(solution)/shard_map/second_half/ppermute | solution.py:115
  61.7 9.2 %copy-start.7 = (bf16[2,2,80,512]{3,2,1,0:T(8,128)(2,1)S(1)}, bf16[2,2,80,512]{3,2,1,0:T(8,128)(2,1)}, u32[]{:S(2)}) copy-start(bf16[2,2,80,512]{3,2,1,0:T(8,128)(2,1)} %get-tuple-element.89) | copy-start | bytes 983044
  61.7 9.3 %copy-start.8 = (bf16[2,2,80,512]{3,2,1,0:T(8,128)(2,1)S(1)}, bf16[2,2,80,512]{3,2,1,0:T(8,128)(2,1)}, u32[]{:S(2)}) copy-start(bf16[2,2,80,512]{3,2,1,0:T(8,128)(2,1)} %get-tuple-element.110) | copy-start | bytes 983044
  61.7 16.7 %copy-start.5 = (bf16[2,2,80,512]{3,2,1,0:T(8,128)(2,1)S(1)}, bf16[2,2,80,512]{3,2,1,0:T(8,128)(2,1)}, u32[]{:S(2)}) copy-start(bf16[2,2,80,512]{3,2,1,0:T(8,128)(2,1)} %get-tuple-element.118) | copy-start | bytes 983044
  61.7 9.3 %collective-permute-start.11 = (bf16[2,2,80,512]{3,2,1,0:T(8,128)(2,1)S(1)}, bf16[2,2,80,512]{3,2,1,0:T(8,128)(2,1)S(1)}, u32[]{:S(2)}, u32[]{:S(2)}) collective-permute-start(bf16[2,2,80,512]{3,2,1,0:T(8,128)(2,1)S(1)} %pad_maximum_fusion.1), channel_id=1, source_target_pairs={{0,16},{16,0},{1,17},{17,1},{2,18},{18,2},{3,19},{19,3},{4,20},{20... | collective-permute-start | bytes 983048 | tf_op jit(solution)/shard_map/first_half/ppermute | solution.py:46
  70.8 8.9 %copy-start.4 = (bf16[2,2,80,512]{3,2,1,0:T(8,128)(2,1)S(1)}, bf16[2,2,80,512]{3,2,1,0:T(8,128)(2,1)}, u32[]{:S(2)}) copy-start(bf16[2,2,80,512]{3,2,1,0:T(8,128)(2,1)} %get-tuple-element.116) | copy-start | bytes 983044
  71.1 7.3 %collective-permute-start.13 = (bf16[2,2,80,512]{3,2,1,0:T(8,128)(2,1)S(1)}, bf16[2,2,80,512]{3,2,1,0:T(8,128)(2,1)S(1)}, u32[]{:S(2)}, u32[]{:S(2)}) collective-permute-start(bf16[2,2,80,512]{3,2,1,0:T(8,128)(2,1)S(1)} %fusion.4), channel_id=1, source_target_pairs={{0,4},{4,0},{8,12},{12,8},{1,5},{5,1},{9,13},{13,9},{2,6},{6,2},{1... | collective-permute-start | bytes 983048 | tf_op jit(solution)/shard_map/second_half/ppermute | solution.py:115
  71.4 8.4 %collective-permute-start.12 = (bf16[2,2,80,512]{3,2,1,0:T(8,128)(2,1)S(1)}, bf16[2,2,80,512]{3,2,1,0:T(8,128)(2,1)S(1)}, u32[]{:S(2)}, u32[]{:S(2)}) collective-permute-start(bf16[2,2,80,512]{3,2,1,0:T(8,128)(2,1)S(1)} %fusion.5), channel_id=1, source_target_pairs={{0,12},{12,0},{4,8},{8,4},{1,13},{13,1},{5,9},{9,5},{2,14},{14,2},... | collective-permute-start | bytes 983048 | tf_op jit(solution)/shard_map/second_half/ppermute | solution.py:115
  80.0 7.2 %collective-permute-start.14 = (bf16[2,2,80,512]{3,2,1,0:T(8,128)(2,1)S(1)}, bf16[2,2,80,512]{3,2,1,0:T(8,128)(2,1)S(1)}, u32[]{:S(2)}, u32[]{:S(2)}) collective-permute-start(bf16[2,2,80,512]{3,2,1,0:T(8,128)(2,1)S(1)} %pad_maximum_fusion.2), channel_id=1, source_target_pairs={{0,16},{16,0},{1,17},{17,1},{2,18},{18,2},{3,19},{19,3},{4,20},{20... | collective-permute-start | bytes 983048 | tf_op jit(solution)/shard_map/second_half/ppermute | solution.py:46
  108.7 53.9 %copy-start.1 = (f32[128]{0:T(128)S(1)}, f32[128]{0:T(128)}, u32[]{:S(2)}) copy-start(f32[128]{0:T(128)} %param.21) | copy-start | bytes 1540
  109.7 15.0 %collective-permute-start.16 = (bf16[2,2,2,16,320]{4,3,2,1,0:T(8,128)(2,1)S(1)}, bf16[2,2,2,16,320]{4,3,2,1,0:T(8,128)(2,1)S(1)}, u32[]{:S(2)}, u32[]{:S(2)}) collective-permute-start(bf16[2,2,2,16,320]{4,3,2,1,0:T(8,128)(2,1)S(1)} %get-tuple-element.152), channel_id=1, source_target_pairs={{0,16},{16,0},{1,17},{17,1},{2,18},{18,2},{3,19},{19,3},{4,20},{20... | collective-permute-start | bytes 245768 | tf_op jit(solution)/shard_map/hidden/ppermute | solution.py:346
  111.2 14.5 %collective-permute-start.15 = (f32[80,512]{1,0:T(8,128)S(1)}, f32[80,512]{1,0:T(8,128)S(1)}, u32[]{:S(2)}, u32[]{:S(2)}) collective-permute-start(f32[80,512]{1,0:T(8,128)S(1)} %get-tuple-element.123), channel_id=1, source_target_pairs={{2,128},{34,160},{66,192},{98,224},{128,2},{160,34},{192,66},{224,... | collective-permute-start | bytes 491528 | tf_op jit(solution)/shard_map/place/ppermute | solution.py:441
  111.9 24.2 %all-to-all-start.1 = ((f32[256,1,128]{2,1,0:T(1,128)}), f32[256,1,128]{2,1,0:T(1,128)S(1)}, u32[]{:S(2)}, u32[]{:S(2)}) async-start(f32[256,1,128]{2,1,0:T(1,128)} %bitcast.26), calls=%async_computation.1 | async-start | bytes 262144 | tf_op jit(solution)/shard_map/squares/all_to_all | solution.py:438
  136.4 5.1 %collective-permute-start.17 = (bf16[80,512]{1,0:T(8,128)(2,1)S(1)}, bf16[80,512]{1,0:T(8,128)(2,1)S(1)}, u32[]{:S(2)}, u32[]{:S(2)}) collective-permute-start(bf16[80,512]{1,0:T(8,128)(2,1)S(1)} %get-tuple-element.132.refs_0_), channel_id=1, source_target_pairs={{0,4},{4,0},{8,12},{12,8},{1,5},{5,1},{9,13},{13,9},{2,6},{6,2},{1... | collective-permute-start | bytes 245768 | tf_op jit(solution)/shard_map/project/ppermute | solution.py:339
  137.3 6.9 %collective-permute-start.18 = (bf16[80,512]{1,0:T(8,128)(2,1)S(1)}, bf16[80,512]{1,0:T(8,128)(2,1)S(1)}, u32[]{:S(2)}, u32[]{:S(2)}) collective-permute-start(bf16[80,512]{1,0:T(8,128)(2,1)S(1)} %get-tuple-element.132.refs_0_), channel_id=1, source_target_pairs={{0,8},{4,12},{8,0},{12,4},{1,9},{5,13},{9,1},{13,5},{2,10},{6,14},... | collective-permute-start | bytes 245768 | tf_op jit(solution)/shard_map/project/ppermute | solution.py:339
  139.9 5.9 %collective-permute-start.19 = (bf16[80,512]{1,0:T(8,128)(2,1)S(1)}, bf16[80,512]{1,0:T(8,128)(2,1)S(1)}, u32[]{:S(2)}, u32[]{:S(2)}) collective-permute-start(bf16[80,512]{1,0:T(8,128)(2,1)S(1)} %get-tuple-element.132.refs_0_), channel_id=1, source_target_pairs={{0,12},{4,8},{8,4},{12,0},{1,13},{5,9},{9,5},{13,1},{2,14},{6,10},... | collective-permute-start | bytes 245768 | tf_op jit(solution)/shard_map/project/ppermute | solution.py:339
  146.9 15.7 %all-to-all-start.2 = ((bf16[16,16,512]{2,1,0:T(8,128)(2,1)}), bf16[16,16,512]{2,1,0:T(8,128)(2,1)S(1)}, u32[]{:S(2)}, u32[]{:S(2)}) async-start(bf16[16,16,512]{2,1,0:T(8,128)(2,1)} %bitcast.40), calls=%async_computation.2 | async-start | bytes 524288 | tf_op jit(solution)/shard_map/project/all_to_all | solution.py:451

commit v6 on v5

--- a/solution.py
+++ b/solution.py
@@ -381,17 +381,14 @@
             one_got, two_got, hidden, query_heads, state, upstream_other
         )
         one_passed = add(one_near, one_got[0])
-        one_passed, upstream_other = together(one_passed, upstream_other)
+        two_passed = add(two_near, two_got[0])
+        one_passed, two_passed, upstream_other = together(one_passed, two_passed, upstream_other)
         one_last = along_y(one_passed, 1)
+        two_last = along_y(two_passed, 0)
     with jax.named_scope("second_half"):
         away, three_near, three_mine = product(tokens, upstream_other, 0, own_rows)
-        away, tokens_other, two_near = together(away, tokens_other, two_near)
+        away, tokens_other = together(away, tokens_other)
         three_got = along_y(away, 0)
-    with jax.named_scope("first_half"):
-        two_passed = add(two_near, two_got[0])
-        two_passed, tokens_other = together(two_passed, tokens_other)
-        two_last = along_y(two_passed, 0)
-    with jax.named_scope("second_half"):
         away, four_near, four_mine = product(tokens_other, upstream_other, 1, own_rows)
         away, one_last, two_last = together(away, one_last, two_last)
         four_got = along_y(away, 1)

time: 165 us -> 163 us (0.988)
  starting transfers between devices: 49.6 us -> 47.5 us
  transfers between devices with their start and end apart: 22 -> 22, of which waited for: 12 -> 11; matrix products, arithmetic and copies ran while one was open for 6% -> 6% of each run, Pallas kernels for 14% -> 17%
where the time goes in v6:
time: 163 us; the launch traced here: 162 us
  starting transfers between devices  47.5 us (29%)
  waiting for transfers between devices  47.3 us (29%)
  Pallas kernels  31.1 us (19%)
  blocking collectives  20.7 us (13%)
  other arithmetic  8.82 us (5%)
  local copies, waits for them, and re-layouts  5.56 us (3%)
    all_to_all x1, blocking collectives, local(): parts = lax.all_to_all(parts, 'z', 0, 0)  20.7 us
    pallas_call x4, Pallas kernels, product(): pl.pallas_call(product_kernel, out_shape=(pltpu.HBM((2, 2, 2, rows, colum...  18.6 us
    all_to_all x1, starting transfers between devices, local(): squares = lax.all_to_all(squares, EVERY, 0, 0, tiled=True)  13.4 us
    ppermute x4, starting transfers between devices, trade(): got = lax.ppermute(sent, mesh_axis, partners)  12 us
    all_to_all x1, waiting for transfers between devices, local(): squares = lax.all_to_all(squares, EVERY, 0, 0, tiled=True)  10.3 us
    all_to_all x1, waiting for transfers between devices, local(): lax.all_to_all(partial.reshape(16, states, columns), ('z', 'xl'), 0, 0)  10.2 us
    ppermute x8, waiting for transfers between devices, along_y(): return lax.ppermute(values, 'y', PAIRING[pairing])  9.59 us
    ppermute x8, starting transfers between devices, along_y(): return lax.ppermute(values, 'y', PAIRING[pairing])  8.55 us
  transfers between devices with their start and end apart: 22, of which 11 were waited for; matrix products, arithmetic and copies ran while one was open for 6% of the time, Pallas kernels for 17%

profile of v6, /device:TPU:24, one launch (start us, length us, event | category | flops | bytes accessed | tf_op | source)
XLA Modules:
  0.0 162.1 jit_solution(9266798096816494540)
XLA Ops:
  0.7 3.1 %collective-permute-start.6 = (bf16[1024,2,256]{2,1,0:T(2,128)(2,1)}, bf16[1024,2,256]{2,1,0:T(2,128)(2,1)S(1)}, u32[]{:S(2)}, u32[]{:S(2)}) collective-permute-start(bf16[1024,2,256]{2,1,0:T(2,128)(2,1)} %param.12), channel_id=1, source_target_pairs={{0,2},{2,0},{1,3},{3,1},{4,6},{6,4},{5,7},{7,5},{8,10},{10,8},{9,1... | collective-permute-start | bytes 3145736 | tf_op jit(solution)/shard_map/exchange/ppermute | solution.py:46
  3.9 1.5 copy.59
  5.4 4.7 %product.4 = (bf16[2,2,2,80,512]{4,3,2,1,0:T(8,128)(2,1)}, bf16[2,2,80,512]{3,2,1,0:T(8,128)(2,1)}, bf16[2,2,80,512]{3,2,1,0:T(8,128)(2,1)}) custom-call(s32[4]{0:T(128)S(1)} %get-tuple-element.158.order, bf16[1024,1280]{1,0:T(8,128)(2,1)} %left_ref.3, bf16[1024,512]{1,0:T(8,128)(2,1)S(1)} %bitcast.88), custom_call_target="tpu_custom_call" | custom-call | tf_op jit(solution)/shard_map/first_half/product/pallas_call | solution.py:85
  10.4 2.0 %collective-permute-start.3 = (bf16[2,2,2,16,320]{4,3,2,1,0:T(8,128)(2,1)S(1)}, bf16[2,2,2,16,320]{4,3,2,1,0:T(8,128)(2,1)S(1)}, u32[]{:S(2)}, u32[]{:S(2)}) collective-permute-start(bf16[2,2,2,16,320]{4,3,2,1,0:T(8,128)(2,1)S(1)} %get-tuple-element.154), channel_id=1, source_target_pairs={{0,32},{32,0},{64,96},{96,64},{128,160},{160,128},{192,224},{224,1... | collective-permute-start | bytes 245768 | tf_op jit(solution)/shard_map/hidden/ppermute | solution.py:346
  13.1 4.6 %product.5 = (bf16[2,2,2,80,512]{4,3,2,1,0:T(8,128)(2,1)}, bf16[2,2,80,512]{3,2,1,0:T(8,128)(2,1)}, bf16[2,2,80,512]{3,2,1,0:T(8,128)(2,1)}) custom-call(s32[4]{0:T(128)S(1)} %get-tuple-element.159.order, bf16[1024,1280]{1,0:T(8,128)(2,1)} %collective-permute-done.left_ref, bf16[1024,512]{1,0:T(8,128)(2,1)S(1)} %bitcast.89), custom_call_target="tpu_custom_call" | custom-call | tf_op jit(solution)/shard_map/first_half/product/pallas_call | solution.py:85
  18.9 3.3 %collective-permute-start.4 = (bf16[2,2,2,16,320]{4,3,2,1,0:T(8,128)(2,1)S(1)}, bf16[2,2,2,16,320]{4,3,2,1,0:T(8,128)(2,1)S(1)}, u32[]{:S(2)}, u32[]{:S(2)}) collective-permute-start(bf16[2,2,2,16,320]{4,3,2,1,0:T(8,128)(2,1)S(1)} %get-tuple-element.152), channel_id=1, source_target_pairs={{0,64},{32,96},{64,0},{96,32},{128,192},{160,224},{192,128},{224,1... | collective-permute-start | bytes 245768 | tf_op jit(solution)/shard_map/hidden/ppermute | solution.py:346
  23.2 3.3 %collective-permute-done.4 = bf16[2,2,2,16,320]{4,3,2,1,0:T(8,128)(2,1)S(1)} collective-permute-done((bf16[2,2,2,16,320]{4,3,2,1,0:T(8,128)(2,1)S(1)}, bf16[2,2,2,16,320]{4,3,2,1,0:T(8,128)(2,1)S(1)}, u32[]{:S(2)}, u32[]{:S(2)}) %collective-permute-start.4) | collective-permute-done | bytes 81952 | tf_op jit(solution)/shard_map/hidden/ppermute | solution.py:346
  26.5 6.0 %collective-permute-start.5 = (bf16[2,2,2,16,320]{4,3,2,1,0:T(8,128)(2,1)S(1)}, bf16[2,2,2,16,320]{4,3,2,1,0:T(8,128)(2,1)S(1)}, u32[]{:S(2)}, u32[]{:S(2)}) collective-permute-start(bf16[2,2,2,16,320]{4,3,2,1,0:T(8,128)(2,1)S(1)} %get-tuple-element.150), channel_id=1, source_target_pairs={{0,128},{32,160},{64,192},{96,224},{128,0},{160,32},{192,64},{224,... | collective-permute-start | bytes 245768 | tf_op jit(solution)/shard_map/hidden/ppermute | solution.py:346
  32.6 1.2 pad_maximum_fusion
  33.8 2.6 %collective-permute-done.5 = bf16[2,2,2,16,320]{4,3,2,1,0:T(8,128)(2,1)S(1)} collective-permute-done((bf16[2,2,2,16,320]{4,3,2,1,0:T(8,128)(2,1)S(1)}, bf16[2,2,2,16,320]{4,3,2,1,0:T(8,128)(2,1)S(1)}, u32[]{:S(2)}, u32[]{:S(2)}) %collective-permute-start.5) | collective-permute-done | bytes 81952 | tf_op jit(solution)/shard_map/hidden/ppermute | solution.py:346
  36.8 1.8 %fusion.11 = bf16[2,2,80,512]{3,2,1,0:T(8,128)(2,1)} fusion(bf16[2,2,80,512]{3,2,1,0:T(8,128)(2,1)} %get-tuple-element.70, bf16[2,2,2,80,512]{4,3,2,1,0:T(8,128)(2,1)S(1)} %collective-permute-done.1), kind=kLoop, calls=%fused_computation.20 | loop fusion | flops 655360 | bytes 983040 | tf_op jit(solution)/shard_map/first_half/convert_element_type | solution.py:111
  38.6 1.9 %fusion.10 = bf16[2,2,80,512]{3,2,1,0:T(8,128)(2,1)} fusion(bf16[2,2,80,512]{3,2,1,0:T(8,128)(2,1)S(1)} %copy-done.6, bf16[2,2,2,80,512]{4,3,2,1,0:T(8,128)(2,1)} %collective-permute-done.2), kind=kLoop, calls=%fused_computation.18 | loop fusion | flops 655360 | bytes 983040 | tf_op jit(solution)/shard_map/first_half/convert_element_type | solution.py:111
  40.5 2.2 %collective-permute-start.8 = (bf16[2,2,80,512]{3,2,1,0:T(8,128)(2,1)}, bf16[2,2,80,512]{3,2,1,0:T(8,128)(2,1)}, u32[]{:S(2)}, u32[]{:S(2)}) collective-permute-start(bf16[2,2,80,512]{3,2,1,0:T(8,128)(2,1)} %fusion.11), channel_id=1, source_target_pairs={{0,12},{12,0},{4,8},{8,4},{1,13},{13,1},{5,9},{9,5},{2,14},{14,2},... | collective-permute-start | bytes 983048 | tf_op jit(solution)/shard_map/first_half/ppermute | solution.py:115
  42.6 4.6 %product.6 = (bf16[2,2,2,80,512]{4,3,2,1,0:T(8,128)(2,1)}, bf16[2,2,80,512]{3,2,1,0:T(8,128)(2,1)}, bf16[2,2,80,512]{3,2,1,0:T(8,128)(2,1)}) custom-call(s32[4]{0:T(128)S(1)} %get-tuple-element.158.order, bf16[1024,1280]{1,0:T(8,128)(2,1)} %left_ref.3, bf16[1024,512]{1,0:T(8,128)(2,1)S(1)} %bitcast.90), custom_call_target="tpu_custom_call" | custom-call | tf_op jit(solution)/shard_map/second_half/product/pallas_call | solution.py:85
  47.3 2.0 %collective-permute-start.7 = (bf16[2,2,2,80,512]{4,3,2,1,0:T(8,128)(2,1)}, bf16[2,2,2,80,512]{4,3,2,1,0:T(8,128)(2,1)S(1)}, u32[]{:S(2)}, u32[]{:S(2)}) collective-permute-start(bf16[2,2,2,80,512]{4,3,2,1,0:T(8,128)(2,1)} %get-tuple-element.91), channel_id=1, source_target_pairs={{0,4},{4,0},{8,12},{12,8},{1,5},{5,1},{9,13},{13,9},{2,6},{6,2},{1... | collective-permute-start | bytes 1966088 | tf_op jit(solution)/shard_map/second_half/ppermute | solution.py:115
  49.3 4.7 %product.7 = (bf16[2,2,2,80,512]{4,3,2,1,0:T(8,128)(2,1)}, bf16[2,2,80,512]{3,2,1,0:T(8,128)(2,1)}, bf16[2,2,80,512]{3,2,1,0:T(8,128)(2,1)}) custom-call(s32[4]{0:T(128)S(1)} %get-tuple-element.159.order, bf16[1024,1280]{1,0:T(8,128)(2,1)} %collective-permute-done.left_ref, bf16[1024,512]{1,0:T(8,128)(2,1)S(1)} %bitcast.91), custom_call_target="tpu_custom_call" | custom-call | tf_op jit(solution)/shard_map/second_half/product/pallas_call | solution.py:85
  54.0 1.1 collective-permute-start.10
  55.1 1.2 fusion.7
  58.3 8.4 %old_attention.1 = (f32[2,4,32,128]{3,2,1,0:T(8,128)S(1)}, f32[2,4,32,128]{3,2,1,0:T(8,128)S(1)}, f32[2,4,32,128]{3,2,1,0:T(8,128)S(1)}) custom-call(s32[4]{0:T(128)S(1)} %copy-done, bf16[2,4,32,128]{3,2,1,0:T(8,128)(2,1)S(1)} %bitcast.93, bf16[4,2048,256]{2,1,0:T(8,128)(2,1)} %key_ref.1, bf16[4,2048,256]{2,1,0:T(8,128)(2,1)} %value_ref.1), custom_call_target="tpu_custom_call" | custom-call | tf_op jit(solution)/shard_map/old/old_attention/pallas_call | solution.py:143
  66.8 2.7 %collective-permute-done.10 = bf16[2,2,2,80,512]{4,3,2,1,0:T(8,128)(2,1)S(1)} collective-permute-done((bf16[2,2,2,80,512]{4,3,2,1,0:T(8,128)(2,1)}, bf16[2,2,2,80,512]{4,3,2,1,0:T(8,128)(2,1)S(1)}, u32[]{:S(2)}, u32[]{:S(2)}) %collective-permute-start.10) | collective-permute-done | bytes 655392 | tf_op jit(solution)/shard_map/second_half/ppermute | solution.py:115
  71.1 5.8 %collective-permute-done.13 = bf16[2,2,80,512]{3,2,1,0:T(8,128)(2,1)S(1)} collective-permute-done((bf16[2,2,80,512]{3,2,1,0:T(8,128)(2,1)S(1)}, bf16[2,2,80,512]{3,2,1,0:T(8,128)(2,1)S(1)}, u32[]{:S(2)}, u32[]{:S(2)}) %collective-permute-start.13) | collective-permute-done | bytes 327712 | tf_op jit(solution)/shard_map/second_half/ppermute | solution.py:115
  79.1 6.5 %collective-permute-done.14 = bf16[2,2,80,512]{3,2,1,0:T(8,128)(2,1)S(1)} collective-permute-done((bf16[2,2,80,512]{3,2,1,0:T(8,128)(2,1)S(1)}, bf16[2,2,80,512]{3,2,1,0:T(8,128)(2,1)S(1)}, u32[]{:S(2)}, u32[]{:S(2)}) %collective-permute-start.14) | collective-permute-done | bytes 327712 | tf_op jit(solution)/shard_map/second_half/ppermute | solution.py:46
  85.9 20.7 %all_to_all.22.parts_ref = bf16[8,80,512]{2,1,0:T(8,128)(2,1)S(1)} all-to-all(bf16[8,80,512]{2,1,0:T(8,128)(2,1)S(1)} %maximum_select_fusion), channel_id=1, replica_groups=mesh['z'=8,'xl'=2,'y'=4,'xh'=2,'core'=2] {'z'}, dimensions={0} | all-to-all | bytes 1310720 | tf_op jit(solution)/shard_map/reduce_z/all_to_all | solution.py:420
  108.9 13.4 %all-to-all-start.1 = ((f32[256,1,128]{2,1,0:T(1,128)}), f32[256,1,128]{2,1,0:T(1,128)S(1)}, u32[]{:S(2)}, u32[]{:S(2)}) async-start(f32[256,1,128]{2,1,0:T(1,128)} %bitcast.26), calls=%async_computation.1 | async-start | bytes 262144 | tf_op jit(solution)/shard_map/squares/all_to_all | solution.py:435
  123.4 10.3 %all-to-all-done.1 = f32[256,1,128]{2,1,0:T(1,128)S(1)} async-done(((f32[256,1,128]{2,1,0:T(1,128)}), f32[256,1,128]{2,1,0:T(1,128)S(1)}, u32[]{:S(2)}, u32[]{:S(2)}) %all-to-all-start.1) | async-done | bytes 131104 | tf_op jit(solution)/shard_map/squares/all_to_all | solution.py:435
  135.0 2.7 %collective-permute-start.18 = (bf16[80,512]{1,0:T(8,128)(2,1)S(1)}, bf16[80,512]{1,0:T(8,128)(2,1)S(1)}, u32[]{:S(2)}, u32[]{:S(2)}) collective-permute-start(bf16[80,512]{1,0:T(8,128)(2,1)S(1)} %get-tuple-element.128.refs_0_), channel_id=1, source_target_pairs={{0,8},{4,12},{8,0},{12,4},{1,9},{5,13},{9,1},{13,5},{2,10},{6,14},... | collective-permute-start | bytes 245768 | tf_op jit(solution)/shard_map/project/ppermute | solution.py:339
  137.6 1.2 collective-permute-start.19
  139.2 2.7 %collective-permute-done.18.refs_2_ = bf16[80,512]{1,0:T(8,128)(2,1)S(1)} collective-permute-done((bf16[80,512]{1,0:T(8,128)(2,1)S(1)}, bf16[80,512]{1,0:T(8,128)(2,1)S(1)}, u32[]{:S(2)}, u32[]{:S(2)}) %collective-permute-start.18) | collective-permute-done | bytes 81952 | tf_op jit(solution)/shard_map/project/ppermute | solution.py:339
  141.9 1.7 %collective-permute-done.19.refs_3_ = bf16[80,512]{1,0:T(8,128)(2,1)S(1)} collective-permute-done((bf16[80,512]{1,0:T(8,128)(2,1)S(1)}, bf16[80,512]{1,0:T(8,128)(2,1)S(1)}, u32[]{:S(2)}, u32[]{:S(2)}) %collective-permute-start.19) | collective-permute-done | bytes 81952 | tf_op jit(solution)/shard_map/project/ppermute | solution.py:339
  144.5 3.5 %all-to-all-start.2 = ((bf16[16,16,512]{2,1,0:T(8,128)(2,1)}), bf16[16,16,512]{2,1,0:T(8,128)(2,1)S(1)}, u32[]{:S(2)}, u32[]{:S(2)}) async-start(bf16[16,16,512]{2,1,0:T(8,128)(2,1)} %bitcast.40), calls=%async_computation.2 | async-start | bytes 524288 | tf_op jit(solution)/shard_map/project/all_to_all | solution.py:448
  150.0 10.2 %all-to-all-done.2.part_ref = bf16[16,16,512]{2,1,0:T(8,128)(2,1)S(1)} async-done(((bf16[16,16,512]{2,1,0:T(8,128)(2,1)}), bf16[16,16,512]{2,1,0:T(8,128)(2,1)S(1)}, u32[]{:S(2)}, u32[]{:S(2)}) %all-to-all-start.2) | async-done | bytes 262176 | tf_op jit(solution)/shard_map/project/all_to_all | solution.py:448
  160.2 1.9 %fresh_attention.1 = (bf16[4,4,256]{2,1,0:T(4,128)(2,1)}, bf16[4,4,256]{2,1,0:T(4,128)(2,1)}, bf16[4,4,2048]{2,1,0:T(4,128)(2,1)}) custom-call(bf16[16,16,512]{2,1,0:T(8,128)(2,1)S(1)} %all-to-all-done.2.part_ref, bf16[2,128,128]{2,1,0:T(8,128)(2,1)S(1)} %bitcast.94, f32[2,128,128]{2,1,0:T(8,128)S(1)} %bitcast.96, f32[2,128,128]{2,1,0:T(8,128)S(1)} %bitcast.97, ...), custom_call_target="tpu_custom_call" | custom-call | tf_op jit(solution)/shard_map/fresh/fresh_attention/pallas_call | solution.py:220
  (95 shorter events, 17.5 us)
Async XLA Ops:
  0.6 9.5 %copy-start.9 = (bf16[4,4,5120]{2,1,0:T(4,128)(2,1)S(1)}, bf16[4,4,5120]{2,1,0:T(4,128)(2,1)}, u32[]{:S(2)}) copy-start(bf16[4,4,5120]{2,1,0:T(4,128)(2,1)} %param.16) | copy-start | bytes 491524
  0.6 9.5 %collective-permute-start = (bf16[1024,1280]{1,0:T(8,128)(2,1)}, bf16[1024,1280]{1,0:T(8,128)(2,1)}, u32[]{:S(2)}, u32[]{:S(2)}) collective-permute-start(bf16[1024,1280]{1,0:T(8,128)(2,1)} %left_ref.3), channel_id=1, source_target_pairs={{0,1},{1,0},{2,3},{3,2},{4,5},{5,4},{6,7},{7,6},{8,9},{9,8},{10,11... | collective-permute-start | bytes 7864328 | tf_op jit(solution)/shard_map/exchange/ppermute | solution.py:46
  0.7 35.8 %collective-permute-start.6 = (bf16[1024,2,256]{2,1,0:T(2,128)(2,1)}, bf16[1024,2,256]{2,1,0:T(2,128)(2,1)S(1)}, u32[]{:S(2)}, u32[]{:S(2)}) collective-permute-start(bf16[1024,2,256]{2,1,0:T(2,128)(2,1)} %param.12), channel_id=1, source_target_pairs={{0,2},{2,0},{1,3},{3,1},{4,6},{6,4},{5,7},{7,5},{8,10},{10,8},{9,1... | collective-permute-start | bytes 3145736 | tf_op jit(solution)/shard_map/exchange/ppermute | solution.py:46
  10.1 22.5 %copy-start.10 = (f32[80,2,256]{2,1,0:T(2,128)S(1)}, f32[80,2,256]{2,1,0:T(2,128)}, u32[]{:S(2)}) copy-start(f32[80,2,256]{2,1,0:T(2,128)} %param.15) | copy-start | bytes 491524
  10.4 8.4 %collective-permute-start.3 = (bf16[2,2,2,16,320]{4,3,2,1,0:T(8,128)(2,1)S(1)}, bf16[2,2,2,16,320]{4,3,2,1,0:T(8,128)(2,1)S(1)}, u32[]{:S(2)}, u32[]{:S(2)}) collective-permute-start(bf16[2,2,2,16,320]{4,3,2,1,0:T(8,128)(2,1)S(1)} %get-tuple-element.154), channel_id=1, source_target_pairs={{0,32},{32,0},{64,96},{96,64},{128,160},{160,128},{192,224},{224,1... | collective-permute-start | bytes 245768 | tf_op jit(solution)/shard_map/hidden/ppermute | solution.py:346
  12.4 24.4 %collective-permute-start.1 = (bf16[2,2,2,80,512]{4,3,2,1,0:T(8,128)(2,1)}, bf16[2,2,2,80,512]{4,3,2,1,0:T(8,128)(2,1)S(1)}, u32[]{:S(2)}, u32[]{:S(2)}) collective-permute-start(bf16[2,2,2,80,512]{4,3,2,1,0:T(8,128)(2,1)} %get-tuple-element.72), channel_id=1, source_target_pairs={{0,4},{4,0},{8,12},{12,8},{1,5},{5,1},{9,13},{13,9},{2,6},{6,2},{1... | collective-permute-start | bytes 1966088 | tf_op jit(solution)/shard_map/first_half/ppermute | solution.py:115
  17.7 19.1 %collective-permute-start.2 = (bf16[2,2,2,80,512]{4,3,2,1,0:T(8,128)(2,1)}, bf16[2,2,2,80,512]{4,3,2,1,0:T(8,128)(2,1)}, u32[]{:S(2)}, u32[]{:S(2)}) collective-permute-start(bf16[2,2,2,80,512]{4,3,2,1,0:T(8,128)(2,1)} %get-tuple-element.74), channel_id=1, source_target_pairs={{0,12},{12,0},{4,8},{8,4},{1,13},{13,1},{5,9},{9,5},{2,14},{14,2},... | collective-permute-start | bytes 1966088 | tf_op jit(solution)/shard_map/first_half/ppermute | solution.py:115
  18.9 7.6 %collective-permute-start.4 = (bf16[2,2,2,16,320]{4,3,2,1,0:T(8,128)(2,1)S(1)}, bf16[2,2,2,16,320]{4,3,2,1,0:T(8,128)(2,1)S(1)}, u32[]{:S(2)}, u32[]{:S(2)}) collective-permute-start(bf16[2,2,2,16,320]{4,3,2,1,0:T(8,128)(2,1)S(1)} %get-tuple-element.152), channel_id=1, source_target_pairs={{0,64},{32,96},{64,0},{96,32},{128,192},{160,224},{192,128},{224,1... | collective-permute-start | bytes 245768 | tf_op jit(solution)/shard_map/hidden/ppermute | solution.py:346
  23.1 15.5 %copy-start.6 = (bf16[2,2,80,512]{3,2,1,0:T(8,128)(2,1)S(1)}, bf16[2,2,80,512]{3,2,1,0:T(8,128)(2,1)}, u32[]{:S(2)}) copy-start(bf16[2,2,80,512]{3,2,1,0:T(8,128)(2,1)} %get-tuple-element.85) | copy-start | bytes 983044
  26.5 9.9 %collective-permute-start.5 = (bf16[2,2,2,16,320]{4,3,2,1,0:T(8,128)(2,1)S(1)}, bf16[2,2,2,16,320]{4,3,2,1,0:T(8,128)(2,1)S(1)}, u32[]{:S(2)}, u32[]{:S(2)}) collective-permute-start(bf16[2,2,2,16,320]{4,3,2,1,0:T(8,128)(2,1)S(1)} %get-tuple-element.150), channel_id=1, source_target_pairs={{0,128},{32,160},{64,192},{96,224},{128,0},{160,32},{192,64},{224,... | collective-permute-start | bytes 245768 | tf_op jit(solution)/shard_map/hidden/ppermute | solution.py:346
  38.6 16.5 %copy-start.3 = (bf16[2,2,80,512]{3,2,1,0:T(8,128)(2,1)S(1)}, bf16[2,2,80,512]{3,2,1,0:T(8,128)(2,1)}, u32[]{:S(2)}) copy-start(bf16[2,2,80,512]{3,2,1,0:T(8,128)(2,1)} %get-tuple-element.98) | copy-start | bytes 983044
  40.5 13.5 %collective-permute-start.8 = (bf16[2,2,80,512]{3,2,1,0:T(8,128)(2,1)}, bf16[2,2,80,512]{3,2,1,0:T(8,128)(2,1)}, u32[]{:S(2)}, u32[]{:S(2)}) collective-permute-start(bf16[2,2,80,512]{3,2,1,0:T(8,128)(2,1)} %fusion.11), channel_id=1, source_target_pairs={{0,12},{12,0},{4,8},{8,4},{1,13},{13,1},{5,9},{9,5},{2,14},{14,2},... | collective-permute-start | bytes 983048 | tf_op jit(solution)/shard_map/first_half/ppermute | solution.py:115
  42.6 11.3 %collective-permute-start.9 = (bf16[2,2,80,512]{3,2,1,0:T(8,128)(2,1)}, bf16[2,2,80,512]{3,2,1,0:T(8,128)(2,1)}, u32[]{:S(2)}, u32[]{:S(2)}) collective-permute-start(bf16[2,2,80,512]{3,2,1,0:T(8,128)(2,1)} %fusion.10), channel_id=1, source_target_pairs={{0,4},{4,0},{8,12},{12,8},{1,5},{5,1},{9,13},{13,9},{2,6},{6,2},{1... | collective-permute-start | bytes 983048 | tf_op jit(solution)/shard_map/first_half/ppermute | solution.py:115
  42.6 13.7 %copy-start.2 = (bf16[2,2,80,512]{3,2,1,0:T(8,128)(2,1)S(1)}, bf16[2,2,80,512]{3,2,1,0:T(8,128)(2,1)}, u32[]{:S(2)}) copy-start(bf16[2,2,80,512]{3,2,1,0:T(8,128)(2,1)} %get-tuple-element.92) | copy-start | bytes 983044
  47.3 11.0 %copy-start = (s32[4]{0:T(128)S(1)}, s32[4]{0:T(128)}, u32[]{:S(2)}) copy-start(s32[4]{0:T(128)} %length_ref.1) | copy-start | bytes 52
  47.3 19.4 %collective-permute-start.7 = (bf16[2,2,2,80,512]{4,3,2,1,0:T(8,128)(2,1)}, bf16[2,2,2,80,512]{4,3,2,1,0:T(8,128)(2,1)S(1)}, u32[]{:S(2)}, u32[]{:S(2)}) collective-permute-start(bf16[2,2,2,80,512]{4,3,2,1,0:T(8,128)(2,1)} %get-tuple-element.91), channel_id=1, source_target_pairs={{0,4},{4,0},{8,12},{12,8},{1,5},{5,1},{9,13},{13,9},{2,6},{6,2},{1... | collective-permute-start | bytes 1966088 | tf_op jit(solution)/shard_map/second_half/ppermute | solution.py:115
  54.0 15.5 %collective-permute-start.10 = (bf16[2,2,2,80,512]{4,3,2,1,0:T(8,128)(2,1)}, bf16[2,2,2,80,512]{4,3,2,1,0:T(8,128)(2,1)S(1)}, u32[]{:S(2)}, u32[]{:S(2)}) collective-permute-start(bf16[2,2,2,80,512]{4,3,2,1,0:T(8,128)(2,1)} %get-tuple-element.107), channel_id=1, source_target_pairs={{0,12},{12,0},{4,8},{8,4},{1,13},{13,1},{5,9},{9,5},{2,14},{14,2},... | collective-permute-start | bytes 1966088 | tf_op jit(solution)/shard_map/second_half/ppermute | solution.py:115
  57.6 11.9 %copy-start.8 = (bf16[2,2,80,512]{3,2,1,0:T(8,128)(2,1)S(1)}, bf16[2,2,80,512]{3,2,1,0:T(8,128)(2,1)}, u32[]{:S(2)}) copy-start(bf16[2,2,80,512]{3,2,1,0:T(8,128)(2,1)} %get-tuple-element.106) | copy-start | bytes 983044
  57.6 19.3 %copy-start.5 = (bf16[2,2,80,512]{3,2,1,0:T(8,128)(2,1)S(1)}, bf16[2,2,80,512]{3,2,1,0:T(8,128)(2,1)}, u32[]{:S(2)}) copy-start(bf16[2,2,80,512]{3,2,1,0:T(8,128)(2,1)} %get-tuple-element.114) | copy-start | bytes 983044
  57.6 12.0 %collective-permute-start.11 = (bf16[2,2,80,512]{3,2,1,0:T(8,128)(2,1)S(1)}, bf16[2,2,80,512]{3,2,1,0:T(8,128)(2,1)S(1)}, u32[]{:S(2)}, u32[]{:S(2)}) collective-permute-start(bf16[2,2,80,512]{3,2,1,0:T(8,128)(2,1)S(1)} %pad_maximum_fusion.1), channel_id=1, source_target_pairs={{0,16},{16,0},{1,17},{17,1},{2,18},{18,2},{3,19},{19,3},{4,20},{20... | collective-permute-start | bytes 983048 | tf_op jit(solution)/shard_map/first_half/ppermute | solution.py:46
  66.7 11.5 %copy-start.4 = (bf16[2,2,80,512]{3,2,1,0:T(8,128)(2,1)S(1)}, bf16[2,2,80,512]{3,2,1,0:T(8,128)(2,1)}, u32[]{:S(2)}) copy-start(bf16[2,2,80,512]{3,2,1,0:T(8,128)(2,1)} %get-tuple-element.112) | copy-start | bytes 983044
  69.6 7.3 %collective-permute-start.13 = (bf16[2,2,80,512]{3,2,1,0:T(8,128)(2,1)S(1)}, bf16[2,2,80,512]{3,2,1,0:T(8,128)(2,1)S(1)}, u32[]{:S(2)}, u32[]{:S(2)}) collective-permute-start(bf16[2,2,80,512]{3,2,1,0:T(8,128)(2,1)S(1)} %fusion.4), channel_id=1, source_target_pairs={{0,4},{4,0},{8,12},{12,8},{1,5},{5,1},{9,13},{13,9},{2,6},{6,2},{1... | collective-permute-start | bytes 983048 | tf_op jit(solution)/shard_map/second_half/ppermute | solution.py:115
  69.9 8.4 %collective-permute-start.12 = (bf16[2,2,80,512]{3,2,1,0:T(8,128)(2,1)S(1)}, bf16[2,2,80,512]{3,2,1,0:T(8,128)(2,1)S(1)}, u32[]{:S(2)}, u32[]{:S(2)}) collective-permute-start(bf16[2,2,80,512]{3,2,1,0:T(8,128)(2,1)S(1)} %fusion.5), channel_id=1, source_target_pairs={{0,12},{12,0},{4,8},{8,4},{1,13},{13,1},{5,9},{9,5},{2,14},{14,2},... | collective-permute-start | bytes 983048 | tf_op jit(solution)/shard_map/second_half/ppermute | solution.py:115
  78.4 7.2 %collective-permute-start.14 = (bf16[2,2,80,512]{3,2,1,0:T(8,128)(2,1)S(1)}, bf16[2,2,80,512]{3,2,1,0:T(8,128)(2,1)S(1)}, u32[]{:S(2)}, u32[]{:S(2)}) collective-permute-start(bf16[2,2,80,512]{3,2,1,0:T(8,128)(2,1)S(1)} %pad_maximum_fusion.2), channel_id=1, source_target_pairs={{0,16},{16,0},{1,17},{17,1},{2,18},{18,2},{3,19},{19,3},{4,20},{20... | collective-permute-start | bytes 983048 | tf_op jit(solution)/shard_map/second_half/ppermute | solution.py:46
  106.6 53.6 %copy-start.1 = (f32[128]{0:T(128)S(1)}, f32[128]{0:T(128)}, u32[]{:S(2)}) copy-start(f32[128]{0:T(128)} %param.21) | copy-start | bytes 1540
  107.5 14.7 %collective-permute-start.16 = (bf16[2,2,2,16,320]{4,3,2,1,0:T(8,128)(2,1)S(1)}, bf16[2,2,2,16,320]{4,3,2,1,0:T(8,128)(2,1)S(1)}, u32[]{:S(2)}, u32[]{:S(2)}) collective-permute-start(bf16[2,2,2,16,320]{4,3,2,1,0:T(8,128)(2,1)S(1)} %get-tuple-element.148), channel_id=1, source_target_pairs={{0,16},{16,0},{1,17},{17,1},{2,18},{18,2},{3,19},{19,3},{4,20},{20... | collective-permute-start | bytes 245768 | tf_op jit(solution)/shard_map/hidden/ppermute | solution.py:346
  108.2 15.1 %collective-permute-start.15 = (f32[80,512]{1,0:T(8,128)S(1)}, f32[80,512]{1,0:T(8,128)S(1)}, u32[]{:S(2)}, u32[]{:S(2)}) collective-permute-start(f32[80,512]{1,0:T(8,128)S(1)} %get-tuple-element.119), channel_id=1, source_target_pairs={{2,128},{34,160},{66,192},{98,224},{128,2},{160,34},{192,66},{224,... | collective-permute-start | bytes 491528 | tf_op jit(solution)/shard_map/place/ppermute | solution.py:438
  108.9 24.8 %all-to-all-start.1 = ((f32[256,1,128]{2,1,0:T(1,128)}), f32[256,1,128]{2,1,0:T(1,128)S(1)}, u32[]{:S(2)}, u32[]{:S(2)}) async-start(f32[256,1,128]{2,1,0:T(1,128)} %bitcast.26), calls=%async_computation.1 | async-start | bytes 262144 | tf_op jit(solution)/shard_map/squares/all_to_all | solution.py:435
  134.1 5.1 %collective-permute-start.17 = (bf16[80,512]{1,0:T(8,128)(2,1)S(1)}, bf16[80,512]{1,0:T(8,128)(2,1)S(1)}, u32[]{:S(2)}, u32[]{:S(2)}) collective-permute-start(bf16[80,512]{1,0:T(8,128)(2,1)S(1)} %get-tuple-element.128.refs_0_), channel_id=1, source_target_pairs={{0,4},{4,0},{8,12},{12,8},{1,5},{5,1},{9,13},{13,9},{2,6},{6,2},{1... | collective-permute-start | bytes 245768 | tf_op jit(solution)/shard_map/project/ppermute | solution.py:339
  135.0 6.9 %collective-permute-start.18 = (bf16[80,512]{1,0:T(8,128)(2,1)S(1)}, bf16[80,512]{1,0:T(8,128)(2,1)S(1)}, u32[]{:S(2)}, u32[]{:S(2)}) collective-permute-start(bf16[80,512]{1,0:T(8,128)(2,1)S(1)} %get-tuple-element.128.refs_0_), channel_id=1, source_target_pairs={{0,8},{4,12},{8,0},{12,4},{1,9},{5,13},{9,1},{13,5},{2,10},{6,14},... | collective-permute-start | bytes 245768 | tf_op jit(solution)/shard_map/project/ppermute | solution.py:339
  137.6 5.9 %collective-permute-start.19 = (bf16[80,512]{1,0:T(8,128)(2,1)S(1)}, bf16[80,512]{1,0:T(8,128)(2,1)S(1)}, u32[]{:S(2)}, u32[]{:S(2)}) collective-permute-start(bf16[80,512]{1,0:T(8,128)(2,1)S(1)} %get-tuple-element.128.refs_0_), channel_id=1, source_target_pairs={{0,12},{4,8},{8,4},{12,0},{1,13},{5,9},{9,5},{13,1},{2,14},{6,10},... | collective-permute-start | bytes 245768 | tf_op jit(solution)/shard_map/project/ppermute | solution.py:339
  144.5 15.7 %all-to-all-start.2 = ((bf16[16,16,512]{2,1,0:T(8,128)(2,1)}), bf16[16,16,512]{2,1,0:T(8,128)(2,1)S(1)}, u32[]{:S(2)}, u32[]{:S(2)}) async-start(bf16[16,16,512]{2,1,0:T(8,128)(2,1)} %bitcast.40), calls=%async_computation.2 | async-start | bytes 524288 | tf_op jit(solution)/shard_map/project/all_to_all | solution.py:448
  (1 other events, 9.2 us)
